TPU v7x, 32 devices: a whole 2x2x4 slice. The times are simulated.
32 devices in a mesh: slab: 16 (over z, y, x), grp: 2 (over core).
Axes of the slice: x: 2, y: 2, z: 4, core: 2. Of those that a mesh axis runs over, the one named last changes fastest.
Arguments:
- saturation: float32 [32, 64, 256], P(('slab', 'grp')), may hold values from 0.5 to 3
- inlet_mask: int32 [32, 64, 256], P(('slab', 'grp')), may hold values 0 or 1
- crystal_size: float32 [131072], P(('slab', 'grp')), may hold values from 0.5 to 2
- crystal_weight: float32 [131072], P(('slab', 'grp')), may hold values from 0.3 to 3
- crystal_cell: int32 [131072], P(('slab', 'grp')), may hold values from 0 to 32767
- live_count: int32 [32], P(('slab', 'grp')), may hold values from 1024 to 4096, as said below
- nucleus_cell: int32 [32, 4, 512], P(('slab', 'grp')), may hold values from 0 to 32767
- nucleus_count: int32 [32, 4, 512], P(('slab', 'grp')), may hold values from 1 to 8
- migrant_rows: int32 [32, 2, 512], P(('slab', 'grp')), may hold values from 0 to 4095, as said below
- migrant_count: int32 [32, 2], P(('slab', 'grp')), may hold values from 0 to 512
Outputs:
- saturation_out: float32 [32, 64, 256], P(('slab', 'grp'))
- size_out: float32 [131072], P(('slab', 'grp'))
- arrivals: float32 [32, 2, 2, 512], P(('slab', 'grp'))
Inputs may be any that keep to these rules, and one draw needn't show every extreme that they name: `live_count`: about a quarter of the devices hold exactly 4096 live rows, the others a quarter to a third of that. `migrant_rows`: rows of the device's own parcels below its live count, all distinct; the list toward the lower slab lies in the lower half of the live rows, the other in the upper half.
All inputs are finite; a program needn't handle non-finite values. No bound on the sum of `inlet_mask` on one device may be relied on, other than what follows from the above.
Results may differ from a plain program's by a relative error of at most 0.00007.
Values sent between devices are 32-bit elements; how exact they have to be, the bound alone decides.
No kernel may reach another device: no remote copies, remote signals or barrier semaphores. Data moves between devices by JAX's collectives and lax.ppermute only.
A program may use at most 64 MiB of HBM per device.

v0:
```python
import jax
import jax.numpy as jnp
from jax import lax
from jax.sharding import PartitionSpec as P

BLOCK = 2048
STEPS = 2
SUBS = 2


GROWTH = 0.08
VOLUME = 1.0
NUCLEATE = 0.02
DIFFUSE = 0.12
INLET = 4.0


def extended(cells, sides, width):
    for axis, dim in sides:
        count = lax.axis_size(axis)
        ends = count - 1
        head = lax.slice_in_dim(cells, 0, width, axis=dim)
        tail = lax.slice_in_dim(cells, cells.shape[dim] - width, cells.shape[dim], axis=dim)
        cells = jnp.concatenate(
            [
                lax.ppermute(tail, axis, [(i, (i + 1) % count) for i in range(ends)]),
                cells,
                lax.ppermute(head, axis, [((i + 1) % count, i) for i in range(ends)]),
            ],
            axis=dim,
        )
    return cells


def passed_along(value, axis, steps):
    count = lax.axis_size(axis)
    leading, last = (max(0, -steps), min(count, count - steps))
    return lax.ppermute(value, axis, [(source, source + steps) for source in range(leading, last)])


def transport(padded_x, inlet_weight):
    field_mid = padded_x[1:-1]
    padded_yz = jnp.pad(field_mid, ((0, 0), (1, 1), (1, 1)))
    beside = padded_x[2:] + padded_x[:-2]
    beside = beside + padded_yz[:, 2:, 1:-1] + padded_yz[:, :-2, 1:-1]
    beside = beside + padded_yz[:, 1:-1, 2:] + padded_yz[:, 1:-1, :-2]
    field_mid = field_mid + DIFFUSE * (beside - 6.0 * field_mid)
    return field_mid + inlet_weight * (INLET - field_mid)


def cell_tables(cells, line_count, line_width):
    line_of = cells // line_width
    place_of = cells % line_width
    hot_line = (line_of[:, None] == lax.iota(jnp.int32, line_count)[None, :]).astype(jnp.float32)
    hot_place = (place_of[:, None] == lax.iota(jnp.int32, line_width)[None, :]).astype(jnp.float32)
    return (hot_line, hot_place)


def read_cells(slab_lines, hot_line, hot_place):
    picked = jnp.dot(
        hot_line, slab_lines, precision=lax.Precision.HIGHEST, preferred_element_type=jnp.float32
    )
    return jnp.sum(picked * hot_place, axis=1)


def spread_cells(hot_line, hot_place, mass):
    return lax.dot_general(
        hot_line,
        hot_place * mass[:, None],
        (((0,), (0,)), ((), ())),
        precision=lax.Precision.HIGHEST,
        preferred_element_type=jnp.float32,
    )


def parcel_step(
    slab_lines, crystal, crystal_weight, crystal_cell, live_total, event_cell, event_count
):
    line_count, line_width = slab_lines.shape
    event_line, event_place = cell_tables(event_cell, line_count, line_width)
    event_mass = (
        event_count.astype(jnp.float32)
        * NUCLEATE
        * jax.nn.softplus(read_cells(slab_lines, event_line, event_place) - 1.0)
    )
    deposit = spread_cells(event_line, event_place, event_mass)

    def one_block(block_index, state_pair):
        sizes_now, deposit_now = state_pair
        first_row = block_index * BLOCK
        part_size = lax.dynamic_slice_in_dim(sizes_now, first_row, BLOCK)
        part_weight = lax.dynamic_slice_in_dim(crystal_weight, first_row, BLOCK)
        part_cell = lax.dynamic_slice_in_dim(crystal_cell, first_row, BLOCK)
        part_live = (first_row + lax.iota(jnp.int32, BLOCK) < live_total).astype(jnp.float32)
        hot_line, hot_place = cell_tables(part_cell, line_count, line_width)
        local_sat = read_cells(slab_lines, hot_line, hot_place)
        enlarged = part_size + part_live * GROWTH * jax.nn.softplus(local_sat - 1.0)
        consumed = (
            part_live
            * part_weight
            * VOLUME
            * (enlarged * enlarged * enlarged - part_size * part_size * part_size)
        )
        sizes_now = lax.dynamic_update_slice_in_dim(sizes_now, enlarged, first_row, 0)
        return (sizes_now, deposit_now + spread_cells(hot_line, hot_place, consumed))

    block_count = (live_total + BLOCK - 1) // BLOCK
    crystal, deposit = lax.fori_loop(0, block_count, one_block, (crystal, deposit))
    return (crystal, deposit)


def local(
    saturation,
    inlet_mask,
    crystal_size,
    crystal_weight,
    crystal_cell,
    live_count,
    nucleus_cell,
    nucleus_count,
    migrant_rows,
    migrant_count,
):
    width_z = saturation.shape[2]
    parcels = crystal_size.shape[0]
    slots = migrant_rows.shape[2]
    live_total = live_count[0]
    active_rows = (lax.iota(jnp.int32, parcels) < live_total).astype(jnp.float32)
    inlet_weight = inlet_mask.astype(jnp.float32)
    crystal = crystal_size
    field = saturation
    for step_index in range(STEPS):
        for sub_index in range(SUBS):
            substep = step_index * SUBS + sub_index
            slab_field = lax.all_gather(field, "grp", axis=0, tiled=True)
            crystal, deposit = parcel_step(
                slab_field.reshape(-1, width_z),
                crystal,
                crystal_weight,
                crystal_cell,
                live_total,
                nucleus_cell[0, substep],
                nucleus_count[0, substep],
            )
            field = field - lax.psum_scatter(
                deposit.reshape(slab_field.shape), "grp", scatter_dimension=0, tiled=True
            )
        padded_x = extended(field, ((("slab", "grp"), 0),), 1)
        field = transport(padded_x, inlet_weight)
    size_out = active_rows * crystal
    rows = migrant_rows[0]
    slot_live = (lax.iota(jnp.int32, slots)[None, :] < migrant_count[0][:, None]).astype(
        jnp.float32
    )
    sent = (
        jnp.stack([jnp.take(size_out, rows), jnp.take(crystal_weight, rows)], axis=1)
        * slot_live[:, None, :]
    )
    from_lower = passed_along(sent[1], "slab", 1)
    from_upper = passed_along(sent[0], "slab", -1)
    arrivals = jnp.stack([from_lower, from_upper], axis=0)[None]
    return (field, size_out, arrivals)


def solution(mesh):
    in_specs = (
        P(("slab", "grp"), None, None),
        P(("slab", "grp"), None, None),
        P(("slab", "grp")),
        P(("slab", "grp")),
        P(("slab", "grp")),
        P(("slab", "grp")),
        P(("slab", "grp"), None, None),
        P(("slab", "grp"), None, None),
        P(("slab", "grp"), None, None),
        P(("slab", "grp"), None),
    )
    out_specs = (
        P(("slab", "grp"), None, None),
        P(("slab", "grp")),
        P(("slab", "grp"), None, None, None),
    )
    return jax.shard_map(local, mesh=mesh, in_specs=in_specs, out_specs=out_specs, check_vma=False)
```

profile of v0, /device:TPU:8, one launch (start us, length us, event | category | flops | bytes accessed | tf_op | source)
XLA Modules:
  0.0 130.5 jit_solution(16329384678726518906)
XLA Ops:
  7.2 0.0 reduce-scatter.5.cloned.1.call-start
  7.9 0.9 convert_multiply_fusion
  8.7 2.1 %all_gather.12 = f32[2,64,256]{2,1,0:T(8,128)S(1)} all-gather(f32[1,64,256]{2,1,0:T(8,128)} %param.20), channel_id=1, replica_groups=mesh['slab'=16,'grp'=2] {'grp'}, dimensions={0}, use_global_device_ids=true | all-gather | bytes 196608 | tf_op jit(solution)/shard_map/all_gather | solution.py:135
  10.9 0.5 fusion.76
  11.5 0.5 fusion.86
  12.0 0.2 copy-done
  12.2 4.4 %while.56 = (s32[]{:T(128)}, f32[4096]{0:T(1024)S(1)}, f32[128,256]{1,0:T(8,128)S(1)}, s32[]{:T(128)}, s32[]{:T(128)}, /*index=5*/s32[4096]{0:T(1024)S(1)}, f32[...) while((s32[]{:T(128)}, f32[4096]{0:T(1024)S(1)}, ...), condition=%wide.region_3.4_spmd, body=%wide.region_1.3_spmd.sunk | while | flops 1614141440 | bytes 536771 | solution.py:108
  12.2 1.7 %fusion.184 = f32[2048]{0:T(1024)S(1)} fusion(f32[128,256]{1,0:T(8,128)S(1)} %get-tuple-element.810, s32[2048]{0:T(1024)S(1)} %add_select_fusion.25, s32[2048]{0:T(1024)S(1)} %get-tuple-element.741), kind=kOutput, calls=%fused_computation.6.clone.1 | convolution fusion | flops 807139328 | bytes 155648 | tf_op jit(solution)/shard_map/while/body/dot_general | solution.py:60
  13.9 0.7 fusion.185
  14.6 0.3 dynamic_update_slice.28
  14.9 1.7 %fusion.186 = f32[128,256]{1,0:T(8,128)S(1)} fusion(f32[128,256]{1,0:T(8,128)S(1)} %get-tuple-element.794, f32[2048]{0:T(1024)S(1)} %get-tuple-element.743, s32[2048]{0:T(1024)S(1)} %add_select_fusion.25, s32[2048]{0:T(1024)S(1)} %get-tuple-element.741), kind=kOutput, calls=%fused_computation.7.clone.1 | convolution fusion | flops 806912000 | bytes 286720 | tf_op jit(solution)/shard_map/while/body/dot_general | solution.py:67
  16.6 0.6 copy-done.6
  17.3 0.0 reduce-scatter.7.cloned.1.call-start
  17.4 13.2 %reduce-scatter.5.cloned.1.call-done = f32[1,64,256]{2,1,0:T(8,128)} async-done(((f32[2,64,256]{2,1,0:T(8,128)}), f32[1,64,256]{2,1,0:T(8,128)}) %reduce-scatter.5.cloned.1.call-update) | async-done | bytes 65552 | tf_op jit(solution)/shard_map/reduce_scatter | solution.py:145
  30.6 0.8 sub.125
  31.4 1.9 %all_gather.13 = f32[2,64,256]{2,1,0:T(8,128)S(1)} all-gather(f32[1,64,256]{2,1,0:T(8,128)S(1)} %sub.125), channel_id=1, replica_groups=mesh['slab'=16,'grp'=2] {'grp'}, dimensions={0}, use_global_device_ids=true | all-gather | bytes 196608 | tf_op jit(solution)/shard_map/all_gather | solution.py:135
  33.3 0.5 fusion.77
  33.9 0.5 fusion.84
  34.4 4.4 %while.57 = (s32[]{:T(128)}, f32[4096]{0:T(1024)S(1)}, f32[128,256]{1,0:T(8,128)S(1)}, s32[]{:T(128)}, s32[]{:T(128)}, /*index=5*/s32[4096]{0:T(1024)S(1)}, f32[...) while((s32[]{:T(128)}, f32[4096]{0:T(1024)S(1)}, ...), condition=%wide.region_8.9_spmd, body=%wide.region_6.8_spmd.sunk | while | flops 1614141440 | bytes 536771 | solution.py:108
  34.4 1.7 %fusion.190 = f32[2048]{0:T(1024)S(1)} fusion(f32[128,256]{1,0:T(8,128)S(1)} %get-tuple-element.846, s32[2048]{0:T(1024)S(1)} %add_select_fusion.27, s32[2048]{0:T(1024)S(1)} %get-tuple-element.753), kind=kOutput, calls=%fused_computation.37.clone.1 | convolution fusion | flops 807139328 | bytes 155648 | tf_op jit(solution)/shard_map/while/body/dot_general | solution.py:60
  36.1 0.7 fusion.191
  36.8 0.3 dynamic_update_slice.29
  37.1 1.7 %fusion.192 = f32[128,256]{1,0:T(8,128)S(1)} fusion(f32[128,256]{1,0:T(8,128)S(1)} %get-tuple-element.830, f32[2048]{0:T(1024)S(1)} %get-tuple-element.755, s32[2048]{0:T(1024)S(1)} %add_select_fusion.27, s32[2048]{0:T(1024)S(1)} %get-tuple-element.753), kind=kOutput, calls=%fused_computation.38.clone.1 | convolution fusion | flops 806912000 | bytes 286720 | tf_op jit(solution)/shard_map/while/body/dot_general | solution.py:67
  38.8 0.6 copy-done.7
  39.5 0.0 reduce-scatter.9.cloned.1.call-start
  39.6 13.1 %reduce-scatter.7.cloned.1.call-done = f32[1,64,256]{2,1,0:T(8,128)} async-done(((f32[2,64,256]{2,1,0:T(8,128)}), f32[1,64,256]{2,1,0:T(8,128)}) %reduce-scatter.7.cloned.1.call-update) | async-done | bytes 65552 | tf_op jit(solution)/shard_map/reduce_scatter | solution.py:145
  52.7 0.8 sub.128
  53.6 4.2 %collective-permute-start = (f32[1,64,256]{2,1,0:T(8,128)S(1)}, f32[1,64,256]{2,1,0:T(8,128)S(1)}, u32[]{:S(2)}, u32[]{:S(2)}) collective-permute-start(f32[1,64,256]{2,1,0:T(8,128)S(1)} %sub.128), channel_id=1, source_target_pairs={{1,0},{2,1},{3,2},{4,3},{5,4},{6,5},{7,6},{8,7},{9,8},{10,9},{11,1... | collective-permute-start | bytes 196616 | tf_op jit(solution)/shard_map/ppermute | solution.py:28
  57.8 1.9 %collective-permute-start.1 = (f32[1,64,256]{2,1,0:T(8,128)S(1)}, f32[1,64,256]{2,1,0:T(8,128)S(1)}, u32[]{:S(2)}, u32[]{:S(2)}) collective-permute-start(f32[1,64,256]{2,1,0:T(8,128)S(1)} %sub.128), channel_id=1, source_target_pairs={{0,1},{1,2},{2,3},{3,4},{4,5},{5,6},{6,7},{7,8},{8,9},{9,10},{10,1... | collective-permute-start | bytes 196616 | tf_op jit(solution)/shard_map/ppermute | solution.py:26
  59.7 5.4 %collective-permute-done.1 = f32[1,64,256]{2,1,0:T(8,128)S(1)} collective-permute-done((f32[1,64,256]{2,1,0:T(8,128)S(1)}, f32[1,64,256]{2,1,0:T(8,128)S(1)}, u32[]{:S(2)}, u32[]{:S(2)}) %collective-permute-start.1) | collective-permute-done | bytes 65568 | tf_op jit(solution)/shard_map/ppermute | solution.py:26
  65.1 0.1 multiply_add_fusion.1
  65.3 1.9 %all_gather.14 = f32[2,64,256]{2,1,0:T(8,128)S(1)} all-gather(f32[1,64,256]{2,1,0:T(8,128)S(1)} %multiply_add_fusion.1), channel_id=1, replica_groups=mesh['slab'=16,'grp'=2] {'grp'}, dimensions={0}, use_global_device_ids=true | all-gather | bytes 196608 | tf_op jit(solution)/shard_map/all_gather | solution.py:135
  67.2 0.5 fusion.78
  67.7 0.5 fusion.82
  68.2 4.4 %while.58 = (s32[]{:T(128)}, f32[4096]{0:T(1024)S(1)}, f32[128,256]{1,0:T(8,128)S(1)}, s32[]{:T(128)}, s32[]{:T(128)}, /*index=5*/s32[4096]{0:T(1024)S(1)}, f32[...) while((s32[]{:T(128)}, f32[4096]{0:T(1024)S(1)}, ...), condition=%wide.region_13.14_spmd, body=%wide.region_11.13_spmd.sunk | while | flops 1614141440 | bytes 536771 | solution.py:108
  68.3 1.7 %fusion.196 = f32[2048]{0:T(1024)S(1)} fusion(f32[128,256]{1,0:T(8,128)S(1)} %get-tuple-element.882, s32[2048]{0:T(1024)S(1)} %add_select_fusion.29, s32[2048]{0:T(1024)S(1)} %get-tuple-element.765), kind=kOutput, calls=%fused_computation.68.clone.1 | convolution fusion | flops 807139328 | bytes 155648 | tf_op jit(solution)/shard_map/while/body/dot_general | solution.py:60
  69.9 0.7 fusion.197
  70.6 0.3 dynamic_update_slice.30
  70.9 1.7 %fusion.198 = f32[128,256]{1,0:T(8,128)S(1)} fusion(f32[128,256]{1,0:T(8,128)S(1)} %get-tuple-element.866, f32[2048]{0:T(1024)S(1)} %get-tuple-element.767, s32[2048]{0:T(1024)S(1)} %add_select_fusion.29, s32[2048]{0:T(1024)S(1)} %get-tuple-element.765), kind=kOutput, calls=%fused_computation.69.clone.1 | convolution fusion | flops 806912000 | bytes 286720 | tf_op jit(solution)/shard_map/while/body/dot_general | solution.py:67
  72.7 0.6 copy-done.8
  73.3 0.0 reduce-scatter.11.cloned.1.call-start
  73.4 0.1 compare_convert_fusion
  73.5 6.1 %gather_fusion.1 = f32[1024]{0:T(1024)S(1)} fusion(f32[4096]{0:T(1024)S(1)} %get-tuple-element.930, s32[1024]{0:T(1024)S(1)} %broadcast_clamp_fusion), kind=kCustom, calls=%fused_computation.1.clone | custom fusion | bytes 12288 | tf_op jit(solution)/shard_map/jit(_take)/gather | solution.py:156
  79.7 4.2 %reduce-scatter.9.cloned.1.call-done = f32[1,64,256]{2,1,0:T(8,128)} async-done(((f32[2,64,256]{2,1,0:T(8,128)}), f32[1,64,256]{2,1,0:T(8,128)}) %reduce-scatter.9.cloned.1.call-update) | async-done | bytes 65552 | tf_op jit(solution)/shard_map/reduce_scatter | solution.py:145
  83.8 0.8 sub.133
  84.7 2.1 %all_gather.15 = f32[2,64,256]{2,1,0:T(8,128)S(1)} all-gather(f32[1,64,256]{2,1,0:T(8,128)S(1)} %sub.133), channel_id=1, replica_groups=mesh['slab'=16,'grp'=2] {'grp'}, dimensions={0}, use_global_device_ids=true | all-gather | bytes 196608 | tf_op jit(solution)/shard_map/all_gather | solution.py:135
  86.8 0.5 fusion.79
  87.3 0.5 fusion.80
  87.8 4.4 %while.59 = (s32[]{:T(128)}, f32[4096]{0:T(1024)S(1)}, f32[128,256]{1,0:T(8,128)S(1)}, s32[]{:T(128)}, s32[]{:T(128)}, /*index=5*/s32[4096]{0:T(1024)S(1)}, f32[...) while((s32[]{:T(128)}, f32[4096]{0:T(1024)S(1)}, ...), condition=%wide.region_18.19_spmd, body=%wide.region_16.18_spmd.sunk | while | flops 1614141440 | bytes 536771 | solution.py:108
  87.9 1.7 %fusion.202 = f32[2048]{0:T(1024)S(1)} fusion(f32[128,256]{1,0:T(8,128)S(1)} %get-tuple-element.918, s32[2048]{0:T(1024)S(1)} %add_select_fusion.31, s32[2048]{0:T(1024)S(1)} %get-tuple-element.777), kind=kOutput, calls=%fused_computation.99.clone.1 | convolution fusion | flops 807139328 | bytes 155648 | tf_op jit(solution)/shard_map/while/body/dot_general | solution.py:60
  89.5 0.7 fusion.203
  90.2 0.3 dynamic_update_slice.31
  90.5 1.7 %fusion.204 = f32[128,256]{1,0:T(8,128)S(1)} fusion(f32[128,256]{1,0:T(8,128)S(1)} %get-tuple-element.902, f32[2048]{0:T(1024)S(1)} %get-tuple-element.779, s32[2048]{0:T(1024)S(1)} %add_select_fusion.31, s32[2048]{0:T(1024)S(1)} %get-tuple-element.777), kind=kOutput, calls=%fused_computation.100.clone.1 | convolution fusion | flops 806912000 | bytes 286720 | tf_op jit(solution)/shard_map/while/body/dot_general | solution.py:67
  92.3 0.6 copy-done.9
  93.0 6.2 %gather_fusion = f32[1024]{0:T(1024)S(1)} fusion(f32[4096]{0:T(1024)S(1)} %fusion.130, s32[1024]{0:T(1024)S(1)} %broadcast_clamp_fusion), kind=kCustom, calls=%fused_computation.clone | custom fusion | bytes 12288 | tf_op jit(solution)/shard_map/jit(_take)/gather | solution.py:156
  99.2 8.7 %collective-permute-start.5 = (f32[2,512]{1,0:T(2,128)S(1)}, f32[2,512]{1,0:T(2,128)S(1)}, u32[]{:S(2)}, u32[]{:S(2)}) collective-permute-start(f32[2,512]{1,0:T(2,128)S(1)} %get-tuple-element.529), channel_id=1, source_target_pairs={{2,0},{4,2},{6,4},{8,6},{10,8},{12,10},{14,12},{16,14},{18,16},{20... | collective-permute-start | bytes 12296 | tf_op jit(solution)/shard_map/ppermute | solution.py:38
  107.9 1.9 %collective-permute-start.4 = (f32[2,512]{1,0:T(2,128)S(1)}, f32[2,512]{1,0:T(2,128)S(1)}, u32[]{:S(2)}, u32[]{:S(2)}) collective-permute-start(f32[2,512]{1,0:T(2,128)S(1)} %get-tuple-element.528), channel_id=1, source_target_pairs={{0,2},{2,4},{4,6},{6,8},{8,10},{10,12},{12,14},{14,16},{16,18},{18... | collective-permute-start | bytes 12296 | tf_op jit(solution)/shard_map/ppermute | solution.py:38
  109.9 0.0 reduce-scatter.11.cloned.1.call-done
  109.9 0.8 sub.136
  110.8 5.1 %collective-permute-start.2 = (f32[1,64,256]{2,1,0:T(8,128)S(1)}, f32[1,64,256]{2,1,0:T(8,128)S(1)}, u32[]{:S(2)}, u32[]{:S(2)}) collective-permute-start(f32[1,64,256]{2,1,0:T(8,128)S(1)} %sub.136), channel_id=1, source_target_pairs={{1,0},{2,1},{3,2},{4,3},{5,4},{6,5},{7,6},{8,7},{9,8},{10,9},{11,1... | collective-permute-start | bytes 196616 | tf_op jit(solution)/shard_map/ppermute | solution.py:28
  115.8 1.9 %collective-permute-start.3 = (f32[1,64,256]{2,1,0:T(8,128)S(1)}, f32[1,64,256]{2,1,0:T(8,128)S(1)}, u32[]{:S(2)}, u32[]{:S(2)}) collective-permute-start(f32[1,64,256]{2,1,0:T(8,128)S(1)} %sub.136), channel_id=1, source_target_pairs={{0,1},{1,2},{2,3},{3,4},{4,5},{5,6},{6,7},{7,8},{8,9},{9,10},{10,1... | collective-permute-start | bytes 196616 | tf_op jit(solution)/shard_map/ppermute | solution.py:26
  117.8 0.6 maximum_bitcast_fusion
  118.4 4.8 %collective-permute-done.3 = f32[1,64,256]{2,1,0:T(8,128)S(1)} collective-permute-done((f32[1,64,256]{2,1,0:T(8,128)S(1)}, f32[1,64,256]{2,1,0:T(8,128)S(1)}, u32[]{:S(2)}, u32[]{:S(2)}) %collective-permute-start.3) | collective-permute-done | bytes 65568 | tf_op jit(solution)/shard_map/ppermute | solution.py:26
  123.2 0.7 multiply_add_fusion
  (57 shorter events, 0.5 us)
Async XLA Ops:
  7.2 3.7 %copy-start.11 = (s32[1,4,512]{2,1,0:T(4,128)S(1)}, s32[1,4,512]{2,1,0:T(4,128)}, u32[]{:S(2)}) copy-start(s32[1,4,512]{2,1,0:T(4,128)} %param.26) | copy-start | bytes 24580
  7.2 23.4 %reduce-scatter.5.cloned.1.call-start = ((), (), s32[]{:S(2)}) async-start(), calls=%async_computation.4 | async-start | bytes 196608 | tf_op jit(solution)/shard_map/reduce_scatter | solution.py:145
  11.4 0.7 copy-start
  11.5 0.7 copy-start.2
  11.5 0.7 copy-start.3
  16.6 0.7 copy-start.6
  16.6 13.9 %copy-start.4 = (f32[1,64,256]{2,1,0:T(8,128)S(1)}, f32[1,64,256]{2,1,0:T(8,128)}, u32[]{:S(2)}) copy-start(f32[1,64,256]{2,1,0:T(8,128)} %param.20) | copy-start | bytes 196612
  17.3 35.4 %reduce-scatter.7.cloned.1.call-start = ((), (), s32[]{:S(2)}) async-start(), calls=%async_computation.5 | async-start | bytes 196608 | tf_op jit(solution)/shard_map/reduce_scatter | solution.py:145
  38.8 0.7 copy-start.7
  38.8 0.7 copy-start.10
  39.5 25.6 %copy-start.5 = (s32[1,64,256]{2,1,0:T(8,128)S(1)}, s32[1,64,256]{2,1,0:T(8,128)}, u32[]{:S(2)}) copy-start(s32[1,64,256]{2,1,0:T(8,128)} %param.21) | copy-start | bytes 196612
  39.5 44.3 %reduce-scatter.9.cloned.1.call-start = ((), (), s32[]{:S(2)}) async-start(), calls=%async_computation.6 | async-start | bytes 196608 | tf_op jit(solution)/shard_map/reduce_scatter | solution.py:145
  53.6 6.1 %collective-permute-start = (f32[1,64,256]{2,1,0:T(8,128)S(1)}, f32[1,64,256]{2,1,0:T(8,128)S(1)}, u32[]{:S(2)}, u32[]{:S(2)}) collective-permute-start(f32[1,64,256]{2,1,0:T(8,128)S(1)} %sub.128), channel_id=1, source_target_pairs={{1,0},{2,1},{3,2},{4,3},{5,4},{6,5},{7,6},{8,7},{9,8},{10,9},{11,1... | collective-permute-start | bytes 196616 | tf_op jit(solution)/shard_map/ppermute | solution.py:28
  57.8 7.4 %collective-permute-start.1 = (f32[1,64,256]{2,1,0:T(8,128)S(1)}, f32[1,64,256]{2,1,0:T(8,128)S(1)}, u32[]{:S(2)}, u32[]{:S(2)}) collective-permute-start(f32[1,64,256]{2,1,0:T(8,128)S(1)} %sub.128), channel_id=1, source_target_pairs={{0,1},{1,2},{2,3},{3,4},{4,5},{5,6},{6,7},{7,8},{8,9},{9,10},{10,1... | collective-permute-start | bytes 196616 | tf_op jit(solution)/shard_map/ppermute | solution.py:26
  72.7 0.7 copy-start.8
  72.7 0.7 copy-start.12
  73.3 36.5 %reduce-scatter.11.cloned.1.call-start = ((), (), s32[]{:S(2)}) async-start(), calls=%async_computation.7 | async-start | bytes 196608 | tf_op jit(solution)/shard_map/reduce_scatter | solution.py:145
  92.3 0.7 copy-start.9
  93.0 6.2 %copy-start.1 = (f32[4096]{0:T(1024)}, f32[4096]{0:T(1024)S(1)}, u32[]{:S(2)}) copy-start(f32[4096]{0:T(1024)S(1)} %fusion.130) | copy-start | bytes 49156
  99.2 18.5 %collective-permute-start.5 = (f32[2,512]{1,0:T(2,128)S(1)}, f32[2,512]{1,0:T(2,128)S(1)}, u32[]{:S(2)}, u32[]{:S(2)}) collective-permute-start(f32[2,512]{1,0:T(2,128)S(1)} %get-tuple-element.529), channel_id=1, source_target_pairs={{2,0},{4,2},{6,4},{8,6},{10,8},{12,10},{14,12},{16,14},{18,16},{20... | collective-permute-start | bytes 12296 | tf_op jit(solution)/shard_map/ppermute | solution.py:38
  107.9 9.8 %collective-permute-start.4 = (f32[2,512]{1,0:T(2,128)S(1)}, f32[2,512]{1,0:T(2,128)S(1)}, u32[]{:S(2)}, u32[]{:S(2)}) collective-permute-start(f32[2,512]{1,0:T(2,128)S(1)} %get-tuple-element.528), channel_id=1, source_target_pairs={{0,2},{2,4},{4,6},{6,8},{8,10},{10,12},{12,14},{14,16},{16,18},{18... | collective-permute-start | bytes 12296 | tf_op jit(solution)/shard_map/ppermute | solution.py:38
  110.8 7.6 %collective-permute-start.2 = (f32[1,64,256]{2,1,0:T(8,128)S(1)}, f32[1,64,256]{2,1,0:T(8,128)S(1)}, u32[]{:S(2)}, u32[]{:S(2)}) collective-permute-start(f32[1,64,256]{2,1,0:T(8,128)S(1)} %sub.136), channel_id=1, source_target_pairs={{1,0},{2,1},{3,2},{4,3},{5,4},{6,5},{7,6},{8,7},{9,8},{10,9},{11,1... | collective-permute-start | bytes 196616 | tf_op jit(solution)/shard_map/ppermute | solution.py:28
  115.8 7.4 %collective-permute-start.3 = (f32[1,64,256]{2,1,0:T(8,128)S(1)}, f32[1,64,256]{2,1,0:T(8,128)S(1)}, u32[]{:S(2)}, u32[]{:S(2)}) collective-permute-start(f32[1,64,256]{2,1,0:T(8,128)S(1)} %sub.136), channel_id=1, source_target_pairs={{0,1},{1,2},{2,3},{3,4},{4,5},{5,6},{6,7},{7,8},{8,9},{9,10},{10,1... | collective-permute-start | bytes 196616 | tf_op jit(solution)/shard_map/ppermute | solution.py:26
Sparse Core Ops, SparseCore 0:
  17.4 13.0 reduce-scatter.4
  39.6 13.0 reduce-scatter.6
  73.5 10.3 reduce-scatter.8
  93.1 13.0 reduce-scatter.10
where the time goes:
time: 130 us
  waiting for transfers between devices  40.8 us (31%)
  starting transfers between devices  23.9 us (18%)
  matrix products  17.5 us (13%)
  local copies, waits for them, and re-layouts  16.5 us (13%)
  between operations  14.9 us (11%)
  other arithmetic  8.73 us (7%)
  blocking collectives  7.99 us (6%)
    reduce_scatter x4, waiting for transfers between devices, local(): lax.psum_scatter(deposit.reshape(slab_field.shape), 'grp', scatter_dimens...  30.5 us
    ppermute x2, starting transfers between devices, passed_along(): lax.ppermute(value, axis, [(source, source + steps) for source in range(l...  10.6 us
    ppermute x2, waiting for transfers between devices, extended(): lax.ppermute(tail, axis, [(i, (i + 1) % count) for i in range(ends)])  10.3 us
    ppermute x2, starting transfers between devices, extended(): lax.ppermute(head, axis, [((i + 1) % count, i) for i in range(ends)])  9.26 us
    dot_general x8, matrix products, read_cells(): jnp.dot(hot_line, slab_lines, precision=lax.Precision.HIGHEST, preferred_...  8.76 us
    dot_general x8, matrix products, spread_cells(): lax.dot_general(hot_line, hot_place * mass[:, None], (((0,), (0,)), ((),...  8.71 us
    all_gather x4, blocking collectives, local(): slab_field = lax.all_gather(field, 'grp', axis=0, tiled=True)  7.99 us
    gather x2, local copies, waits for them, and re-layouts, local(): jnp.take(size_out, rows)  6.16 us
  transfers between devices with their start and end apart: 10, of which 5 were waited for; matrix products, arithmetic and copies ran while one was open for 11% of the time, Pallas kernels for 0%

commit v1 on v0

v1 whole, which is shorter than its diff:
```python
import functools

import jax
import jax.numpy as jnp
from jax import lax
from jax.experimental import pallas as pl
from jax.experimental.pallas import tpu as pltpu
from jax.sharding import PartitionSpec as P

STEPS = 2
SUBS = 2

GROWTH = 0.08
NUCLEATE = 0.02
DIFFUSE = 0.12
INLET = 4.0

LANES = 128
F32 = jnp.float32
BF16 = jnp.bfloat16
NT = (((1,), (1,)), ((), ()))
NN = (((1,), (0,)), ((), ()))


def softplus(x):
    return jnp.maximum(x, 0.0) + jnp.log1p(jnp.exp(-jnp.abs(x)))


def pieces(x):
    high = x.astype(BF16)
    return high, (x - high.astype(F32)).astype(BF16)


def hot(count, row):
    width = row.shape[1]
    index = lax.broadcasted_iota(jnp.int32, (count, width), 0)
    return jnp.where(index == row, 1.0, 0.0).astype(BF16)


def moments_kernel(away, size, weight, cell, live, event_cell, event_count, out, left, right, event_left):
    rows = size.shape[0]
    lines, places = out.shape[1:]
    plane = lax.axis_index("grp")
    plane = 1 - plane if away else plane
    first_line = plane * lines
    number = lax.broadcasted_iota(jnp.int32, size.shape, 0) * LANES + lax.broadcasted_iota(jnp.int32, size.shape, 1)
    sizes = size[...]
    zeroth = jnp.where(number < live[0], weight[...], 0.0)
    first = zeroth * sizes
    second = first * sizes
    parts = [part for moment in (zeroth, first, second) for part in pieces(moment)]
    parts = [part.astype(F32) for part in parts]
    cells = cell[...]
    line = cells // places - first_line
    place = cells % places
    for r in range(rows):
        where = pl.ds(r * LANES, LANES)
        hot_line = hot(lines, line[r : r + 1])
        for c, part in enumerate(parts):
            left[pl.ds(c * lines, lines), where] = hot_line * part[r : r + 1].astype(BF16)
        right[:, where] = hot(places, place[r : r + 1])
    sums = lax.dot_general(left[...], right[...], NT, preferred_element_type=F32)
    for c in range(3):
        out[c] = sums[2 * c * lines : (2 * c + 1) * lines] + sums[(2 * c + 1) * lines : (2 * c + 2) * lines]
    for k in range(STEPS * SUBS):
        cells = event_cell[0, pl.ds(k, 1), :]
        counts = event_count[0, pl.ds(k, 1), :].astype(F32).astype(BF16)
        hot_line = hot(lines, cells // places - first_line) * counts
        out[3 + k] = lax.dot_general(hot_line, hot(places, cells % places), NT, preferred_element_type=F32)


def moments(away, size, weight, cell, live, event_cell, event_count, plane_shape):
    parcels = size.shape[0] * size.shape[1]
    lines, places = plane_shape
    return pl.pallas_call(
        functools.partial(moments_kernel, away),
        out_shape=jax.ShapeDtypeStruct((3 + STEPS * SUBS, lines, places), F32),
        in_specs=[pl.BlockSpec(memory_space=pltpu.VMEM)] * 3
        + [pl.BlockSpec(memory_space=pltpu.SMEM)]
        + [pl.BlockSpec(memory_space=pltpu.VMEM)] * 2,
        out_specs=pl.BlockSpec(memory_space=pltpu.VMEM),
        scratch_shapes=[
            pltpu.VMEM((6 * lines, parcels), BF16),
            pltpu.VMEM((places, parcels), BF16),
            pltpu.VMEM((lines, event_cell.shape[2]), BF16),
        ],
        compiler_params=pltpu.CompilerParams(vmem_limit_bytes=32 << 20),
        cost_estimate=pl.CostEstimate(flops=2 * 6 * lines * parcels * places, bytes_accessed=1 << 19, transcendentals=0),
        name="moments_away" if away else "moments_home",
    )(size, weight, cell, live, event_cell, event_count)


def substep(field, zeroth, first, second, counts, grown):
    rate = softplus(field - 1.0)
    growth = GROWTH * rate
    taken = growth * (3.0 * second + growth * (3.0 * first + growth * zeroth))
    field = field - (taken + counts * (NUCLEATE * rate))
    second = second + growth * (2.0 * first + growth * zeroth)
    first = first + growth * zeroth
    return field, first, second, grown + growth


def first_kernel(field, home, away, out, state):
    total = [home[c] + away[c] for c in range(home.shape[0])]
    zeroth, first, second = total[:3]
    now, grown = field[0], jnp.zeros_like(field[0])
    for k in range(SUBS):
        now, first, second, grown = substep(now, zeroth, first, second, total[3 + k], grown)
    out[0] = now
    for c, value in enumerate([zeroth, first, second, grown] + total[3 + SUBS :]):
        state[c] = value


def moved(field):
    lines, places = field.shape
    line = lax.broadcasted_iota(jnp.int32, field.shape, 0)
    place = lax.broadcasted_iota(jnp.int32, field.shape, 1)
    total = jnp.where(line == 0, 0.0, pltpu.roll(field, 1, 0))
    total += jnp.where(line == lines - 1, 0.0, pltpu.roll(field, lines - 1, 0))
    total += jnp.where(place == 0, 0.0, pltpu.roll(field, 1, 1))
    total += jnp.where(place == places - 1, 0.0, pltpu.roll(field, places - 1, 1))
    return total


def transport(field, beside, other, inlet):
    around = beside + other + moved(field)
    field = field + DIFFUSE * (around - 6.0 * field)
    return field + inlet * (INLET - field)


def second_kernel(field, beside, other, inlet, state, out):
    now = transport(field[0], beside[0], other[0], inlet[0].astype(F32))
    zeroth, first, second, grown = (state[c] for c in range(4))
    for k in range(SUBS):
        now, first, second, grown = substep(now, zeroth, first, second, state[4 + k], grown)
    out[0] = now
    out[1] = grown


def third_kernel(planes, received, partner, inlet, out):
    lines = out.shape[1]
    out[0] = transport(planes[0], received[pl.ds(0, lines)], partner[0], inlet[0].astype(F32))


def migrants_kernel(size, weight, cell, rows, count, keep, send):
    side = lax.axis_index("grp")
    table_rows = size.shape[0]
    slots = rows.shape[2]
    places = 256
    sizes, weights, cells = size[...], weight[...], cell[...]
    table = []
    for values in (sizes, weights):
        rest = values
        for _ in range(3):
            part = rest.astype(BF16)
            rest = rest - part.astype(F32)
            table.append(part)
    table += [(cells // places).astype(F32).astype(BF16), (cells % places).astype(F32).astype(BF16)]
    table = jnp.concatenate(table, axis=1)
    slot = lax.broadcasted_iota(jnp.int32, (1, slots), 1)
    for out, j in ((keep, side), (send, 1 - side)):
        row = jnp.where(j == 0, rows[0, 0:1, :], rows[0, 1:2, :])
        valid = jnp.where(slot < count[0, j], 1.0, 0.0)
        hot_row = hot(table_rows, row // LANES)
        picked = lax.dot_general(table, hot_row, (((0,), (0,)), ((), ())), preferred_element_type=F32)
        hot_lane = hot(LANES, row % LANES).astype(F32)
        found = [
            jnp.sum(picked[c * LANES : (c + 1) * LANES] * hot_lane, axis=0, keepdims=True) for c in range(8)
        ]
        out[0:1] = (found[0] + found[1] + found[2]) * valid
        out[1:2] = (found[3] + found[4] + found[5]) * valid
        out[2:3] = found[6]
        out[3:4] = found[7]
        out[4:5] = valid
        out[5:8] = jnp.zeros((3, slots), F32)


def grown_at(stacked, line, place):
    lines = stacked.shape[0] // 2
    picked = lax.dot_general(stacked, hot(stacked.shape[1], place), NN, preferred_element_type=F32)
    picked = picked[:lines] + picked[lines:]
    index = lax.broadcasted_iota(jnp.int32, picked.shape, 0)
    return jnp.sum(jnp.where(index == line, picked, 0.0), axis=0, keepdims=True)


def both_planes(mine, partner):
    side = lax.axis_index("grp")
    low = jnp.where(side == 0, mine, partner)
    high = jnp.where(side == 0, partner, mine)
    whole = jnp.concatenate([low, high], axis=0)
    return jnp.concatenate(pieces(whole), axis=0)


def leaving_kernel(planes, partner, kept, taken, out):
    lines, places = planes.shape[1:]
    stacked = both_planes(planes[1], partner[1])
    out[pl.ds(0, lines)] = planes[0]
    at = lines
    for part in (kept, taken):
        grown = grown_at(stacked, part[2:3].astype(jnp.int32), part[3:4].astype(jnp.int32))
        sizes = part[0:1] + grown * part[4:5]
        for row in (sizes, part[1:2]):
            for first in range(0, row.shape[1], places):
                out[at : at + 1] = row[:, first : first + places]
                at += 1


def sizes_kernel(planes, partner, size, cell, live, out):
    places = planes.shape[2]
    stacked = both_planes(planes[1], partner[1])
    cells = cell[...]
    line = cells // places
    place = cells % places
    number = lax.broadcasted_iota(jnp.int32, size.shape, 0) * LANES + lax.broadcasted_iota(jnp.int32, size.shape, 1)
    sizes = size[...]
    active = number < live[0]
    group = 4
    for r in range(0, size.shape[0], group):
        lines_now = jnp.concatenate([line[r + i : r + i + 1] for i in range(group)], axis=1)
        places_now = jnp.concatenate([place[r + i : r + i + 1] for i in range(group)], axis=1)
        grown = grown_at(stacked, lines_now, places_now)
        for i in range(group):
            out[r + i : r + i + 1] = grown[:, i * LANES : (i + 1) * LANES]
    out[...] = jnp.where(active, sizes + out[...], 0.0)


def arrivals_kernel(mine, relayed, out):
    side = lax.axis_index("grp")
    places = mine.shape[1]
    slots = out.shape[3]
    parts = slots // places
    for v in range(2):
        for p in range(parts):
            where = pl.ds(p * places, places)
            own = mine[v * parts + p : v * parts + p + 1]
            other = relayed[v * parts + p : v * parts + p + 1]
            out[0, 0, v : v + 1, where] = jnp.where(side == 0, own, other)
            out[0, 1, v : v + 1, where] = jnp.where(side == 0, other, own)


VMEM = pl.BlockSpec(memory_space=pltpu.VMEM)
SMEM = pl.BlockSpec(memory_space=pltpu.SMEM)


def call(kernel, out_shape, *args, smem=(), name=None):
    return pl.pallas_call(
        kernel,
        out_shape=out_shape,
        in_specs=[SMEM if i in smem else VMEM for i in range(len(args))],
        out_specs=jax.tree.map(lambda _: VMEM, out_shape),
        compiler_params=pltpu.CompilerParams(vmem_limit_bytes=16 << 20),
        name=name,
    )(*args)


def local(
    saturation,
    inlet_mask,
    crystal_size,
    crystal_weight,
    crystal_cell,
    live_count,
    nucleus_cell,
    nucleus_count,
    migrant_rows,
    migrant_count,
):
    plane_shape = saturation.shape[1:]
    lines, places = plane_shape
    slots = migrant_rows.shape[2]
    parcels = crystal_size.shape[0]
    shape = lambda *dims: jax.ShapeDtypeStruct(dims, F32)
    size, weight, cell = (a.reshape(-1, LANES) for a in (crystal_size, crystal_weight, crystal_cell))
    swap = lambda value: lax.ppermute(value, "grp", [(0, 1), (1, 0)])
    slabs, grps = lax.axis_size("slab"), lax.axis_size("grp")
    outward = []
    for s in range(slabs - 1):
        outward.append((s * grps + 1, (s + 1) * grps))
        outward.append(((s + 1) * grps, s * grps + 1))
    across = lambda value: lax.ppermute(value, ("slab", "grp"), outward)

    away = moments(True, size, weight, cell, live_count, nucleus_cell, nucleus_count, plane_shape)
    away = swap(away)
    home = moments(False, size, weight, cell, live_count, nucleus_cell, nucleus_count, plane_shape)
    field, state = call(
        first_kernel, (shape(1, lines, places), shape(4 + SUBS, lines, places)), saturation, home, away, name="first"
    )
    beside = across(field)
    other = swap(field)
    kept, given = call(
        migrants_kernel, (shape(8, slots), shape(8, slots)), size, weight, cell, migrant_rows, migrant_count, smem=(4,), name="migrants"
    )
    taken = swap(given)
    planes = call(second_kernel, shape(2, lines, places), field, beside, other, inlet_mask, state, name="second")
    partner = swap(planes)
    leaving = call(
        leaving_kernel, shape(lines + 4 * slots // places, places), planes, partner, kept, taken, name="leaving"
    )
    received = across(leaving)
    size_out = call(
        sizes_kernel, shape(parcels // LANES, LANES), planes, partner, size, cell, live_count, smem=(4,), name="sizes"
    )
    part = 2 * slots // places
    relayed = swap(received[lines : lines + part])
    mine = received[lines + part :]
    field_out = call(third_kernel, shape(1, lines, places), planes, received, partner, inlet_mask, name="third")
    arrivals = call(arrivals_kernel, shape(1, 2, 2, slots), mine, relayed, name="arrivals")
    return (field_out, size_out.reshape(-1), arrivals)


def solution(mesh):
    in_specs = (
        P(("slab", "grp"), None, None),
        P(("slab", "grp"), None, None),
        P(("slab", "grp")),
        P(("slab", "grp")),
        P(("slab", "grp")),
        P(("slab", "grp")),
        P(("slab", "grp"), None, None),
        P(("slab", "grp"), None, None),
        P(("slab", "grp"), None, None),
        P(("slab", "grp"), None),
    )
    out_specs = (
        P(("slab", "grp"), None, None),
        P(("slab", "grp")),
        P(("slab", "grp"), None, None, None),
    )
    return jax.shard_map(local, mesh=mesh, in_specs=in_specs, out_specs=out_specs, check_vma=False)
```

time: 130 us -> 32.1 us (0.25)
  the two profiles are of different devices: /device:TPU:8 before, /device:TPU:9 now
where the time goes in v1:
time: 32.1 us; the launch traced here: 31.5 us
  starting transfers between devices  10.5 us (33%)
  Pallas kernels  9.15 us (29%)
  waiting for transfers between devices  6.91 us (22%)
  local copies, waits for them, and re-layouts  3.56 us (11%)
  between operations  1.39 us (4%)
    ppermute x2, waiting for transfers between devices, local(): across = lambda value: lax.ppermute(value, ('slab', 'grp'), outward)  6.04 us
    ppermute x2, starting transfers between devices, local(): across = lambda value: lax.ppermute(value, ('slab', 'grp'), outward)  5.59 us
    pallas_call x7, Pallas kernels, call(): pl.pallas_call(kernel, out_shape=out_shape, in_specs=[SMEM if i in smem e...  5.16 us
    ppermute x5, starting transfers between devices, local(): swap = lambda value: lax.ppermute(value, 'grp', [(0, 1), (1, 0)])  4.9 us
    pallas_call x2, Pallas kernels, moments(): pl.pallas_call(functools.partial(moments_kernel, away), out_shape=jax.Sha...  3.99 us
    unnamed x18, local copies, waits for them, and re-layouts  3.56 us
    ppermute x5, waiting for transfers between devices, local(): swap = lambda value: lax.ppermute(value, 'grp', [(0, 1), (1, 0)])  0.88 us
  transfers between devices with their start and end apart: 7, of which 3 were waited for; matrix products, arithmetic and copies ran while one was open for 0% of the time, Pallas kernels for 18%

profile of v1, /device:TPU:9, one launch (start us, length us, event | category | flops | bytes accessed | tf_op | source)
XLA Modules:
  0.0 31.5 jit_solution(13708445295658604609)
XLA Ops:
  1.3 0.0 copy-start.1
  1.3 0.7 %copy-done.1 = f32[4096]{0:T(1024)S(1)} copy-done((f32[4096]{0:T(1024)S(1)}, f32[4096]{0:T(1024)}, u32[]{:S(2)}) %copy-start.1) | copy-done | bytes 16408
  2.0 0.0 copy-start.2
  2.0 0.7 %copy-done.2 = s32[4096]{0:T(1024)S(1)} copy-done((s32[4096]{0:T(1024)S(1)}, s32[4096]{0:T(1024)}, u32[]{:S(2)}) %copy-start.2) | copy-done | bytes 16408
  2.7 0.0 copy-start.4
  2.7 0.7 %copy-done.4 = f32[4096]{0:T(1024)S(1)} copy-done((f32[4096]{0:T(1024)S(1)}, f32[4096]{0:T(1024)}, u32[]{:S(2)}) %copy-start.4) | copy-done | bytes 16408
  3.4 0.0 copy-start.7
  3.4 0.7 %copy-done.7 = s32[1,4,512]{2,1,0:T(4,128)S(1)} copy-done((s32[1,4,512]{2,1,0:T(4,128)S(1)}, s32[1,4,512]{2,1,0:T(4,128)}, u32[]{:S(2)}) %copy-start.7) | copy-done | bytes 8216
  4.1 0.0 copy-start.8
  4.1 0.7 %copy-done.8 = s32[1,4,512]{2,1,0:T(4,128)S(1)} copy-done((s32[1,4,512]{2,1,0:T(4,128)S(1)}, s32[1,4,512]{2,1,0:T(4,128)}, u32[]{:S(2)}) %copy-start.8) | copy-done | bytes 8216
  4.8 2.0 %moments_away.1 = f32[7,64,256]{2,1,0:T(8,128)S(1)} custom-call(f32[32,128]{1,0:T(8,128)S(1)} %bitcast.4, f32[32,128]{1,0:T(8,128)S(1)} %bitcast.12, s32[32,128]{1,0:T(8,128)S(1)} %bitcast.8, s32[1]{0:T(128)S(6)} %copy.13.live, s32[1,4,512]{2,1,0:T(4,128)S(1)} %copy-done.7, s32[1,4,512]{2,1,0:T(4,128)S(1)} %copy-done.8), custom_call_target="tpu_custom_call" | custom-call | flops 805306368 | bytes 524288 | tf_op jit(solution)/shard_map/moments_away/pallas_call | solution.py:75
  6.8 0.0 copy-start.3
  6.8 0.7 %collective-permute-start = (f32[7,64,256]{2,1,0:T(8,128)S(1)}, f32[7,64,256]{2,1,0:T(8,128)S(1)}, u32[]{:S(2)}, u32[]{:S(2)}) collective-permute-start(f32[7,64,256]{2,1,0:T(8,128)S(1)} %moments_away.1), channel_id=1, source_target_pairs={{0,1},{1,0},{2,3},{3,2},{4,5},{5,4},{6,7},{7,6},{8,9},{9,8},{10,11... | collective-permute-start | bytes 1376264 | tf_op jit(solution)/shard_map/ppermute | solution.py:274
  7.6 2.0 %moments_home.1.home = f32[7,64,256]{2,1,0:T(8,128)S(1)} custom-call(f32[32,128]{1,0:T(8,128)S(1)} %bitcast.5, f32[32,128]{1,0:T(8,128)S(1)} %bitcast.13, s32[32,128]{1,0:T(8,128)S(1)} %bitcast.9, s32[1]{0:T(128)S(6)} %copy.13.live, s32[1,4,512]{2,1,0:T(4,128)S(1)} %copy-done.7, s32[1,4,512]{2,1,0:T(4,128)S(1)} %copy-done.8), custom_call_target="tpu_custom_call" | custom-call | flops 805306368 | bytes 524288 | tf_op jit(solution)/shard_map/moments_home/pallas_call | solution.py:75
  9.6 0.0 copy-start
  9.6 0.0 collective-permute-done.away
  9.6 0.0 copy-done.3
  9.6 0.2 first.1
  9.8 3.0 %collective-permute-start.1 = (f32[1,64,256]{2,1,0:T(8,128)S(1)}, f32[1,64,256]{2,1,0:T(8,128)S(1)}, u32[]{:S(2)}, u32[]{:S(2)}) collective-permute-start(f32[1,64,256]{2,1,0:T(8,128)S(1)} %get-tuple-element.7.field), channel_id=1, source_target_pairs={{1,2},{2,1},{3,4},{4,3},{5,6},{6,5},{7,8},{8,7},{9,10},{10,9},{11,... | collective-permute-start | bytes 196616 | tf_op jit(solution)/shard_map/ppermute | solution.py:280
  12.8 1.4 %collective-permute-start.2 = (f32[1,64,256]{2,1,0:T(8,128)S(1)}, f32[1,64,256]{2,1,0:T(8,128)S(1)}, u32[]{:S(2)}, u32[]{:S(2)}) collective-permute-start(f32[1,64,256]{2,1,0:T(8,128)S(1)} %get-tuple-element.7.field), channel_id=1, source_target_pairs={{0,1},{1,0},{2,3},{3,2},{4,5},{5,4},{6,7},{7,6},{8,9},{9,8},{10,11... | collective-permute-start | bytes 196616 | tf_op jit(solution)/shard_map/ppermute | solution.py:274
  14.2 1.9 %collective-permute-done.1.beside = f32[1,64,256]{2,1,0:T(8,128)S(1)} collective-permute-done((f32[1,64,256]{2,1,0:T(8,128)S(1)}, f32[1,64,256]{2,1,0:T(8,128)S(1)}, u32[]{:S(2)}, u32[]{:S(2)}) %collective-permute-start.1) | collective-permute-done | bytes 65568 | tf_op jit(solution)/shard_map/ppermute | solution.py:280
  16.1 0.0 collective-permute-done.2.other
  16.1 0.0 copy-done
  16.1 0.0 copy-start.5
  16.1 0.0 copy-start.6
  16.1 0.3 second.1.planes
  16.4 1.3 %collective-permute-start.3 = (f32[2,64,256]{2,1,0:T(8,128)S(1)}, f32[2,64,256]{2,1,0:T(8,128)S(1)}, u32[]{:S(2)}, u32[]{:S(2)}) collective-permute-start(f32[2,64,256]{2,1,0:T(8,128)S(1)} %second.1.planes), channel_id=1, source_target_pairs={{0,1},{1,0},{2,3},{3,2},{4,5},{5,4},{6,7},{7,6},{8,9},{9,8},{10,11... | collective-permute-start | bytes 393224 | tf_op jit(solution)/shard_map/ppermute | solution.py:274
  17.7 0.0 copy-done.5
  17.7 0.0 copy-done.6
  17.7 1.3 %migrants.1 = (f32[8,512]{1,0:T(8,128)S(1)}, f32[8,512]{1,0:T(8,128)S(1)}) custom-call(f32[32,128]{1,0:T(8,128)S(1)} %bitcast.6, f32[32,128]{1,0:T(8,128)S(1)} %bitcast.14, s32[32,128]{1,0:T(8,128)S(1)} %bitcast.10, s32[1,2,512]{2,1,0:T(2,128)S(1)} %copy-done.5, s32[1,2]{1,0:T(1,128)S(1)} %copy-done.6), custom_call_target="tpu_custom_call" | custom-call | tf_op jit(solution)/shard_map/migrants/pallas_call | solution.py:246
  19.0 0.4 %collective-permute-start.4 = (f32[8,512]{1,0:T(8,128)S(1)}, f32[8,512]{1,0:T(8,128)S(1)}, u32[]{:S(2)}, u32[]{:S(2)}) collective-permute-start(f32[8,512]{1,0:T(8,128)S(1)} %get-tuple-element.10), channel_id=1, source_target_pairs={{0,1},{1,0},{2,3},{3,2},{4,5},{5,4},{6,7},{7,6},{8,9},{9,8},{10,11... | collective-permute-start | bytes 49160 | tf_op jit(solution)/shard_map/ppermute | solution.py:274
  19.4 0.9 %collective-permute-done.4.taken = f32[8,512]{1,0:T(8,128)S(1)} collective-permute-done((f32[8,512]{1,0:T(8,128)S(1)}, f32[8,512]{1,0:T(8,128)S(1)}, u32[]{:S(2)}, u32[]{:S(2)}) %collective-permute-start.4) | collective-permute-done | bytes 16416 | tf_op jit(solution)/shard_map/ppermute | solution.py:274
  20.2 0.0 collective-permute-done.3.partner
  20.2 0.3 %leaving.1 = f32[72,256]{1,0:T(8,128)S(1)} custom-call(f32[2,64,256]{2,1,0:T(8,128)S(1)} %second.1.planes, f32[2,64,256]{2,1,0:T(8,128)S(1)} %collective-permute-done.3.partner, f32[8,512]{1,0:T(8,128)S(1)} %get-tuple-element.9.kept, f32[8,512]{1,0:T(8,128)S(1)} %collective-permute-done.4.taken), custom_call_target="tpu_custom_call" | custom-call | tf_op jit(solution)/shard_map/leaving/pallas_call | solution.py:246
  20.6 2.6 %collective-permute-start.5 = (f32[72,256]{1,0:T(8,128)S(1)}, f32[72,256]{1,0:T(8,128)S(1)}, u32[]{:S(2)}, u32[]{:S(2)}) collective-permute-start(f32[72,256]{1,0:T(8,128)S(1)} %leaving.1), channel_id=1, source_target_pairs={{1,2},{2,1},{3,4},{4,3},{5,6},{6,5},{7,8},{8,7},{9,10},{10,9},{11,... | collective-permute-start | bytes 221192 | tf_op jit(solution)/shard_map/ppermute | solution.py:280
  23.1 4.2 %collective-permute-done.5.received = f32[72,256]{1,0:T(8,128)S(1)} collective-permute-done((f32[72,256]{1,0:T(8,128)S(1)}, f32[72,256]{1,0:T(8,128)S(1)}, u32[]{:S(2)}, u32[]{:S(2)}) %collective-permute-start.5) | collective-permute-done | bytes 73760 | tf_op jit(solution)/shard_map/ppermute | solution.py:280
  27.3 1.1 %collective-permute-start.6 = (f32[4,256]{1,0:T(4,128)S(1)}, f32[4,256]{1,0:T(4,128)S(1)}, u32[]{:S(2)}, u32[]{:S(2)}) collective-permute-start(f32[4,256]{1,0:T(4,128)S(1)} %get-tuple-element.11), channel_id=1, source_target_pairs={{0,1},{1,0},{2,3},{3,2},{4,5},{5,4},{6,7},{7,6},{8,9},{9,8},{10,11... | collective-permute-start | bytes 12296 | tf_op jit(solution)/shard_map/ppermute | solution.py:274
  28.4 1.7 %sizes.1 = f32[32,128]{1,0:T(8,128)} custom-call(f32[2,64,256]{2,1,0:T(8,128)S(1)} %second.1.planes, f32[2,64,256]{2,1,0:T(8,128)S(1)} %collective-permute-done.3.partner, f32[32,128]{1,0:T(8,128)S(1)} %bitcast.7, s32[32,128]{1,0:T(8,128)S(1)} %bitcast.11, s32[1]{0:T(128)S(6)} %copy.13.live), custom_call_target="tpu_custom_call" | custom-call | tf_op jit(solution)/shard_map/sizes/pallas_call | solution.py:246
  30.1 0.8 %third.1 = f32[1,64,256]{2,1,0:T(8,128)} custom-call(f32[2,64,256]{2,1,0:T(8,128)S(1)} %second.1.planes, f32[72,256]{1,0:T(8,128)S(1)} %collective-permute-done.5.received, f32[2,64,256]{2,1,0:T(8,128)S(1)} %collective-permute-done.3.partner, s32[1,64,256]{2,1,0:T(8,128)S(1)} %copy-done), custom_call_target="tpu_custom_call" | custom-call | tf_op jit(solution)/shard_map/third/pallas_call | solution.py:246
  30.9 0.0 collective-permute-done.6.relayed
  30.9 0.6 %arrivals.1 = f32[1,2,2,512]{3,2,1,0:T(2,128)} custom-call(f32[4,256]{1,0:T(4,128)S(1)} %get-tuple-element.12.mine, f32[4,256]{1,0:T(4,128)S(1)} %collective-permute-done.6.relayed), custom_call_target="tpu_custom_call" | custom-call | tf_op jit(solution)/shard_map/arrivals/pallas_call | solution.py:246
  (1 shorter events, 0.0 us)
Async XLA Ops:
  1.3 0.7 %copy-start.1 = (f32[4096]{0:T(1024)S(1)}, f32[4096]{0:T(1024)}, u32[]{:S(2)}) copy-start(f32[4096]{0:T(1024)} %param.12) | copy-start | bytes 49156
  2.0 0.7 %copy-start.2 = (s32[4096]{0:T(1024)S(1)}, s32[4096]{0:T(1024)}, u32[]{:S(2)}) copy-start(s32[4096]{0:T(1024)} %param.14) | copy-start | bytes 49156
  2.7 0.7 %copy-start.4 = (f32[4096]{0:T(1024)S(1)}, f32[4096]{0:T(1024)}, u32[]{:S(2)}) copy-start(f32[4096]{0:T(1024)} %param.13) | copy-start | bytes 49156
  3.4 0.7 %copy-start.7 = (s32[1,4,512]{2,1,0:T(4,128)S(1)}, s32[1,4,512]{2,1,0:T(4,128)}, u32[]{:S(2)}) copy-start(s32[1,4,512]{2,1,0:T(4,128)} %event_cell.3) | copy-start | bytes 24580
  4.1 0.7 %copy-start.8 = (s32[1,4,512]{2,1,0:T(4,128)S(1)}, s32[1,4,512]{2,1,0:T(4,128)}, u32[]{:S(2)}) copy-start(s32[1,4,512]{2,1,0:T(4,128)} %event_count.3) | copy-start | bytes 24580
  6.8 2.8 %copy-start.3 = (f32[1,64,256]{2,1,0:T(8,128)S(1)}, f32[1,64,256]{2,1,0:T(8,128)}, u32[]{:S(2)}) copy-start(f32[1,64,256]{2,1,0:T(8,128)} %field.1) | copy-start | bytes 196612
  6.8 2.8 %collective-permute-start = (f32[7,64,256]{2,1,0:T(8,128)S(1)}, f32[7,64,256]{2,1,0:T(8,128)S(1)}, u32[]{:S(2)}, u32[]{:S(2)}) collective-permute-start(f32[7,64,256]{2,1,0:T(8,128)S(1)} %moments_away.1), channel_id=1, source_target_pairs={{0,1},{1,0},{2,3},{3,2},{4,5},{5,4},{6,7},{7,6},{8,9},{9,8},{10,11... | collective-permute-start | bytes 1376264 | tf_op jit(solution)/shard_map/ppermute | solution.py:274
  9.6 6.5 %copy-start = (s32[1,64,256]{2,1,0:T(8,128)S(1)}, s32[1,64,256]{2,1,0:T(8,128)}, u32[]{:S(2)}) copy-start(s32[1,64,256]{2,1,0:T(8,128)} %inlet.3) | copy-start | bytes 196612
  9.8 6.3 %collective-permute-start.1 = (f32[1,64,256]{2,1,0:T(8,128)S(1)}, f32[1,64,256]{2,1,0:T(8,128)S(1)}, u32[]{:S(2)}, u32[]{:S(2)}) collective-permute-start(f32[1,64,256]{2,1,0:T(8,128)S(1)} %get-tuple-element.7.field), channel_id=1, source_target_pairs={{1,2},{2,1},{3,4},{4,3},{5,6},{6,5},{7,8},{8,7},{9,10},{10,9},{11,... | collective-permute-start | bytes 196616 | tf_op jit(solution)/shard_map/ppermute | solution.py:280
  12.8 3.3 %collective-permute-start.2 = (f32[1,64,256]{2,1,0:T(8,128)S(1)}, f32[1,64,256]{2,1,0:T(8,128)S(1)}, u32[]{:S(2)}, u32[]{:S(2)}) collective-permute-start(f32[1,64,256]{2,1,0:T(8,128)S(1)} %get-tuple-element.7.field), channel_id=1, source_target_pairs={{0,1},{1,0},{2,3},{3,2},{4,5},{5,4},{6,7},{7,6},{8,9},{9,8},{10,11... | collective-permute-start | bytes 196616 | tf_op jit(solution)/shard_map/ppermute | solution.py:274
  16.1 1.6 %copy-start.5 = (s32[1,2,512]{2,1,0:T(2,128)S(1)}, s32[1,2,512]{2,1,0:T(2,128)}, u32[]{:S(2)}) copy-start(s32[1,2,512]{2,1,0:T(2,128)} %rows.1) | copy-start | bytes 12292
  16.1 1.6 %copy-start.6 = (s32[1,2]{1,0:T(1,128)S(1)}, s32[1,2]{1,0:T(1,128)}, u32[]{:S(2)}) copy-start(s32[1,2]{1,0:T(1,128)} %count.1) | copy-start | bytes 28
  16.4 3.8 %collective-permute-start.3 = (f32[2,64,256]{2,1,0:T(8,128)S(1)}, f32[2,64,256]{2,1,0:T(8,128)S(1)}, u32[]{:S(2)}, u32[]{:S(2)}) collective-permute-start(f32[2,64,256]{2,1,0:T(8,128)S(1)} %second.1.planes), channel_id=1, source_target_pairs={{0,1},{1,0},{2,3},{3,2},{4,5},{5,4},{6,7},{7,6},{8,9},{9,8},{10,11... | collective-permute-start | bytes 393224 | tf_op jit(solution)/shard_map/ppermute | solution.py:274
  19.0 1.2 %collective-permute-start.4 = (f32[8,512]{1,0:T(8,128)S(1)}, f32[8,512]{1,0:T(8,128)S(1)}, u32[]{:S(2)}, u32[]{:S(2)}) collective-permute-start(f32[8,512]{1,0:T(8,128)S(1)} %get-tuple-element.10), channel_id=1, source_target_pairs={{0,1},{1,0},{2,3},{3,2},{4,5},{5,4},{6,7},{7,6},{8,9},{9,8},{10,11... | collective-permute-start | bytes 49160 | tf_op jit(solution)/shard_map/ppermute | solution.py:274
  20.6 6.8 %collective-permute-start.5 = (f32[72,256]{1,0:T(8,128)S(1)}, f32[72,256]{1,0:T(8,128)S(1)}, u32[]{:S(2)}, u32[]{:S(2)}) collective-permute-start(f32[72,256]{1,0:T(8,128)S(1)} %leaving.1), channel_id=1, source_target_pairs={{1,2},{2,1},{3,4},{4,3},{5,6},{6,5},{7,8},{8,7},{9,10},{10,9},{11,... | collective-permute-start | bytes 221192 | tf_op jit(solution)/shard_map/ppermute | solution.py:280
  27.3 3.6 %collective-permute-start.6 = (f32[4,256]{1,0:T(4,128)S(1)}, f32[4,256]{1,0:T(4,128)S(1)}, u32[]{:S(2)}, u32[]{:S(2)}) collective-permute-start(f32[4,256]{1,0:T(4,128)S(1)} %get-tuple-element.11), channel_id=1, source_target_pairs={{0,1},{1,0},{2,3},{3,2},{4,5},{5,4},{6,7},{7,6},{8,9},{9,8},{10,11... | collective-permute-start | bytes 12296 | tf_op jit(solution)/shard_map/ppermute | solution.py:274

commit v2 on v1

v2 whole, which is shorter than its diff:
```python
import functools

import jax
import jax.numpy as jnp
from jax import lax
from jax.experimental import pallas as pl
from jax.experimental.pallas import tpu as pltpu
from jax.sharding import PartitionSpec as P

STEPS = 2
SUBS = 2

GROWTH = 0.08
NUCLEATE = 0.02
DIFFUSE = 0.12
INLET = 4.0

LANES = 128
F32 = jnp.float32
BF16 = jnp.bfloat16
NT = (((1,), (1,)), ((), ()))
NN = (((1,), (0,)), ((), ()))
TN = (((0,), (0,)), ((), ()))


def softplus(x):
    return jnp.maximum(x, 0.0) + jnp.log1p(jnp.exp(-jnp.abs(x)))


def pieces(x):
    high = x.astype(BF16)
    return high, (x - high.astype(F32)).astype(BF16)


def hot(count, row):
    index = lax.broadcasted_iota(jnp.int32, (count, row.shape[1]), 0)
    return jnp.where(index == row, 1.0, 0.0).astype(BF16)


def row_numbers(shape):
    return lax.broadcasted_iota(jnp.int32, shape, 0) * LANES + lax.broadcasted_iota(jnp.int32, shape, 1)


def swapped():
    slab = lax.axis_index("slab")
    return (slab == 0) | (slab == lax.axis_size("slab") - 1)


def sending_side():
    grp = lax.axis_index("grp")
    return jnp.where(swapped(), 1 - grp, grp)


def has_beside():
    slab, grp = lax.axis_index("slab"), lax.axis_index("grp")
    return jnp.where(grp == 0, slab > 0, slab < lax.axis_size("slab") - 1)


def across_pairs(slabs):
    last = slabs - 1
    up_out = lambda s: 0 if s == 0 else 1
    down_out = lambda s: 1 if s == last else 0
    pairs = [(s * 2 + up_out(s), (s + 1) * 2) for s in range(last)]
    pairs += [((s + 1) * 2 + down_out(s + 1), s * 2 + 1) for s in range(last)]
    return pairs + [(1, 0), (last * 2, last * 2 + 1)]


def plane_moments(plane, size, weight, cell, plane_shape):
    lines, places = plane_shape
    sizes = size[...]
    zeroth = weight[...]
    first = zeroth * sizes
    parts = [part.astype(F32) for moment in (zeroth, first, first * sizes) for part in pieces(moment)]
    line = cell[...] // places - plane * lines
    place = cell[...] % places
    group = 4
    sums = jnp.zeros((len(parts) * lines, places), F32)
    for start in range(0, sizes.shape[0], group):
        left, right = [], []
        for r in range(start, start + group):
            hot_line = hot(lines, line[r : r + 1])
            left.append(jnp.concatenate([hot_line * part[r : r + 1].astype(BF16) for part in parts], axis=0))
            right.append(hot(places, place[r : r + 1]))
        left, right = jnp.concatenate(left, axis=1), jnp.concatenate(right, axis=1)
        sums = sums + lax.dot_general(left, right, NT, preferred_element_type=F32)
    return [sums[2 * c * lines : (2 * c + 1) * lines] + sums[(2 * c + 1) * lines : (2 * c + 2) * lines] for c in range(3)]


def plane_counts(plane, event_cell, event_count, k, plane_shape):
    lines, places = plane_shape
    cells = event_cell[0, pl.ds(k, 1), :]
    counts = event_count[0, pl.ds(k, 1), :].astype(F32).astype(BF16)
    left = hot(lines, cells // places - plane * lines) * counts
    return lax.dot_general(left, hot(places, cells % places), NT, preferred_element_type=F32)


def away_kernel(*refs):
    inputs, live, out, kept, active, sems = refs[:8], refs[8], refs[9], refs[10:18], *refs[18:]
    copies = [pltpu.make_async_copy(src, dst, sems.at[i]) for i, (src, dst) in enumerate(zip(inputs, kept))]
    for copy in copies:
        copy.start()
    for copy in copies[:6]:
        copy.wait()
    size, weight, cell, event_cell, event_count, field = kept[:6]
    active[...] = jnp.where(row_numbers(size.shape) < live[0], 1.0, 0.0)
    weight[...] = weight[...] * active[...]
    plane_shape = out.shape[1:]
    plane = 1 - sending_side()
    for c, moment in enumerate(plane_moments(plane, size, weight, cell, plane_shape)):
        out[c] = moment
    for k in range(SUBS):
        out[3 + k] = plane_counts(plane, event_cell, event_count, k, plane_shape)
    out[3 + SUBS] = field[0]
    for copy in copies[6:]:
        copy.wait()


def home_kernel(size, weight, cell, event_cell, event_count, out, late):
    plane_shape = out.shape[1:]
    plane = sending_side()
    for c, moment in enumerate(plane_moments(plane, size, weight, cell, plane_shape)):
        out[c] = moment
    for k in range(SUBS):
        out[3 + k] = plane_counts(plane, event_cell, event_count, k, plane_shape)
    grp = lax.axis_index("grp")
    for k in range(SUBS):
        late[k] = plane_counts(grp, event_cell, event_count, SUBS + k, plane_shape)
        late[SUBS + k] = plane_counts(1 - grp, event_cell, event_count, SUBS + k, plane_shape)


def substep(field, zeroth, first, second, counts, grown):
    rate = softplus(field - 1.0)
    growth = GROWTH * rate
    taken = growth * (3.0 * second + growth * (3.0 * first + growth * zeroth))
    field = field - (taken + counts * (NUCLEATE * rate))
    second = second + growth * (2.0 * first + growth * zeroth)
    first = first + growth * zeroth
    return field, first, second, grown + growth


def first_kernel(field, home, away, late, out, state):
    now = jnp.where(swapped(), away[3 + SUBS], field[0])
    zeroth, first, second = (home[c] + away[c] for c in range(3))
    grown = jnp.zeros_like(now)
    for k in range(SUBS):
        now, first, second, grown = substep(now, zeroth, first, second, home[3 + k] + away[3 + k], grown)
    out[0] = now
    for c, value in enumerate((now, zeroth, first, second, grown)):
        state[c] = value
    for k in range(SUBS):
        state[5 + k] = late[SUBS + k]


def moved(field):
    lines, places = field.shape
    line = lax.broadcasted_iota(jnp.int32, field.shape, 0)
    place = lax.broadcasted_iota(jnp.int32, field.shape, 1)
    total = jnp.where(line == 0, 0.0, pltpu.roll(field, 1, 0))
    total += jnp.where(line == lines - 1, 0.0, pltpu.roll(field, lines - 1, 0))
    total += jnp.where(place == 0, 0.0, pltpu.roll(field, 1, 1))
    total += jnp.where(place == places - 1, 0.0, pltpu.roll(field, places - 1, 1))
    return total


def transport(field, beside, other, inlet):
    around = jnp.where(has_beside(), beside, 0.0) + other + moved(field)
    field = field + DIFFUSE * (around - 6.0 * field)
    return field + inlet * (INLET - field)


def second_kernel(beside, mine, other, late, inlet, given, out):
    lines = beside.shape[1]
    state = [jnp.where(swapped(), other[c], mine[c]) for c in range(5)]
    partner_field = jnp.where(swapped(), mine[0], other[0])
    now, zeroth, first, second, grown = state
    now = transport(now, beside[0], partner_field, inlet[0].astype(F32))
    for k in range(SUBS):
        now, first, second, grown = substep(now, zeroth, first, second, late[k] + other[5 + k], grown)
    out[pl.ds(0, lines)] = now
    out[pl.ds(lines, lines)] = grown
    out[pl.ds(2 * lines, given.shape[0])] = given[...]


def third_kernel(planes, received, partner, inlet, out):
    lines = out.shape[1]
    here = pl.ds(0, lines)
    out[0] = transport(planes[here], received[here], partner[here], inlet[0].astype(F32))


def migrants_kernel(size, weight, cell, rows, count, keep, give, *, places):
    side = sending_side()
    table_rows = size.shape[0]
    slots = rows.shape[2]
    table = []
    for values in (size[...], weight[...]):
        rest = values
        for _ in range(3):
            part = rest.astype(BF16)
            rest = rest - part.astype(F32)
            table.append(part)
    cells = cell[...]
    table += [(cells // places).astype(F32).astype(BF16), (cells % places).astype(F32).astype(BF16)]
    table = jnp.concatenate(table, axis=1)
    slot = lax.broadcasted_iota(jnp.int32, (1, slots), 1)
    for out, j in ((keep, side), (give, 1 - side)):
        row = jnp.where(j == 0, rows[0, 0:1, :], rows[0, 1:2, :])
        used = jnp.where(j == 0, count[0:1, 0:1], count[0:1, 1:2])
        valid = jnp.where(slot < used, 1.0, 0.0)
        picked = lax.dot_general(table, hot(table_rows, row // LANES), TN, preferred_element_type=F32)
        hot_lane = hot(LANES, row % LANES).astype(F32)
        found = [jnp.sum(picked[c * LANES : (c + 1) * LANES] * hot_lane, axis=0, keepdims=True) for c in range(8)]
        sizes = (found[0] + found[1] + found[2]) * valid
        weights = (found[3] + found[4] + found[5]) * valid
        at = 0
        for value in (sizes, weights, found[6], found[7], valid):
            for start in range(0, slots, places):
                out[at : at + 1] = value[:, start : start + places]
                at += 1
        out[at:] = jnp.zeros((out.shape[0] - at, places), F32)


def grown_at(stacked, line, place):
    lines = stacked.shape[0] // 2
    picked = lax.dot_general(stacked, hot(stacked.shape[1], place), NN, preferred_element_type=F32)
    picked = picked[:lines] + picked[lines:]
    index = lax.broadcasted_iota(jnp.int32, picked.shape, 0)
    return jnp.sum(jnp.where(index == line, picked, 0.0), axis=0, keepdims=True)


def both_planes(planes, partner, lines):
    grp = lax.axis_index("grp")
    mine, other = planes[pl.ds(lines, lines)], partner[pl.ds(lines, lines)]
    low = jnp.where(grp == 0, mine, other)
    high = jnp.where(grp == 0, other, mine)
    return jnp.concatenate(pieces(jnp.concatenate([low, high], axis=0)), axis=0)


def leaving_kernel(planes, partner, kept, out, *, lines, parts):
    stacked = both_planes(planes, partner, lines)
    here = pl.ds(0, lines)
    out[here] = jnp.where(swapped(), partner[here], planes[here])
    grp = lax.axis_index("grp")
    taken = partner[pl.ds(2 * lines, kept.shape[0])]
    keeping = kept[...]
    at = lines
    for one, other in ((keeping, taken), (taken, keeping)):
        part = jnp.where(grp == 0, one, other)
        rows = [part[i : i + 1] for i in range(5 * parts)]
        line = jnp.concatenate(rows[2 * parts : 3 * parts], axis=1).astype(jnp.int32)
        place = jnp.concatenate(rows[3 * parts : 4 * parts], axis=1).astype(jnp.int32)
        grown = grown_at(stacked, line, place)
        places = part.shape[1]
        for p in range(parts):
            out[at + p : at + p + 1] = rows[p] + grown[:, p * places : (p + 1) * places] * rows[4 * parts + p]
            out[at + parts + p : at + parts + p + 1] = rows[parts + p]
        at += 2 * parts


def sizes_kernel(planes, partner, size, cell, active, out, *, lines):
    places = planes.shape[1]
    stacked = both_planes(planes, partner, lines)
    cells = cell[...]
    line = cells // places
    place = cells % places
    group = 4
    found = []
    for start in range(0, size.shape[0], group):
        each = range(start, start + group)
        grown = grown_at(
            stacked,
            jnp.concatenate([line[r : r + 1] for r in each], axis=1),
            jnp.concatenate([place[r : r + 1] for r in each], axis=1),
        )
        found += [grown[:, i * LANES : (i + 1) * LANES] for i in range(group)]
    grown = jnp.concatenate(found, axis=0)
    out[...] = active[...] * (size[...] + grown)


def arrivals_kernel(received, relayed, out, *, lines, parts):
    slab, grp = lax.axis_index("slab"), lax.axis_index("grp")
    rows = 2 * parts
    pick = lambda block: jnp.where(grp == 0, block[:rows], block[rows:])
    mine = pick(received[pl.ds(lines, 2 * rows)])
    other = pick(relayed[...])
    lower = jnp.where(slab > 0, jnp.where(grp == 0, mine, other), 0.0)
    upper = jnp.where(slab < lax.axis_size("slab") - 1, jnp.where(grp == 0, other, mine), 0.0)
    places = mine.shape[1]
    for side, value in enumerate((lower, upper)):
        for v in range(2):
            for p in range(parts):
                at = v * parts + p
                out[0, side, v : v + 1, pl.ds(p * places, places)] = value[at : at + 1]


VMEM = pl.BlockSpec(memory_space=pltpu.VMEM)
SMEM = pl.BlockSpec(memory_space=pltpu.SMEM)
HBM = pl.BlockSpec(memory_space=pltpu.HBM)


def shape(*dims):
    return jax.ShapeDtypeStruct(dims, F32)


def call(kernel, out_shape, *args, name, cost=0, limit=16, scratch=(), specs=None):
    return pl.pallas_call(
        kernel,
        out_shape=out_shape,
        in_specs=specs or [VMEM] * len(args),
        out_specs=jax.tree.map(lambda _: VMEM, out_shape),
        scratch_shapes=scratch,
        compiler_params=pltpu.CompilerParams(vmem_limit_bytes=limit << 20),
        cost_estimate=pl.CostEstimate(flops=cost, bytes_accessed=0, transcendentals=0) if cost else None,
        name=name,
    )(*args)


def local(
    saturation,
    inlet_mask,
    crystal_size,
    crystal_weight,
    crystal_cell,
    live_count,
    nucleus_cell,
    nucleus_count,
    migrant_rows,
    migrant_count,
):
    lines, places = saturation.shape[1:]
    slots = migrant_rows.shape[2]
    parts = slots // places
    swap = lambda value: lax.ppermute(value, "grp", [(0, 1), (1, 0)])
    pairs = across_pairs(lax.axis_size("slab"))
    across = lambda value: lax.ppermute(value, ("slab", "grp"), pairs)

    inputs = [a.reshape(-1, LANES) for a in (crystal_size, crystal_weight, crystal_cell)]
    inputs += [nucleus_cell, nucleus_count, saturation, inlet_mask, migrant_rows]
    away, size, weight, cell, event_cell, event_count, field, inlet, rows, active = call(
        away_kernel,
        [shape(4 + SUBS, lines, places)]
        + [jax.ShapeDtypeStruct(a.shape, a.dtype) for a in inputs]
        + [shape(*inputs[0].shape)],
        *[pltpu.with_memory_space_constraint(a, pltpu.HBM) for a in inputs],
        live_count,
        specs=[HBM] * 8 + [SMEM],
        scratch=[pltpu.SemaphoreType.DMA((len(inputs),))],
        name="away",
    )
    away = swap(away)
    home, late = call(
        home_kernel,
        (shape(3 + SUBS, lines, places), shape(2 * SUBS, lines, places)),
        size, weight, cell, event_cell, event_count, cost=1 << 30, name="home",
    )
    front, mine = call(
        first_kernel, (shape(1, lines, places), shape(5 + SUBS, lines, places)), field, home, away, late, name="first"
    )
    beside = across(front)
    other = swap(mine)
    info = (shape(16, places), shape(16, places))
    kept, given = call(
        functools.partial(migrants_kernel, places=places), info, size, weight, cell, rows, migrant_count,
        cost=1 << 30, name="migrants",
    )
    planes = call(
        second_kernel, shape(2 * lines + 16, places), beside, mine, other, late, inlet, given, name="second"
    )
    partner = swap(planes)
    leaving = call(
        functools.partial(leaving_kernel, lines=lines, parts=parts),
        shape(lines + 4 * parts, places), planes, partner, kept, name="leaving",
    )
    received = across(leaving)
    size_out = call(
        functools.partial(sizes_kernel, lines=lines), shape(*size.shape), planes, partner, size, cell, active,
        cost=1 << 31, name="sizes",
    )
    relayed = swap(received[lines:])
    field_out = call(third_kernel, shape(1, lines, places), planes, received, partner, inlet, cost=1 << 28, name="third")
    arrivals = call(
        functools.partial(arrivals_kernel, lines=lines, parts=parts), shape(1, 2, 2, slots), received, relayed, name="arrivals"
    )
    return (field_out, size_out.reshape(-1), arrivals)


def solution(mesh):
    in_specs = (
        P(("slab", "grp"), None, None),
        P(("slab", "grp"), None, None),
        P(("slab", "grp")),
        P(("slab", "grp")),
        P(("slab", "grp")),
        P(("slab", "grp")),
        P(("slab", "grp"), None, None),
        P(("slab", "grp"), None, None),
        P(("slab", "grp"), None, None),
        P(("slab", "grp"), None),
    )
    out_specs = (
        P(("slab", "grp"), None, None),
        P(("slab", "grp")),
        P(("slab", "grp"), None, None, None),
    )
    return jax.shard_map(local, mesh=mesh, in_specs=in_specs, out_specs=out_specs, check_vma=False)
```

time: 32.1 us -> 21.5 us (0.67)
  starting transfers between devices: 10.5 us -> 6.44 us
  local copies, waits for them, and re-layouts: 3.56 us -> 0.01 us
  waiting for transfers between devices: 6.91 us -> 5.09 us
  Pallas kernels: 9.15 us -> 8.34 us
    unnamed x18 -> x2, local copies, waits for them, and re-layouts: 3.56 us -> 0.01 us
    ppermute x2, starting transfers between devices: 5.59 us -> 2.09 us  [local(): across = lambda value: lax.ppermute(value, ('slab', 'grp'), pairs)]
    ppermute x2, waiting for transfers between devices: 6.04 us -> 4 us  [local(): across = lambda value: lax.ppermute(value, ('slab', 'grp'), pairs)]
    pallas_call x9, Pallas kernels: 9.15 us -> 8.34 us  [call(): pl.pallas_call(kernel, out_shape=out_shape, in_specs=specs or [VMEM] * le...]
    ppermute x5 -> x4, starting transfers between devices: 4.9 us -> 4.35 us  [local(): swap = lambda value: lax.ppermute(value, 'grp', [(0, 1), (1, 0)])]
    ppermute x5 -> x4, waiting for transfers between devices: 0.88 us -> 1.09 us  [local(): swap = lambda value: lax.ppermute(value, 'grp', [(0, 1), (1, 0)])]
  transfers between devices with their start and end apart: 7 -> 6, of which waited for: 3 -> 4; matrix products, arithmetic and copies ran while one was open for 0% -> 0% of each run, Pallas kernels for 18% -> 22%
where the time goes in v2:
time: 21.5 us; the launch traced here: 21.2 us
  Pallas kernels  8.34 us (39%)
  starting transfers between devices  6.44 us (30%)
  waiting for transfers between devices  5.09 us (24%)
  between operations  1.33 us (6%)
    pallas_call x9, Pallas kernels, call(): pl.pallas_call(kernel, out_shape=out_shape, in_specs=specs or [VMEM] * le...  8.34 us
    ppermute x4, starting transfers between devices, local(): swap = lambda value: lax.ppermute(value, 'grp', [(0, 1), (1, 0)])  4.35 us
    ppermute x2, waiting for transfers between devices, local(): across = lambda value: lax.ppermute(value, ('slab', 'grp'), pairs)  4 us
    ppermute x2, starting transfers between devices, local(): across = lambda value: lax.ppermute(value, ('slab', 'grp'), pairs)  2.09 us
    ppermute x4, waiting for transfers between devices, local(): swap = lambda value: lax.ppermute(value, 'grp', [(0, 1), (1, 0)])  1.09 us
  transfers between devices with their start and end apart: 6, of which 4 were waited for; matrix products, arithmetic and copies ran while one was open for 0% of the time, Pallas kernels for 22%

profile of v2, /device:TPU:9, one launch (start us, length us, event | category | flops | bytes accessed | tf_op | source)
XLA Modules:
  0.0 21.2 jit_solution(8702165789599562477)
XLA Ops:
  1.3 2.2 %away.1 = (f32[6,64,256]{2,1,0:T(8,128)S(1)}, f32[32,128]{1,0:T(8,128)S(1)}, f32[32,128]{1,0:T(8,128)S(1)}, s32[32,128]{1,0:T(8,128)S(1)}, s32[1,4,512]{2,1,0:T(...) custom-call(f32[32,128]{1,0:T(8,128)} %bitcast.4, ...), custom_call_target="tpu_custom_call" | custom-call | tf_op jit(solution)/shard_map/away/pallas_call | solution.py:305
  3.4 0.7 %collective-permute-start = (f32[6,64,256]{2,1,0:T(8,128)S(1)}, f32[6,64,256]{2,1,0:T(8,128)S(1)}, u32[]{:S(2)}, u32[]{:S(2)}) collective-permute-start(f32[6,64,256]{2,1,0:T(8,128)S(1)} %get-tuple-element.26), channel_id=1, source_target_pairs={{0,1},{1,0},{2,3},{3,2},{4,5},{5,4},{6,7},{7,6},{8,9},{9,8},{10,11... | collective-permute-start | bytes 1179656 | tf_op jit(solution)/shard_map/ppermute | solution.py:332
  4.2 1.5 %home.1 = (f32[5,64,256]{2,1,0:T(8,128)S(1)}, f32[4,64,256]{2,1,0:T(8,128)S(1)}) custom-call(f32[32,128]{1,0:T(8,128)S(1)} %get-tuple-element.20.size, f32[32,128]{1,0:T(8,128)S(1)} %get-tuple-element.21.weight, s32[32,128]{1,0:T(8,128)S(1)} %get-tuple-element.22.cell, s32[1,4,512]{2,1,0:T(4,128)S(1)} %get-tuple-element.23.event_cell, ...), custom_call_target="tpu_custom_call" | custom-call | flops 1073741824 | tf_op jit(solution)/shard_map/home/pallas_call | solution.py:305
  5.7 0.0 collective-permute-done.away
  5.7 0.2 first.1
  5.9 0.3 %collective-permute-start.2 = (f32[7,64,256]{2,1,0:T(8,128)S(1)}, f32[7,64,256]{2,1,0:T(8,128)S(1)}, u32[]{:S(2)}, u32[]{:S(2)}) collective-permute-start(f32[7,64,256]{2,1,0:T(8,128)S(1)} %get-tuple-element.29.mine), channel_id=1, source_target_pairs={{0,1},{1,0},{2,3},{3,2},{4,5},{5,4},{6,7},{7,6},{8,9},{9,8},{10,11... | collective-permute-start | bytes 1376264 | tf_op jit(solution)/shard_map/ppermute | solution.py:332
  6.2 0.0 copy-start
  6.2 1.4 %collective-permute-start.1 = (f32[1,64,256]{2,1,0:T(8,128)S(1)}, f32[1,64,256]{2,1,0:T(8,128)S(1)}, u32[]{:S(2)}, u32[]{:S(2)}) collective-permute-start(f32[1,64,256]{2,1,0:T(8,128)S(1)} %get-tuple-element.28), channel_id=1, source_target_pairs={{0,2},{3,4},{5,6},{7,8},{9,10},{11,12},{13,14},{15,16},{17,18},{19... | collective-permute-start | bytes 196616 | tf_op jit(solution)/shard_map/ppermute | solution.py:334
  7.5 0.0 copy-done
  7.5 0.8 %migrants.1 = (f32[16,256]{1,0:T(8,128)S(1)}, f32[16,256]{1,0:T(8,128)S(1)}) custom-call(f32[32,128]{1,0:T(8,128)S(1)} %get-tuple-element.20.size, f32[32,128]{1,0:T(8,128)S(1)} %get-tuple-element.21.weight, s32[32,128]{1,0:T(8,128)S(1)} %get-tuple-element.22.cell, s32[1,2,512]{2,1,0:T(2,128)S(1)} %get-tuple-element.31.rows, s32[1,2]{1,0:T(1,128)S(1)} %copy-done), custom_call_target="tpu_custom_call" | custom-call | flops 1073741824 | tf_op jit(solution)/shard_map/migrants/pallas_call | solution.py:305
  8.3 1.7 %collective-permute-done.1.beside = f32[1,64,256]{2,1,0:T(8,128)S(1)} collective-permute-done((f32[1,64,256]{2,1,0:T(8,128)S(1)}, f32[1,64,256]{2,1,0:T(8,128)S(1)}, u32[]{:S(2)}, u32[]{:S(2)}) %collective-permute-start.1) | collective-permute-done | bytes 65568 | tf_op jit(solution)/shard_map/ppermute | solution.py:334
  10.1 0.0 collective-permute-done.2.other
  10.1 0.3 %second.1.planes = f32[144,256]{1,0:T(8,128)S(1)} custom-call(f32[1,64,256]{2,1,0:T(8,128)S(1)} %collective-permute-done.1.beside, f32[7,64,256]{2,1,0:T(8,128)S(1)} %get-tuple-element.29.mine, f32[7,64,256]{2,1,0:T(8,128)S(1)} %collective-permute-done.2.other, f32[4,64,256]{2,1,0:T(8,128)S(1)} %get-tuple-element.27.late, ...), custom_call_target="tpu_custom_call" | custom-call | tf_op jit(solution)/shard_map/second/pallas_call | solution.py:305
  10.4 2.0 %collective-permute-start.3 = (f32[144,256]{1,0:T(8,128)S(1)}, f32[144,256]{1,0:T(8,128)S(1)}, u32[]{:S(2)}, u32[]{:S(2)}) collective-permute-start(f32[144,256]{1,0:T(8,128)S(1)} %second.1.planes), channel_id=1, source_target_pairs={{0,1},{1,0},{2,3},{3,2},{4,5},{5,4},{6,7},{7,6},{8,9},{9,8},{10,11... | collective-permute-start | bytes 442376 | tf_op jit(solution)/shard_map/ppermute | solution.py:332
  12.4 1.0 %collective-permute-done.3.partner = f32[144,256]{1,0:T(8,128)S(1)} collective-permute-done((f32[144,256]{1,0:T(8,128)S(1)}, f32[144,256]{1,0:T(8,128)S(1)}, u32[]{:S(2)}, u32[]{:S(2)}) %collective-permute-start.3) | collective-permute-done | bytes 147488 | tf_op jit(solution)/shard_map/ppermute | solution.py:332
  13.4 0.3 %leaving.1 = f32[72,256]{1,0:T(8,128)S(1)} custom-call(f32[144,256]{1,0:T(8,128)S(1)} %second.1.planes, f32[144,256]{1,0:T(8,128)S(1)} %collective-permute-done.3.partner, f32[16,256]{1,0:T(8,128)S(1)} %get-tuple-element.33.kept), custom_call_target="tpu_custom_call" | custom-call | tf_op jit(solution)/shard_map/leaving/pallas_call | solution.py:305
  13.8 0.7 %collective-permute-start.4 = (f32[72,256]{1,0:T(8,128)S(1)}, f32[72,256]{1,0:T(8,128)S(1)}, u32[]{:S(2)}, u32[]{:S(2)}) collective-permute-start(f32[72,256]{1,0:T(8,128)S(1)} %leaving.1), channel_id=1, source_target_pairs={{0,2},{3,4},{5,6},{7,8},{9,10},{11,12},{13,14},{15,16},{17,18},{19... | collective-permute-start | bytes 221192 | tf_op jit(solution)/shard_map/ppermute | solution.py:334
  14.5 1.7 %sizes.1 = f32[32,128]{1,0:T(8,128)} custom-call(f32[144,256]{1,0:T(8,128)S(1)} %second.1.planes, f32[144,256]{1,0:T(8,128)S(1)} %collective-permute-done.3.partner, f32[32,128]{1,0:T(8,128)S(1)} %get-tuple-element.20.size, s32[32,128]{1,0:T(8,128)S(1)} %get-tuple-element.22.cell, f32[32,128]{1,0:T(8,128)S(1)} %get-tuple-element.34.active), custom_call_target="tpu_custom_call" | custom-call | flops 2147483648 | tf_op jit(solution)/shard_map/sizes/pallas_call | solution.py:305
  16.2 2.3 %collective-permute-done.4.received = f32[72,256]{1,0:T(8,128)S(1)} collective-permute-done((f32[72,256]{1,0:T(8,128)S(1)}, f32[72,256]{1,0:T(8,128)S(1)}, u32[]{:S(2)}, u32[]{:S(2)}) %collective-permute-start.4) | collective-permute-done | bytes 73760 | tf_op jit(solution)/shard_map/ppermute | solution.py:334
  18.5 1.3 %collective-permute-start.5 = (f32[8,256]{1,0:T(8,128)S(1)}, f32[8,256]{1,0:T(8,128)S(1)}, u32[]{:S(2)}, u32[]{:S(2)}) collective-permute-start(f32[8,256]{1,0:T(8,128)S(1)} %slice.4), channel_id=1, source_target_pairs={{0,1},{1,0},{2,3},{3,2},{4,5},{5,4},{6,7},{7,6},{8,9},{9,8},{10,11... | collective-permute-start | bytes 24584 | tf_op jit(solution)/shard_map/ppermute | solution.py:332
  19.8 0.8 %third.1 = f32[1,64,256]{2,1,0:T(8,128)} custom-call(f32[144,256]{1,0:T(8,128)S(1)} %second.1.planes, f32[72,256]{1,0:T(8,128)S(1)} %collective-permute-done.4.received, f32[144,256]{1,0:T(8,128)S(1)} %collective-permute-done.3.partner, s32[1,64,256]{2,1,0:T(8,128)S(1)} %get-tuple-element.30.inlet), custom_call_target="tpu_custom_call" | custom-call | flops 268435456 | tf_op jit(solution)/shard_map/third/pallas_call | solution.py:305
  20.5 0.1 collective-permute-done.5.relayed
  20.6 0.6 %arrivals.1 = f32[1,2,2,512]{3,2,1,0:T(2,128)} custom-call(f32[72,256]{1,0:T(8,128)S(1)} %collective-permute-done.4.received, f32[8,256]{1,0:T(8,128)S(1)} %collective-permute-done.5.relayed), custom_call_target="tpu_custom_call" | custom-call | tf_op jit(solution)/shard_map/arrivals/pallas_call | solution.py:305
  (1 shorter events, 0.0 us)
Async XLA Ops:
  3.4 2.2 %collective-permute-start = (f32[6,64,256]{2,1,0:T(8,128)S(1)}, f32[6,64,256]{2,1,0:T(8,128)S(1)}, u32[]{:S(2)}, u32[]{:S(2)}) collective-permute-start(f32[6,64,256]{2,1,0:T(8,128)S(1)} %get-tuple-element.26), channel_id=1, source_target_pairs={{0,1},{1,0},{2,3},{3,2},{4,5},{5,4},{6,7},{7,6},{8,9},{9,8},{10,11... | collective-permute-start | bytes 1179656 | tf_op jit(solution)/shard_map/ppermute | solution.py:332
  5.9 4.2 %collective-permute-start.2 = (f32[7,64,256]{2,1,0:T(8,128)S(1)}, f32[7,64,256]{2,1,0:T(8,128)S(1)}, u32[]{:S(2)}, u32[]{:S(2)}) collective-permute-start(f32[7,64,256]{2,1,0:T(8,128)S(1)} %get-tuple-element.29.mine), channel_id=1, source_target_pairs={{0,1},{1,0},{2,3},{3,2},{4,5},{5,4},{6,7},{7,6},{8,9},{9,8},{10,11... | collective-permute-start | bytes 1376264 | tf_op jit(solution)/shard_map/ppermute | solution.py:332
  6.2 1.4 %copy-start = (s32[1,2]{1,0:T(1,128)S(1)}, s32[1,2]{1,0:T(1,128)}, u32[]{:S(2)}) copy-start(s32[1,2]{1,0:T(1,128)} %count.1) | copy-start | bytes 28
  6.2 3.9 %collective-permute-start.1 = (f32[1,64,256]{2,1,0:T(8,128)S(1)}, f32[1,64,256]{2,1,0:T(8,128)S(1)}, u32[]{:S(2)}, u32[]{:S(2)}) collective-permute-start(f32[1,64,256]{2,1,0:T(8,128)S(1)} %get-tuple-element.28), channel_id=1, source_target_pairs={{0,2},{3,4},{5,6},{7,8},{9,10},{11,12},{13,14},{15,16},{17,18},{19... | collective-permute-start | bytes 196616 | tf_op jit(solution)/shard_map/ppermute | solution.py:334
  10.4 3.0 %collective-permute-start.3 = (f32[144,256]{1,0:T(8,128)S(1)}, f32[144,256]{1,0:T(8,128)S(1)}, u32[]{:S(2)}, u32[]{:S(2)}) collective-permute-start(f32[144,256]{1,0:T(8,128)S(1)} %second.1.planes), channel_id=1, source_target_pairs={{0,1},{1,0},{2,3},{3,2},{4,5},{5,4},{6,7},{7,6},{8,9},{9,8},{10,11... | collective-permute-start | bytes 442376 | tf_op jit(solution)/shard_map/ppermute | solution.py:332
  13.8 4.7 %collective-permute-start.4 = (f32[72,256]{1,0:T(8,128)S(1)}, f32[72,256]{1,0:T(8,128)S(1)}, u32[]{:S(2)}, u32[]{:S(2)}) collective-permute-start(f32[72,256]{1,0:T(8,128)S(1)} %leaving.1), channel_id=1, source_target_pairs={{0,2},{3,4},{5,6},{7,8},{9,10},{11,12},{13,14},{15,16},{17,18},{19... | collective-permute-start | bytes 221192 | tf_op jit(solution)/shard_map/ppermute | solution.py:334
  18.5 2.1 %collective-permute-start.5 = (f32[8,256]{1,0:T(8,128)S(1)}, f32[8,256]{1,0:T(8,128)S(1)}, u32[]{:S(2)}, u32[]{:S(2)}) collective-permute-start(f32[8,256]{1,0:T(8,128)S(1)} %slice.4), channel_id=1, source_target_pairs={{0,1},{1,0},{2,3},{3,2},{4,5},{5,4},{6,7},{7,6},{8,9},{9,8},{10,11... | collective-permute-start | bytes 24584 | tf_op jit(solution)/shard_map/ppermute | solution.py:332

commit v3 on v2

--- a/solution.py
+++ b/solution.py
@@ -41,27 +41,42 @@
     return lax.broadcasted_iota(jnp.int32, shape, 0) * LANES + lax.broadcasted_iota(jnp.int32, shape, 1)
 
 
-def swapped():
+def ends():
     slab = lax.axis_index("slab")
     return (slab == 0) | (slab == lax.axis_size("slab") - 1)
 
 
+def sends_other():
+    return ends() | (lax.axis_index("slab") % 2 == 0)
+
+
+def receives_other():
+    return (lax.axis_index("slab") % 2 == 0) & ~ends()
+
+
 def sending_side():
     grp = lax.axis_index("grp")
-    return jnp.where(swapped(), 1 - grp, grp)
-
-
-def has_beside():
-    slab, grp = lax.axis_index("slab"), lax.axis_index("grp")
-    return jnp.where(grp == 0, slab > 0, slab < lax.axis_size("slab") - 1)
+    return jnp.where(sends_other(), 1 - grp, grp)
+
+
+def receiving_side():
+    grp = lax.axis_index("grp")
+    return jnp.where(receives_other(), 1 - grp, grp)
+
+
+def has_beside(side):
+    slab = lax.axis_index("slab")
+    return jnp.where(side == 0, slab > 0, slab < lax.axis_size("slab") - 1)
 
 
 def across_pairs(slabs):
     last = slabs - 1
-    up_out = lambda s: 0 if s == 0 else 1
-    down_out = lambda s: 1 if s == last else 0
-    pairs = [(s * 2 + up_out(s), (s + 1) * 2) for s in range(last)]
-    pairs += [((s + 1) * 2 + down_out(s + 1), s * 2 + 1) for s in range(last)]
+    up_out = lambda s: 0 if s == 0 else s % 2
+    up_in = lambda s: 1 if s == 0 else s % 2
+    down_out = lambda s: 1 if s == last else 1 - s % 2
+    down_in = lambda s: 0 if s == last else 1 - s % 2
+    pairs = [(s * 2 + up_out(s), (s + 1) * 2 + down_in(s + 1)) for s in range(last)]
+    pairs += [((s + 1) * 2 + down_out(s + 1), s * 2 + up_in(s)) for s in range(last)]
     return pairs + [(1, 0), (last * 2, last * 2 + 1)]
 
 
@@ -115,17 +130,18 @@
         copy.wait()
 
 
-def home_kernel(size, weight, cell, event_cell, event_count, out, late):
+def home_kernel(size, weight, cell, event_cell, event_count, inlet, out, late):
     plane_shape = out.shape[1:]
     plane = sending_side()
     for c, moment in enumerate(plane_moments(plane, size, weight, cell, plane_shape)):
         out[c] = moment
     for k in range(SUBS):
         out[3 + k] = plane_counts(plane, event_cell, event_count, k, plane_shape)
-    grp = lax.axis_index("grp")
-    for k in range(SUBS):
-        late[k] = plane_counts(grp, event_cell, event_count, SUBS + k, plane_shape)
-        late[SUBS + k] = plane_counts(1 - grp, event_cell, event_count, SUBS + k, plane_shape)
+    later = receiving_side()
+    for k in range(SUBS):
+        out[3 + SUBS + k] = plane_counts(1 - later, event_cell, event_count, SUBS + k, plane_shape)
+        late[k] = plane_counts(later, event_cell, event_count, SUBS + k, plane_shape)
+    out[3 + 2 * SUBS] = inlet[0].astype(F32)
 
 
 def substep(field, zeroth, first, second, counts, grown):
@@ -138,17 +154,29 @@
     return field, first, second, grown + growth
 
 
-def first_kernel(field, home, away, late, out, state):
-    now = jnp.where(swapped(), away[3 + SUBS], field[0])
-    zeroth, first, second = (home[c] + away[c] for c in range(3))
-    grown = jnp.zeros_like(now)
-    for k in range(SUBS):
-        now, first, second, grown = substep(now, zeroth, first, second, home[3 + k] + away[3 + k], grown)
-    out[0] = now
-    for c, value in enumerate((now, zeroth, first, second, grown)):
-        state[c] = value
-    for k in range(SUBS):
-        state[5 + k] = late[SUBS + k]
+def first_substeps(field, one, other):
+    zeroth, first, second = (one[c] + other[c] for c in range(3))
+    grown = jnp.zeros_like(field)
+    for k in range(SUBS):
+        field, first, second, grown = substep(field, zeroth, first, second, one[3 + k] + other[3 + k], grown)
+    return field, zeroth, first, second, grown
+
+
+def front_kernel(field, home, away, out):
+    start = jnp.where(sends_other(), away[3 + SUBS], field[0])
+    out[0] = first_substeps(start, home, away)[0]
+
+
+def state_kernel(field, home, away, sent, partner_home, late, inlet, out):
+    other = sends_other()
+    near = first_substeps(jnp.where(other, away[3 + SUBS], field[0]), home, away)
+    far = first_substeps(jnp.where(other, field[0], away[3 + SUBS]), partner_home, sent)
+    for c in range(5):
+        out[c] = jnp.where(ends(), far[c], near[c])
+    out[5] = jnp.where(ends(), near[0], far[0])
+    for k in range(SUBS):
+        out[6 + k] = late[k] + partner_home[3 + SUBS + k]
+    out[6 + SUBS] = jnp.where(receives_other(), partner_home[3 + 2 * SUBS], inlet[0].astype(F32))
 
 
 def moved(field):
@@ -162,29 +190,21 @@
     return total
 
 
-def transport(field, beside, other, inlet):
-    around = jnp.where(has_beside(), beside, 0.0) + other + moved(field)
+def transport(field, beside, other, inlet, side):
+    around = jnp.where(has_beside(side), beside, 0.0) + other + moved(field)
     field = field + DIFFUSE * (around - 6.0 * field)
     return field + inlet * (INLET - field)
 
 
-def second_kernel(beside, mine, other, late, inlet, given, out):
+def second_kernel(beside, state, given, out):
     lines = beside.shape[1]
-    state = [jnp.where(swapped(), other[c], mine[c]) for c in range(5)]
-    partner_field = jnp.where(swapped(), mine[0], other[0])
-    now, zeroth, first, second, grown = state
-    now = transport(now, beside[0], partner_field, inlet[0].astype(F32))
-    for k in range(SUBS):
-        now, first, second, grown = substep(now, zeroth, first, second, late[k] + other[5 + k], grown)
+    now, zeroth, first, second, grown = (state[c] for c in range(5))
+    now = transport(now, beside[0], state[5], state[6 + SUBS], receiving_side())
+    for k in range(SUBS):
+        now, first, second, grown = substep(now, zeroth, first, second, state[6 + k], grown)
     out[pl.ds(0, lines)] = now
     out[pl.ds(lines, lines)] = grown
     out[pl.ds(2 * lines, given.shape[0])] = given[...]
-
-
-def third_kernel(planes, received, partner, inlet, out):
-    lines = out.shape[1]
-    here = pl.ds(0, lines)
-    out[0] = transport(planes[here], received[here], partner[here], inlet[0].astype(F32))
 
 
 def migrants_kernel(size, weight, cell, rows, count, keep, give, *, places):
@@ -228,17 +248,17 @@
 
 
 def both_planes(planes, partner, lines):
-    grp = lax.axis_index("grp")
     mine, other = planes[pl.ds(lines, lines)], partner[pl.ds(lines, lines)]
-    low = jnp.where(grp == 0, mine, other)
-    high = jnp.where(grp == 0, other, mine)
+    first = receiving_side() == 0
+    low = jnp.where(first, mine, other)
+    high = jnp.where(first, other, mine)
     return jnp.concatenate(pieces(jnp.concatenate([low, high], axis=0)), axis=0)
 
 
 def leaving_kernel(planes, partner, kept, out, *, lines, parts):
     stacked = both_planes(planes, partner, lines)
     here = pl.ds(0, lines)
-    out[here] = jnp.where(swapped(), partner[here], planes[here])
+    out[here] = jnp.where(ends(), partner[here], planes[here])
     grp = lax.axis_index("grp")
     taken = partner[pl.ds(2 * lines, kept.shape[0])]
     keeping = kept[...]
@@ -276,20 +296,26 @@
     out[...] = active[...] * (size[...] + grown)
 
 
-def arrivals_kernel(received, relayed, out, *, lines, parts):
+def last_kernel(planes, partner, received, relayed, inlet, field_out, arrivals_out, *, lines, parts):
     slab, grp = lax.axis_index("slab"), lax.axis_index("grp")
+    here = pl.ds(0, lines)
+    other = receives_other()
+    field = jnp.where(other, partner[here], planes[here])
+    beyond = jnp.where(other, planes[here], partner[here])
+    beside = jnp.where(other, relayed[here], received[here])
+    field_out[0] = transport(field, beside, beyond, inlet[0].astype(F32), grp)
     rows = 2 * parts
-    pick = lambda block: jnp.where(grp == 0, block[:rows], block[rows:])
-    mine = pick(received[pl.ds(lines, 2 * rows)])
-    other = pick(relayed[...])
-    lower = jnp.where(slab > 0, jnp.where(grp == 0, mine, other), 0.0)
-    upper = jnp.where(slab < lax.axis_size("slab") - 1, jnp.where(grp == 0, other, mine), 0.0)
+    pick = lambda block: jnp.where(grp == 0, block[lines : lines + rows], block[lines + rows : lines + 2 * rows])
+    mine, theirs = pick(received), pick(relayed)
+    from_lower = receiving_side() == 0
+    lower = jnp.where(slab > 0, jnp.where(from_lower, mine, theirs), 0.0)
+    upper = jnp.where(slab < lax.axis_size("slab") - 1, jnp.where(from_lower, theirs, mine), 0.0)
     places = mine.shape[1]
     for side, value in enumerate((lower, upper)):
         for v in range(2):
             for p in range(parts):
                 at = v * parts + p
-                out[0, side, v : v + 1, pl.ds(p * places, places)] = value[at : at + 1]
+                arrivals_out[0, side, v : v + 1, pl.ds(p * places, places)] = value[at : at + 1]
 
 
 VMEM = pl.BlockSpec(memory_space=pltpu.VMEM)
@@ -335,7 +361,7 @@
 
     inputs = [a.reshape(-1, LANES) for a in (crystal_size, crystal_weight, crystal_cell)]
     inputs += [nucleus_cell, nucleus_count, saturation, inlet_mask, migrant_rows]
-    away, size, weight, cell, event_cell, event_count, field, inlet, rows, active = call(
+    sent, size, weight, cell, event_cell, event_count, field, inlet, rows, active = call(
         away_kernel,
         [shape(4 + SUBS, lines, places)]
         + [jax.ShapeDtypeStruct(a.shape, a.dtype) for a in inputs]
@@ -346,24 +372,27 @@
         scratch=[pltpu.SemaphoreType.DMA((len(inputs),))],
         name="away",
     )
-    away = swap(away)
+    away = swap(sent)
     home, late = call(
         home_kernel,
-        (shape(3 + SUBS, lines, places), shape(2 * SUBS, lines, places)),
-        size, weight, cell, event_cell, event_count, cost=1 << 30, name="home",
-    )
-    front, mine = call(
-        first_kernel, (shape(1, lines, places), shape(5 + SUBS, lines, places)), field, home, away, late, name="first"
-    )
+        (shape(4 + 2 * SUBS, lines, places), shape(SUBS, lines, places)),
+        size, weight, cell, event_cell, event_count, inlet, cost=1 << 30, name="home",
+    )
+    front = call(front_kernel, shape(1, lines, places), field, home, away, name="front")
+    front, late_home = lax.optimization_barrier((front, home))
+    partner_home = swap(late_home)
     beside = across(front)
-    other = swap(mine)
+    state = call(
+        state_kernel, shape(7 + SUBS, lines, places), field, home, away, sent, partner_home, late, inlet,
+        cost=1 << 28, name="state",
+    )
     info = (shape(16, places), shape(16, places))
     kept, given = call(
         functools.partial(migrants_kernel, places=places), info, size, weight, cell, rows, migrant_count,
-        cost=1 << 30, name="migrants",
+        cost=1 << 33, name="migrants",
     )
     planes = call(
-        second_kernel, shape(2 * lines + 16, places), beside, mine, other, late, inlet, given, name="second"
+        second_kernel, shape(2 * lines + 16, places), beside, state, given, name="second"
     )
     partner = swap(planes)
     leaving = call(
@@ -375,10 +404,11 @@
         functools.partial(sizes_kernel, lines=lines), shape(*size.shape), planes, partner, size, cell, active,
         cost=1 << 31, name="sizes",
     )
-    relayed = swap(received[lines:])
-    field_out = call(third_kernel, shape(1, lines, places), planes, received, partner, inlet, cost=1 << 28, name="third")
-    arrivals = call(
-        functools.partial(arrivals_kernel, lines=lines, parts=parts), shape(1, 2, 2, slots), received, relayed, name="arrivals"
+    received, size_out = lax.optimization_barrier((received, size_out))
+    relayed = swap(received)
+    field_out, arrivals = call(
+        functools.partial(last_kernel, lines=lines, parts=parts),
+        (shape(1, lines, places), shape(1, 2, 2, slots)), planes, partner, received, relayed, inlet, name="last",
     )
     return (field_out, size_out.reshape(-1), arrivals)
 

time: 21.5 us -> 20.4 us (0.949)
  starting transfers between devices: 6.44 us -> 4.9 us
  waiting for transfers between devices: 5.09 us -> 5.85 us
  Pallas kernels: 8.34 us -> 8.08 us
    ppermute x4, starting transfers between devices: 4.35 us -> 0.82 us  [local(): swap = lambda value: lax.ppermute(value, 'grp', [(0, 1), (1, 0)])]
    ppermute x4, waiting for transfers between devices: 1.09 us -> 3.74 us  [local(): swap = lambda value: lax.ppermute(value, 'grp', [(0, 1), (1, 0)])]
    ppermute x2, starting transfers between devices: 2.09 us -> 4.09 us  [local(): across = lambda value: lax.ppermute(value, ('slab', 'grp'), pairs)]
    ppermute x2, waiting for transfers between devices: 4 us -> 2.11 us  [local(): across = lambda value: lax.ppermute(value, ('slab', 'grp'), pairs)]
    pallas_call x9, Pallas kernels: 8.34 us -> 8.08 us  [call(): pl.pallas_call(kernel, out_shape=out_shape, in_specs=specs or [VMEM] * le...]
  transfers between devices with their start and end apart: 6 -> 6, of which waited for: 4 -> 5; matrix products, arithmetic and copies ran while one was open for 0% -> 0% of each run, Pallas kernels for 22% -> 22%
where the time goes in v3:
time: 20.4 us; the launch traced here: 20.2 us
  Pallas kernels  8.08 us (40%)
  waiting for transfers between devices  5.85 us (29%)
  starting transfers between devices  4.9 us (24%)
  between operations  1.35 us (7%)
    pallas_call x9, Pallas kernels, call(): pl.pallas_call(kernel, out_shape=out_shape, in_specs=specs or [VMEM] * le...  8.08 us
    ppermute x2, starting transfers between devices, local(): across = lambda value: lax.ppermute(value, ('slab', 'grp'), pairs)  4.09 us
    ppermute x4, waiting for transfers between devices, local(): swap = lambda value: lax.ppermute(value, 'grp', [(0, 1), (1, 0)])  3.74 us
    ppermute x2, waiting for transfers between devices, local(): across = lambda value: lax.ppermute(value, ('slab', 'grp'), pairs)  2.11 us
    ppermute x4, starting transfers between devices, local(): swap = lambda value: lax.ppermute(value, 'grp', [(0, 1), (1, 0)])  0.82 us
  transfers between devices with their start and end apart: 6, of which 5 were waited for; matrix products, arithmetic and copies ran while one was open for 0% of the time, Pallas kernels for 22%

profile of v3, /device:TPU:9, one launch (start us, length us, event | category | flops | bytes accessed | tf_op | source)
XLA Modules:
  0.0 20.2 jit_solution(9027653109204589101)
XLA Ops:
  1.3 2.2 %away.1 = (f32[6,64,256]{2,1,0:T(8,128)S(1)}, f32[32,128]{1,0:T(8,128)S(1)}, f32[32,128]{1,0:T(8,128)S(1)}, s32[32,128]{1,0:T(8,128)S(1)}, s32[1,4,512]{2,1,0:T(...) custom-call(f32[32,128]{1,0:T(8,128)} %bitcast.4, ...), custom_call_target="tpu_custom_call" | custom-call | tf_op jit(solution)/shard_map/away/pallas_call | solution.py:331
  3.4 0.7 %collective-permute-start = (f32[6,64,256]{2,1,0:T(8,128)S(1)}, f32[6,64,256]{2,1,0:T(8,128)S(1)}, u32[]{:S(2)}, u32[]{:S(2)}) collective-permute-start(f32[6,64,256]{2,1,0:T(8,128)S(1)} %get-tuple-element.31.sent), channel_id=1, source_target_pairs={{0,1},{1,0},{2,3},{3,2},{4,5},{5,4},{6,7},{7,6},{8,9},{9,8},{10,11... | collective-permute-start | bytes 1179656 | tf_op jit(solution)/shard_map/ppermute | solution.py:358
  4.2 1.5 %home.1 = (f32[8,64,256]{2,1,0:T(8,128)S(1)}, f32[2,64,256]{2,1,0:T(8,128)S(1)}) custom-call(f32[32,128]{1,0:T(8,128)S(1)} %get-tuple-element.24.size, f32[32,128]{1,0:T(8,128)S(1)} %get-tuple-element.25.weight, s32[32,128]{1,0:T(8,128)S(1)} %get-tuple-element.26.cell, s32[1,4,512]{2,1,0:T(4,128)S(1)} %get-tuple-element.27.event_cell, ...), custom_call_target="tpu_custom_call" | custom-call | flops 1073741824 | tf_op jit(solution)/shard_map/home/pallas_call | solution.py:331
  5.7 0.0 collective-permute-done.away
  5.7 0.2 front.1
  5.9 0.0 copy-start
  5.9 2.1 %collective-permute-start.1 = (f32[1,64,256]{2,1,0:T(8,128)S(1)}, f32[1,64,256]{2,1,0:T(8,128)S(1)}, u32[]{:S(2)}, u32[]{:S(2)}) collective-permute-start(f32[1,64,256]{2,1,0:T(8,128)S(1)} %front.1), channel_id=1, source_target_pairs={{0,2},{3,5},{4,6},{7,9},{8,10},{11,13},{12,14},{15,17},{16,18},{19... | collective-permute-start | bytes 196616 | tf_op jit(solution)/shard_map/ppermute | solution.py:360
  8.0 0.0 collective-permute-start.2
  8.0 0.0 copy-done
  8.0 0.8 %migrants.1 = (f32[16,256]{1,0:T(8,128)S(1)}, f32[16,256]{1,0:T(8,128)S(1)}) custom-call(f32[32,128]{1,0:T(8,128)S(1)} %get-tuple-element.24.size, f32[32,128]{1,0:T(8,128)S(1)} %get-tuple-element.25.weight, s32[32,128]{1,0:T(8,128)S(1)} %get-tuple-element.26.cell, s32[1,2,512]{2,1,0:T(2,128)S(1)} %get-tuple-element.35.rows, s32[1,2]{1,0:T(1,128)S(1)} %copy-done), custom_call_target="tpu_custom_call" | custom-call | flops 8589934592 | tf_op jit(solution)/shard_map/migrants/pallas_call | solution.py:331
  8.8 1.1 %collective-permute-done.2.partner_home = f32[8,64,256]{2,1,0:T(8,128)S(1)} collective-permute-done((f32[8,64,256]{2,1,0:T(8,128)S(1)}, f32[8,64,256]{2,1,0:T(8,128)S(1)}, u32[]{:S(2)}, u32[]{:S(2)}) %collective-permute-start.2) | collective-permute-done | bytes 524320 | tf_op jit(solution)/shard_map/ppermute | solution.py:358
  9.9 0.4 %state.1 = f32[9,64,256]{2,1,0:T(8,128)S(1)} custom-call(f32[1,64,256]{2,1,0:T(8,128)S(1)} %get-tuple-element.23.field, f32[8,64,256]{2,1,0:T(8,128)S(1)} %get-tuple-element.33.home, f32[6,64,256]{2,1,0:T(8,128)S(1)} %collective-permute-done.away, f32[6,64,256]{2,1,0:T(8,128)S(1)} %get-tuple-element.31.sent, ...), custom_call_target="tpu_custom_call" | custom-call | flops 268435456 | tf_op jit(solution)/shard_map/state/pallas_call | solution.py:331
  10.3 0.7 %collective-permute-done.1.beside = f32[1,64,256]{2,1,0:T(8,128)S(1)} collective-permute-done((f32[1,64,256]{2,1,0:T(8,128)S(1)}, f32[1,64,256]{2,1,0:T(8,128)S(1)}, u32[]{:S(2)}, u32[]{:S(2)}) %collective-permute-start.1) | collective-permute-done | bytes 65568 | tf_op jit(solution)/shard_map/ppermute | solution.py:360
  10.9 0.3 %second.1.planes = f32[144,256]{1,0:T(8,128)S(1)} custom-call(f32[1,64,256]{2,1,0:T(8,128)S(1)} %collective-permute-done.1.beside, f32[9,64,256]{2,1,0:T(8,128)S(1)} %state.1, f32[16,256]{1,0:T(8,128)S(1)} %get-tuple-element.36.given), custom_call_target="tpu_custom_call" | custom-call | tf_op jit(solution)/shard_map/second/pallas_call | solution.py:331
  11.2 0.1 collective-permute-start.3
  11.3 1.4 %collective-permute-done.3.partner = f32[144,256]{1,0:T(8,128)S(1)} collective-permute-done((f32[144,256]{1,0:T(8,128)S(1)}, f32[144,256]{1,0:T(8,128)S(1)}, u32[]{:S(2)}, u32[]{:S(2)}) %collective-permute-start.3) | collective-permute-done | bytes 147488 | tf_op jit(solution)/shard_map/ppermute | solution.py:358
  12.7 0.3 %leaving.1 = f32[72,256]{1,0:T(8,128)S(1)} custom-call(f32[144,256]{1,0:T(8,128)S(1)} %second.1.planes, f32[144,256]{1,0:T(8,128)S(1)} %collective-permute-done.3.partner, f32[16,256]{1,0:T(8,128)S(1)} %get-tuple-element.37.kept), custom_call_target="tpu_custom_call" | custom-call | tf_op jit(solution)/shard_map/leaving/pallas_call | solution.py:331
  13.0 2.0 %collective-permute-start.4 = (f32[72,256]{1,0:T(8,128)S(1)}, f32[72,256]{1,0:T(8,128)S(1)}, u32[]{:S(2)}, u32[]{:S(2)}) collective-permute-start(f32[72,256]{1,0:T(8,128)S(1)} %leaving.1), channel_id=1, source_target_pairs={{0,2},{3,5},{4,6},{7,9},{8,10},{11,13},{12,14},{15,17},{16,18},{19... | collective-permute-start | bytes 221192 | tf_op jit(solution)/shard_map/ppermute | solution.py:360
  15.0 1.7 %sizes.1 = f32[32,128]{1,0:T(8,128)} custom-call(f32[144,256]{1,0:T(8,128)S(1)} %second.1.planes, f32[144,256]{1,0:T(8,128)S(1)} %collective-permute-done.3.partner, f32[32,128]{1,0:T(8,128)S(1)} %get-tuple-element.24.size, s32[32,128]{1,0:T(8,128)S(1)} %get-tuple-element.26.cell, f32[32,128]{1,0:T(8,128)S(1)} %get-tuple-element.38.active), custom_call_target="tpu_custom_call" | custom-call | flops 2147483648 | tf_op jit(solution)/shard_map/sizes/pallas_call | solution.py:331
  16.7 1.4 %collective-permute-done.4.received = f32[72,256]{1,0:T(8,128)S(1)} collective-permute-done((f32[72,256]{1,0:T(8,128)S(1)}, f32[72,256]{1,0:T(8,128)S(1)}, u32[]{:S(2)}, u32[]{:S(2)}) %collective-permute-start.4) | collective-permute-done | bytes 73760 | tf_op jit(solution)/shard_map/ppermute | solution.py:360
  18.1 0.0 collective-permute-start.5
  18.2 1.3 %collective-permute-done.5.relayed = f32[72,256]{1,0:T(8,128)S(1)} collective-permute-done((f32[72,256]{1,0:T(8,128)S(1)}, f32[72,256]{1,0:T(8,128)S(1)}, u32[]{:S(2)}, u32[]{:S(2)}) %collective-permute-start.5) | collective-permute-done | bytes 73760 | tf_op jit(solution)/shard_map/ppermute | solution.py:358
  19.4 0.8 %last.1 = (f32[1,64,256]{2,1,0:T(8,128)}, f32[1,2,2,512]{3,2,1,0:T(2,128)}) custom-call(f32[144,256]{1,0:T(8,128)S(1)} %second.1.planes, f32[144,256]{1,0:T(8,128)S(1)} %collective-permute-done.3.partner, f32[72,256]{1,0:T(8,128)S(1)} %collective-permute-done.4.received, f32[72,256]{1,0:T(8,128)S(1)} %collective-permute-done.5.relayed, ...), custom_call_target="tpu_custom_call" | custom-call | tf_op jit(solution)/shard_map/last/pallas_call | solution.py:331
Async XLA Ops:
  3.4 2.2 %collective-permute-start = (f32[6,64,256]{2,1,0:T(8,128)S(1)}, f32[6,64,256]{2,1,0:T(8,128)S(1)}, u32[]{:S(2)}, u32[]{:S(2)}) collective-permute-start(f32[6,64,256]{2,1,0:T(8,128)S(1)} %get-tuple-element.31.sent), channel_id=1, source_target_pairs={{0,1},{1,0},{2,3},{3,2},{4,5},{5,4},{6,7},{7,6},{8,9},{9,8},{10,11... | collective-permute-start | bytes 1179656 | tf_op jit(solution)/shard_map/ppermute | solution.py:358
  5.9 2.1 %copy-start = (s32[1,2]{1,0:T(1,128)S(1)}, s32[1,2]{1,0:T(1,128)}, u32[]{:S(2)}) copy-start(s32[1,2]{1,0:T(1,128)} %count.1) | copy-start | bytes 28
  5.9 5.1 %collective-permute-start.1 = (f32[1,64,256]{2,1,0:T(8,128)S(1)}, f32[1,64,256]{2,1,0:T(8,128)S(1)}, u32[]{:S(2)}, u32[]{:S(2)}) collective-permute-start(f32[1,64,256]{2,1,0:T(8,128)S(1)} %front.1), channel_id=1, source_target_pairs={{0,2},{3,5},{4,6},{7,9},{8,10},{11,13},{12,14},{15,17},{16,18},{19... | collective-permute-start | bytes 196616 | tf_op jit(solution)/shard_map/ppermute | solution.py:360
  8.0 1.9 %collective-permute-start.2 = (f32[8,64,256]{2,1,0:T(8,128)S(1)}, f32[8,64,256]{2,1,0:T(8,128)S(1)}, u32[]{:S(2)}, u32[]{:S(2)}) collective-permute-start(f32[8,64,256]{2,1,0:T(8,128)S(1)} %get-tuple-element.33.home), channel_id=1, source_target_pairs={{0,1},{1,0},{2,3},{3,2},{4,5},{5,4},{6,7},{7,6},{8,9},{9,8},{10,11... | collective-permute-start | bytes 1572872 | tf_op jit(solution)/shard_map/ppermute | solution.py:358
  11.2 1.4 %collective-permute-start.3 = (f32[144,256]{1,0:T(8,128)S(1)}, f32[144,256]{1,0:T(8,128)S(1)}, u32[]{:S(2)}, u32[]{:S(2)}) collective-permute-start(f32[144,256]{1,0:T(8,128)S(1)} %second.1.planes), channel_id=1, source_target_pairs={{0,1},{1,0},{2,3},{3,2},{4,5},{5,4},{6,7},{7,6},{8,9},{9,8},{10,11... | collective-permute-start | bytes 442376 | tf_op jit(solution)/shard_map/ppermute | solution.py:358
  13.0 5.2 %collective-permute-start.4 = (f32[72,256]{1,0:T(8,128)S(1)}, f32[72,256]{1,0:T(8,128)S(1)}, u32[]{:S(2)}, u32[]{:S(2)}) collective-permute-start(f32[72,256]{1,0:T(8,128)S(1)} %leaving.1), channel_id=1, source_target_pairs={{0,2},{3,5},{4,6},{7,9},{8,10},{11,13},{12,14},{15,17},{16,18},{19... | collective-permute-start | bytes 221192 | tf_op jit(solution)/shard_map/ppermute | solution.py:360
  18.1 1.3 %collective-permute-start.5 = (f32[72,256]{1,0:T(8,128)S(1)}, f32[72,256]{1,0:T(8,128)S(1)}, u32[]{:S(2)}, u32[]{:S(2)}) collective-permute-start(f32[72,256]{1,0:T(8,128)S(1)} %collective-permute-done.4.received), channel_id=1, source_target_pairs={{0,1},{1,0},{2,3},{3,2},{4,5},{5,4},{6,7},{7,6},{8,9},{9,8},{10,11... | collective-permute-start | bytes 221192 | tf_op jit(solution)/shard_map/ppermute | solution.py:358

commit v4 on v3

--- a/solution.py
+++ b/solution.py
@@ -80,14 +80,12 @@
     return pairs + [(1, 0), (last * 2, last * 2 + 1)]
 
 
-def plane_moments(plane, size, weight, cell, plane_shape):
+def plane_moments(plane, sizes, weights, cells, plane_shape):
     lines, places = plane_shape
-    sizes = size[...]
-    zeroth = weight[...]
-    first = zeroth * sizes
-    parts = [part.astype(F32) for moment in (zeroth, first, first * sizes) for part in pieces(moment)]
-    line = cell[...] // places - plane * lines
-    place = cell[...] % places
+    first = weights * sizes
+    parts = [part.astype(F32) for moment in (weights, first, first * sizes) for part in pieces(moment)]
+    line = cells // places - plane * lines
+    place = cells % places
     group = 4
     sums = jnp.zeros((len(parts) * lines, places), F32)
     for start in range(0, sizes.shape[0], group):
@@ -101,47 +99,62 @@
     return [sums[2 * c * lines : (2 * c + 1) * lines] + sums[(2 * c + 1) * lines : (2 * c + 2) * lines] for c in range(3)]
 
 
-def plane_counts(plane, event_cell, event_count, k, plane_shape):
+def plane_counts(plane, cells, counts, plane_shape):
     lines, places = plane_shape
-    cells = event_cell[0, pl.ds(k, 1), :]
-    counts = event_count[0, pl.ds(k, 1), :].astype(F32).astype(BF16)
-    left = hot(lines, cells // places - plane * lines) * counts
+    left = hot(lines, cells // places - plane * lines) * counts.astype(BF16)
     return lax.dot_general(left, hot(places, cells % places), NT, preferred_element_type=F32)
 
 
-def away_kernel(*refs):
+def own_events(event_cell, event_count, k):
+    row = pl.ds(k, 1)
+    return event_cell[0, row, :], event_count[0, row, :].astype(F32)
+
+
+def sections(parcel_rows, event_rows, field_rows):
+    sizes = [parcel_rows] * 3 + [event_rows] * 2 + [field_rows] * 2
+    starts = [sum(sizes[:i]) for i in range(len(sizes) + 1)]
+    return [pl.ds(start, size) for start, size in zip(starts, sizes)], starts[-1]
+
+
+def packed_events(packed, spans, k, width):
+    per = width // LANES
+    rows = [packed[pl.ds(span.start + k * per + j, 1)] for span in spans for j in range(per)]
+    cells, counts = jnp.concatenate(rows[:per], axis=1), jnp.concatenate(rows[per:], axis=1)
+    return cells.astype(jnp.int32), counts
+
+
+def load_kernel(*refs):
     inputs, live, out, kept, active, sems = refs[:8], refs[8], refs[9], refs[10:18], *refs[18:]
     copies = [pltpu.make_async_copy(src, dst, sems.at[i]) for i, (src, dst) in enumerate(zip(inputs, kept))]
     for copy in copies:
         copy.start()
-    for copy in copies[:6]:
+    for copy in copies:
         copy.wait()
     size, weight, cell, event_cell, event_count, field = kept[:6]
     active[...] = jnp.where(row_numbers(size.shape) < live[0], 1.0, 0.0)
     weight[...] = weight[...] * active[...]
+    events, width = event_cell.shape[1:]
+    per = width // LANES
+    spans, _ = sections(size.shape[0], events * per, field.shape[1])
+    out[spans[0]] = size[...]
+    out[spans[1]] = weight[...]
+    out[spans[2]] = cell[...].astype(F32)
+    for span, array in ((spans[3], event_cell), (spans[4], event_count)):
+        values = array[0].astype(F32)
+        for k in range(events):
+            for j in range(per):
+                out[pl.ds(span.start + k * per + j, 1)] = values[k : k + 1, j * LANES : (j + 1) * LANES]
+    for j in range(2):
+        out[spans[5 + j]] = field[0, :, pl.ds(j * LANES, LANES)]
+
+
+def home_kernel(size, weight, cell, event_cell, event_count, out):
     plane_shape = out.shape[1:]
-    plane = 1 - sending_side()
-    for c, moment in enumerate(plane_moments(plane, size, weight, cell, plane_shape)):
+    plane = sending_side()
+    for c, moment in enumerate(plane_moments(plane, size[...], weight[...], cell[...], plane_shape)):
         out[c] = moment
     for k in range(SUBS):
-        out[3 + k] = plane_counts(plane, event_cell, event_count, k, plane_shape)
-    out[3 + SUBS] = field[0]
-    for copy in copies[6:]:
-        copy.wait()
-
-
-def home_kernel(size, weight, cell, event_cell, event_count, inlet, out, late):
-    plane_shape = out.shape[1:]
-    plane = sending_side()
-    for c, moment in enumerate(plane_moments(plane, size, weight, cell, plane_shape)):
-        out[c] = moment
-    for k in range(SUBS):
-        out[3 + k] = plane_counts(plane, event_cell, event_count, k, plane_shape)
-    later = receiving_side()
-    for k in range(SUBS):
-        out[3 + SUBS + k] = plane_counts(1 - later, event_cell, event_count, SUBS + k, plane_shape)
-        late[k] = plane_counts(later, event_cell, event_count, SUBS + k, plane_shape)
-    out[3 + 2 * SUBS] = inlet[0].astype(F32)
+        out[3 + k] = plane_counts(plane, *own_events(event_cell, event_count, k), plane_shape)
 
 
 def substep(field, zeroth, first, second, counts, grown):
@@ -154,29 +167,35 @@
     return field, first, second, grown + growth
 
 
-def first_substeps(field, one, other):
-    zeroth, first, second = (one[c] + other[c] for c in range(3))
-    grown = jnp.zeros_like(field)
+def front_kernel(field, home, packed, out, state, *, parcel_rows, events):
+    plane_shape = out.shape[1:]
+    plane = sending_side()
+    spans, _ = sections(parcel_rows, events[0] * events[1] // LANES, plane_shape[0])
+    cells = packed[spans[2]].astype(jnp.int32)
+    zeroth, first, second = plane_moments(plane, packed[spans[0]], packed[spans[1]], cells, plane_shape)
+    zeroth, first, second = zeroth + home[0], first + home[1], second + home[2]
+    theirs = jnp.concatenate([packed[spans[5]], packed[spans[6]]], axis=1)
+    now = jnp.where(sends_other(), theirs, field[0])
+    grown = jnp.zeros_like(now)
     for k in range(SUBS):
-        field, first, second, grown = substep(field, zeroth, first, second, one[3 + k] + other[3 + k], grown)
-    return field, zeroth, first, second, grown
-
-
-def front_kernel(field, home, away, out):
-    start = jnp.where(sends_other(), away[3 + SUBS], field[0])
-    out[0] = first_substeps(start, home, away)[0]
-
-
-def state_kernel(field, home, away, sent, partner_home, late, inlet, out):
-    other = sends_other()
-    near = first_substeps(jnp.where(other, away[3 + SUBS], field[0]), home, away)
-    far = first_substeps(jnp.where(other, field[0], away[3 + SUBS]), partner_home, sent)
+        counts = home[3 + k] + plane_counts(plane, *packed_events(packed, spans[3:5], k, events[1]), plane_shape)
+        now, first, second, grown = substep(now, zeroth, first, second, counts, grown)
+    out[0] = now
+    for c, value in enumerate((now, zeroth, first, second, grown)):
+        state[c] = value
+
+
+def late_kernel(state, packed, event_cell, event_count, inlet, out, late, *, parcel_rows):
+    plane_shape = out.shape[1:]
+    events, width = event_cell.shape[1:]
+    spans, _ = sections(parcel_rows, events * width // LANES, plane_shape[0])
+    plane = receiving_side()
     for c in range(5):
-        out[c] = jnp.where(ends(), far[c], near[c])
-    out[5] = jnp.where(ends(), near[0], far[0])
+        out[c] = state[c]
+    out[5] = inlet[0].astype(F32)
     for k in range(SUBS):
-        out[6 + k] = late[k] + partner_home[3 + SUBS + k]
-    out[6 + SUBS] = jnp.where(receives_other(), partner_home[3 + 2 * SUBS], inlet[0].astype(F32))
+        mine = plane_counts(plane, *own_events(event_cell, event_count, SUBS + k), plane_shape)
+        late[k] = mine + plane_counts(plane, *packed_events(packed, spans[3:5], SUBS + k, width), plane_shape)
 
 
 def moved(field):
@@ -196,12 +215,14 @@
     return field + inlet * (INLET - field)
 
 
-def second_kernel(beside, state, given, out):
+def second_kernel(beside, mine, other, late, given, out):
     lines = beside.shape[1]
-    now, zeroth, first, second, grown = (state[c] for c in range(5))
-    now = transport(now, beside[0], state[5], state[6 + SUBS], receiving_side())
+    now, zeroth, first, second, grown = (jnp.where(ends(), other[c], mine[c]) for c in range(5))
+    partner_field = jnp.where(ends(), mine[0], other[0])
+    inlet = jnp.where(receives_other(), other[5], mine[5])
+    now = transport(now, beside[0], partner_field, inlet, receiving_side())
     for k in range(SUBS):
-        now, first, second, grown = substep(now, zeroth, first, second, state[6 + k], grown)
+        now, first, second, grown = substep(now, zeroth, first, second, late[k], grown)
     out[pl.ds(0, lines)] = now
     out[pl.ds(lines, lines)] = grown
     out[pl.ds(2 * lines, given.shape[0])] = given[...]
@@ -262,18 +283,19 @@
     grp = lax.axis_index("grp")
     taken = partner[pl.ds(2 * lines, kept.shape[0])]
     keeping = kept[...]
-    at = lines
-    for one, other in ((keeping, taken), (taken, keeping)):
-        part = jnp.where(grp == 0, one, other)
-        rows = [part[i : i + 1] for i in range(5 * parts)]
-        line = jnp.concatenate(rows[2 * parts : 3 * parts], axis=1).astype(jnp.int32)
-        place = jnp.concatenate(rows[3 * parts : 4 * parts], axis=1).astype(jnp.int32)
-        grown = grown_at(stacked, line, place)
-        places = part.shape[1]
+    blocks = [jnp.where(grp == 0, one, other) for one, other in ((keeping, taken), (taken, keeping))]
+    pick = lambda c: [block[i : i + 1] for block in blocks for i in range(c * parts, (c + 1) * parts)]
+    sizes, weights, valid = pick(0), pick(1), pick(4)
+    line = jnp.concatenate(pick(2), axis=1).astype(jnp.int32)
+    place = jnp.concatenate(pick(3), axis=1).astype(jnp.int32)
+    grown = grown_at(stacked, line, place)
+    places = planes.shape[1]
+    for j in range(2):
+        at = lines + 2 * parts * j
         for p in range(parts):
-            out[at + p : at + p + 1] = rows[p] + grown[:, p * places : (p + 1) * places] * rows[4 * parts + p]
-            out[at + parts + p : at + parts + p + 1] = rows[parts + p]
-        at += 2 * parts
+            i = j * parts + p
+            out[at + p : at + p + 1] = sizes[i] + grown[:, i * places : (i + 1) * places] * valid[i]
+            out[at + parts + p : at + parts + p + 1] = weights[i]
 
 
 def sizes_kernel(planes, partner, size, cell, active, out, *, lines):
@@ -296,14 +318,22 @@
     out[...] = active[...] * (size[...] + grown)
 
 
-def last_kernel(planes, partner, received, relayed, inlet, field_out, arrivals_out, *, lines, parts):
-    slab, grp = lax.axis_index("slab"), lax.axis_index("grp")
+def rest_kernel(planes, partner, inlet, out):
+    lines = inlet.shape[1]
     here = pl.ds(0, lines)
     other = receives_other()
     field = jnp.where(other, partner[here], planes[here])
     beyond = jnp.where(other, planes[here], partner[here])
-    beside = jnp.where(other, relayed[here], received[here])
-    field_out[0] = transport(field, beside, beyond, inlet[0].astype(F32), grp)
+    keep = 1.0 - inlet[0].astype(F32)
+    field = field + DIFFUSE * (beyond + moved(field) - 6.0 * field)
+    out[0] = keep * field + (1.0 - keep) * INLET
+    out[1] = jnp.where(has_beside(lax.axis_index("grp")), DIFFUSE * keep, 0.0)
+
+
+def last_kernel(rest, received, relayed, field_out, arrivals_out, *, lines, parts):
+    slab, grp = lax.axis_index("slab"), lax.axis_index("grp")
+    here = pl.ds(0, lines)
+    field_out[0] = rest[0] + rest[1] * jnp.where(receives_other(), relayed[here], received[here])
     rows = 2 * parts
     pick = lambda block: jnp.where(grp == 0, block[lines : lines + rows], block[lines + rows : lines + 2 * rows])
     mine, theirs = pick(received), pick(relayed)
@@ -359,40 +389,44 @@
     pairs = across_pairs(lax.axis_size("slab"))
     across = lambda value: lax.ppermute(value, ("slab", "grp"), pairs)
 
+    hbm = lambda a: pltpu.with_memory_space_constraint(a, pltpu.HBM)
+    like = lambda a: jax.ShapeDtypeStruct(a.shape, a.dtype)
     inputs = [a.reshape(-1, LANES) for a in (crystal_size, crystal_weight, crystal_cell)]
     inputs += [nucleus_cell, nucleus_count, saturation, inlet_mask, migrant_rows]
-    sent, size, weight, cell, event_cell, event_count, field, inlet, rows, active = call(
-        away_kernel,
-        [shape(4 + SUBS, lines, places)]
-        + [jax.ShapeDtypeStruct(a.shape, a.dtype) for a in inputs]
-        + [shape(*inputs[0].shape)],
-        *[pltpu.with_memory_space_constraint(a, pltpu.HBM) for a in inputs],
+    parcel_rows, events = inputs[0].shape[0], nucleus_cell.shape[1:]
+    _, packed_rows = sections(parcel_rows, events[0] * events[1] // LANES, lines)
+    packed, size, weight, cell, event_cell, event_count, field, inlet, rows, active = call(
+        load_kernel,
+        [shape(packed_rows, LANES)] + [like(a) for a in inputs] + [shape(*inputs[0].shape)],
+        *[hbm(a) for a in inputs],
         live_count,
         specs=[HBM] * 8 + [SMEM],
         scratch=[pltpu.SemaphoreType.DMA((len(inputs),))],
-        name="away",
-    )
-    away = swap(sent)
-    home, late = call(
-        home_kernel,
-        (shape(4 + 2 * SUBS, lines, places), shape(SUBS, lines, places)),
-        size, weight, cell, event_cell, event_count, inlet, cost=1 << 30, name="home",
-    )
-    front = call(front_kernel, shape(1, lines, places), field, home, away, name="front")
-    front, late_home = lax.optimization_barrier((front, home))
-    partner_home = swap(late_home)
+        name="load",
+    )
+    packed = swap(packed)
+    home = call(
+        home_kernel, shape(3 + SUBS, lines, places), size, weight, cell, event_cell, event_count,
+        cost=1 << 30, name="home",
+    )
+    front, state = call(
+        functools.partial(front_kernel, parcel_rows=parcel_rows, events=events),
+        (shape(1, lines, places), shape(5, lines, places)), field, home, packed, name="front",
+    )
     beside = across(front)
-    state = call(
-        state_kernel, shape(7 + SUBS, lines, places), field, home, away, sent, partner_home, late, inlet,
-        cost=1 << 28, name="state",
-    )
+    _, state = lax.optimization_barrier((front, state))
+    mine, late = call(
+        functools.partial(late_kernel, parcel_rows=parcel_rows), (shape(6, lines, places), shape(SUBS, lines, places)),
+        state, packed, event_cell, event_count, inlet, cost=1 << 28, name="late",
+    )
+    other = swap(mine)
     info = (shape(16, places), shape(16, places))
     kept, given = call(
         functools.partial(migrants_kernel, places=places), info, size, weight, cell, rows, migrant_count,
         cost=1 << 33, name="migrants",
     )
     planes = call(
-        second_kernel, shape(2 * lines + 16, places), beside, state, given, name="second"
+        second_kernel, shape(2 * lines + 16, places), beside, mine, other, late, given, name="second"
     )
     partner = swap(planes)
     leaving = call(
@@ -406,9 +440,10 @@
     )
     received, size_out = lax.optimization_barrier((received, size_out))
     relayed = swap(received)
+    rest = call(rest_kernel, shape(2, lines, places), planes, partner, inlet, cost=1 << 28, name="rest")
     field_out, arrivals = call(
         functools.partial(last_kernel, lines=lines, parts=parts),
-        (shape(1, lines, places), shape(1, 2, 2, slots)), planes, partner, received, relayed, inlet, name="last",
+        (shape(1, lines, places), shape(1, 2, 2, slots)), rest, received, relayed, name="last",
     )
     return (field_out, size_out.reshape(-1), arrivals)
 

time: 20.4 us -> 20 us (0.980)
  waiting for transfers between devices: 5.85 us -> 4.91 us
  local copies, waits for them, and re-layouts: 0.01 us -> 0.57 us
  Pallas kernels: 8.08 us -> 7.86 us
    ppermute x4, waiting for transfers between devices: 3.74 us -> 2.44 us  [local(): swap = lambda value: lax.ppermute(value, 'grp', [(0, 1), (1, 0)])]
    unnamed x2, local copies, waits for them, and re-layouts: 0.01 us -> 0.57 us
    ppermute x2, waiting for transfers between devices: 2.11 us -> 2.47 us  [local(): across = lambda value: lax.ppermute(value, ('slab', 'grp'), pairs)]
    pallas_call x9 -> x10, Pallas kernels: 8.08 us -> 7.86 us  [call(): pl.pallas_call(kernel, out_shape=out_shape, in_specs=specs or [VMEM] * le...]
  transfers between devices with their start and end apart: 6 -> 6, of which waited for: 5 -> 4; matrix products, arithmetic and copies ran while one was open for 0% -> 0% of each run, Pallas kernels for 22% -> 22%
where the time goes in v4:
time: 20 us; the launch traced here: 19.7 us
  Pallas kernels  7.86 us (39%)
  starting transfers between devices  5.02 us (25%)
  waiting for transfers between devices  4.91 us (25%)
  between operations  1.37 us (7%)
  local copies, waits for them, and re-layouts  0.57 us (3%)
    pallas_call x10, Pallas kernels, call(): pl.pallas_call(kernel, out_shape=out_shape, in_specs=specs or [VMEM] * le...  7.86 us
    ppermute x2, starting transfers between devices, local(): across = lambda value: lax.ppermute(value, ('slab', 'grp'), pairs)  4.08 us
    ppermute x2, waiting for transfers between devices, local(): across = lambda value: lax.ppermute(value, ('slab', 'grp'), pairs)  2.47 us
    ppermute x4, waiting for transfers between devices, local(): swap = lambda value: lax.ppermute(value, 'grp', [(0, 1), (1, 0)])  2.44 us
    ppermute x4, starting transfers between devices, local(): swap = lambda value: lax.ppermute(value, 'grp', [(0, 1), (1, 0)])  0.93 us
    unnamed x2, local copies, waits for them, and re-layouts  0.57 us
  transfers between devices with their start and end apart: 6, of which 4 were waited for; matrix products, arithmetic and copies ran while one was open for 0% of the time, Pallas kernels for 22%

profile of v4, /device:TPU:9, one launch (start us, length us, event | category | flops | bytes accessed | tf_op | source)
XLA Modules:
  0.0 19.7 jit_solution(4648593276373126580)
XLA Ops:
  1.3 1.1 %load.1 = (f32[256,128]{1,0:T(8,128)S(1)}, f32[32,128]{1,0:T(8,128)S(1)}, f32[32,128]{1,0:T(8,128)S(1)}, s32[32,128]{1,0:T(8,128)S(1)}, s32[1,4,512]{2,1,0:T(4,1...) custom-call(f32[32,128]{1,0:T(8,128)} %bitcast.4, ...), custom_call_target="tpu_custom_call" | custom-call | tf_op jit(solution)/shard_map/load/pallas_call | solution.py:361
  2.3 0.7 %collective-permute-start = (f32[256,128]{1,0:T(8,128)S(1)}, f32[256,128]{1,0:T(8,128)S(1)}, u32[]{:S(2)}, u32[]{:S(2)}) collective-permute-start(f32[256,128]{1,0:T(8,128)S(1)} %get-tuple-element.30), channel_id=1, source_target_pairs={{0,1},{1,0},{2,3},{3,2},{4,5},{5,4},{6,7},{7,6},{8,9},{9,8},{10,11... | collective-permute-start | bytes 393224 | tf_op jit(solution)/shard_map/ppermute | solution.py:388
  3.1 1.1 %home.1 = f32[5,64,256]{2,1,0:T(8,128)S(1)} custom-call(f32[32,128]{1,0:T(8,128)S(1)} %get-tuple-element.25.size, f32[32,128]{1,0:T(8,128)S(1)} %get-tuple-element.26.weight, s32[32,128]{1,0:T(8,128)S(1)} %get-tuple-element.27.cell, s32[1,4,512]{2,1,0:T(4,128)S(1)} %get-tuple-element.28.event_cell, s32[1,4,512]{2,1,0:T(4,128)S(1)} %get-tuple-element.29.event_count), custom_call_target="tpu_custom_call" | custom-call | flops 1073741824 | tf_op jit(solution)/shard_map/home/pallas_call | solution.py:361
  4.2 0.0 collective-permute-done.packed
  4.2 1.3 %front.1 = (f32[1,64,256]{2,1,0:T(8,128)S(1)}, f32[5,64,256]{2,1,0:T(8,128)S(1)}) custom-call(f32[1,64,256]{2,1,0:T(8,128)S(1)} %get-tuple-element.24.field, f32[5,64,256]{2,1,0:T(8,128)S(1)} %home.1, f32[256,128]{1,0:T(8,128)S(1)} %collective-permute-done.packed), custom_call_target="tpu_custom_call" | custom-call | tf_op jit(solution)/shard_map/front/pallas_call | solution.py:361
  5.5 2.1 %collective-permute-start.1 = (f32[1,64,256]{2,1,0:T(8,128)S(1)}, f32[1,64,256]{2,1,0:T(8,128)S(1)}, u32[]{:S(2)}, u32[]{:S(2)}) collective-permute-start(f32[1,64,256]{2,1,0:T(8,128)S(1)} %get-tuple-element.31), channel_id=1, source_target_pairs={{0,2},{3,5},{4,6},{7,9},{8,10},{11,13},{12,14},{15,17},{16,18},{19... | collective-permute-start | bytes 196616 | tf_op jit(solution)/shard_map/ppermute | solution.py:390
  7.6 0.5 %late.1 = (f32[6,64,256]{2,1,0:T(8,128)S(1)}, f32[2,64,256]{2,1,0:T(8,128)S(1)}) custom-call(f32[5,64,256]{2,1,0:T(8,128)S(1)} %get-tuple-element.32.state, f32[256,128]{1,0:T(8,128)S(1)} %collective-permute-done.packed, s32[1,4,512]{2,1,0:T(4,128)S(1)} %get-tuple-element.28.event_cell, s32[1,4,512]{2,1,0:T(4,128)S(1)} %get-tuple-element.29.event_count, ...), custom_call_target="tpu_custom_call" | custom-call | flops 268435456 | tf_op jit(solution)/shard_map/late/pallas_call | solution.py:361
  8.1 0.0 copy-start
  8.1 0.1 collective-permute-start.2
  8.2 0.6 %copy-done = s32[1,2]{1,0:T(1,128)S(1)} copy-done((s32[1,2]{1,0:T(1,128)S(1)}, s32[1,2]{1,0:T(1,128)}, u32[]{:S(2)}) %copy-start) | copy-done | bytes 32
  8.8 0.8 %migrants.1 = (f32[16,256]{1,0:T(8,128)S(1)}, f32[16,256]{1,0:T(8,128)S(1)}) custom-call(f32[32,128]{1,0:T(8,128)S(1)} %get-tuple-element.25.size, f32[32,128]{1,0:T(8,128)S(1)} %get-tuple-element.26.weight, s32[32,128]{1,0:T(8,128)S(1)} %get-tuple-element.27.cell, s32[1,2,512]{2,1,0:T(2,128)S(1)} %get-tuple-element.36.rows, s32[1,2]{1,0:T(1,128)S(1)} %copy-done), custom_call_target="tpu_custom_call" | custom-call | flops 8589934592 | tf_op jit(solution)/shard_map/migrants/pallas_call | solution.py:361
  9.5 1.0 %collective-permute-done.1.beside = f32[1,64,256]{2,1,0:T(8,128)S(1)} collective-permute-done((f32[1,64,256]{2,1,0:T(8,128)S(1)}, f32[1,64,256]{2,1,0:T(8,128)S(1)}, u32[]{:S(2)}, u32[]{:S(2)}) %collective-permute-start.1) | collective-permute-done | bytes 65568 | tf_op jit(solution)/shard_map/ppermute | solution.py:390
  10.6 0.0 collective-permute-done.2.other
  10.6 0.3 %second.1.planes = f32[144,256]{1,0:T(8,128)S(1)} custom-call(f32[1,64,256]{2,1,0:T(8,128)S(1)} %collective-permute-done.1.beside, f32[6,64,256]{2,1,0:T(8,128)S(1)} %get-tuple-element.34.mine, f32[6,64,256]{2,1,0:T(8,128)S(1)} %collective-permute-done.2.other, f32[2,64,256]{2,1,0:T(8,128)S(1)} %get-tuple-element.35.late, f32[16,256]{1,0:T(8,128)S(1)} %get-tuple-element.37.given), custom_call_target="tpu_custom_call" | custom-call | tf_op jit(solution)/shard_map/second/pallas_call | solution.py:361
  10.9 0.1 collective-permute-start.3
  11.0 1.4 %collective-permute-done.3.partner = f32[144,256]{1,0:T(8,128)S(1)} collective-permute-done((f32[144,256]{1,0:T(8,128)S(1)}, f32[144,256]{1,0:T(8,128)S(1)}, u32[]{:S(2)}, u32[]{:S(2)}) %collective-permute-start.3) | collective-permute-done | bytes 147488 | tf_op jit(solution)/shard_map/ppermute | solution.py:388
  12.3 0.3 %leaving.1 = f32[72,256]{1,0:T(8,128)S(1)} custom-call(f32[144,256]{1,0:T(8,128)S(1)} %second.1.planes, f32[144,256]{1,0:T(8,128)S(1)} %collective-permute-done.3.partner, f32[16,256]{1,0:T(8,128)S(1)} %get-tuple-element.38.kept), custom_call_target="tpu_custom_call" | custom-call | tf_op jit(solution)/shard_map/leaving/pallas_call | solution.py:361
  12.7 2.0 %collective-permute-start.4 = (f32[72,256]{1,0:T(8,128)S(1)}, f32[72,256]{1,0:T(8,128)S(1)}, u32[]{:S(2)}, u32[]{:S(2)}) collective-permute-start(f32[72,256]{1,0:T(8,128)S(1)} %leaving.1), channel_id=1, source_target_pairs={{0,2},{3,5},{4,6},{7,9},{8,10},{11,13},{12,14},{15,17},{16,18},{19... | collective-permute-start | bytes 221192 | tf_op jit(solution)/shard_map/ppermute | solution.py:390
  14.6 1.7 %sizes.1 = f32[32,128]{1,0:T(8,128)} custom-call(f32[144,256]{1,0:T(8,128)S(1)} %second.1.planes, f32[144,256]{1,0:T(8,128)S(1)} %collective-permute-done.3.partner, f32[32,128]{1,0:T(8,128)S(1)} %get-tuple-element.25.size, s32[32,128]{1,0:T(8,128)S(1)} %get-tuple-element.27.cell, f32[32,128]{1,0:T(8,128)S(1)} %get-tuple-element.39.active), custom_call_target="tpu_custom_call" | custom-call | flops 2147483648 | tf_op jit(solution)/shard_map/sizes/pallas_call | solution.py:361
  16.4 1.4 %collective-permute-done.4.received = f32[72,256]{1,0:T(8,128)S(1)} collective-permute-done((f32[72,256]{1,0:T(8,128)S(1)}, f32[72,256]{1,0:T(8,128)S(1)}, u32[]{:S(2)}, u32[]{:S(2)}) %collective-permute-start.4) | collective-permute-done | bytes 73760 | tf_op jit(solution)/shard_map/ppermute | solution.py:390
  17.8 0.1 collective-permute-start.5
  17.9 0.1 rest.1
  18.0 1.1 %collective-permute-done.5.relayed = f32[72,256]{1,0:T(8,128)S(1)} collective-permute-done((f32[72,256]{1,0:T(8,128)S(1)}, f32[72,256]{1,0:T(8,128)S(1)}, u32[]{:S(2)}, u32[]{:S(2)}) %collective-permute-start.5) | collective-permute-done | bytes 73760 | tf_op jit(solution)/shard_map/ppermute | solution.py:388
  19.1 0.6 %last.1 = (f32[1,64,256]{2,1,0:T(8,128)}, f32[1,2,2,512]{3,2,1,0:T(2,128)}) custom-call(f32[2,64,256]{2,1,0:T(8,128)S(1)} %rest.1, f32[72,256]{1,0:T(8,128)S(1)} %collective-permute-done.4.received, f32[72,256]{1,0:T(8,128)S(1)} %collective-permute-done.5.relayed), custom_call_target="tpu_custom_call" | custom-call | tf_op jit(solution)/shard_map/last/pallas_call | solution.py:361
Async XLA Ops:
  2.3 1.9 %collective-permute-start = (f32[256,128]{1,0:T(8,128)S(1)}, f32[256,128]{1,0:T(8,128)S(1)}, u32[]{:S(2)}, u32[]{:S(2)}) collective-permute-start(f32[256,128]{1,0:T(8,128)S(1)} %get-tuple-element.30), channel_id=1, source_target_pairs={{0,1},{1,0},{2,3},{3,2},{4,5},{5,4},{6,7},{7,6},{8,9},{9,8},{10,11... | collective-permute-start | bytes 393224 | tf_op jit(solution)/shard_map/ppermute | solution.py:388
  5.5 5.1 %collective-permute-start.1 = (f32[1,64,256]{2,1,0:T(8,128)S(1)}, f32[1,64,256]{2,1,0:T(8,128)S(1)}, u32[]{:S(2)}, u32[]{:S(2)}) collective-permute-start(f32[1,64,256]{2,1,0:T(8,128)S(1)} %get-tuple-element.31), channel_id=1, source_target_pairs={{0,2},{3,5},{4,6},{7,9},{8,10},{11,13},{12,14},{15,17},{16,18},{19... | collective-permute-start | bytes 196616 | tf_op jit(solution)/shard_map/ppermute | solution.py:390
  8.1 0.7 %copy-start = (s32[1,2]{1,0:T(1,128)S(1)}, s32[1,2]{1,0:T(1,128)}, u32[]{:S(2)}) copy-start(s32[1,2]{1,0:T(1,128)} %count.1) | copy-start | bytes 28
  8.1 2.5 %collective-permute-start.2 = (f32[6,64,256]{2,1,0:T(8,128)S(1)}, f32[6,64,256]{2,1,0:T(8,128)S(1)}, u32[]{:S(2)}, u32[]{:S(2)}) collective-permute-start(f32[6,64,256]{2,1,0:T(8,128)S(1)} %get-tuple-element.34.mine), channel_id=1, source_target_pairs={{0,1},{1,0},{2,3},{3,2},{4,5},{5,4},{6,7},{7,6},{8,9},{9,8},{10,11... | collective-permute-start | bytes 1179656 | tf_op jit(solution)/shard_map/ppermute | solution.py:388
  10.9 1.4 %collective-permute-start.3 = (f32[144,256]{1,0:T(8,128)S(1)}, f32[144,256]{1,0:T(8,128)S(1)}, u32[]{:S(2)}, u32[]{:S(2)}) collective-permute-start(f32[144,256]{1,0:T(8,128)S(1)} %second.1.planes), channel_id=1, source_target_pairs={{0,1},{1,0},{2,3},{3,2},{4,5},{5,4},{6,7},{7,6},{8,9},{9,8},{10,11... | collective-permute-start | bytes 442376 | tf_op jit(solution)/shard_map/ppermute | solution.py:388
  12.7 5.2 %collective-permute-start.4 = (f32[72,256]{1,0:T(8,128)S(1)}, f32[72,256]{1,0:T(8,128)S(1)}, u32[]{:S(2)}, u32[]{:S(2)}) collective-permute-start(f32[72,256]{1,0:T(8,128)S(1)} %leaving.1), channel_id=1, source_target_pairs={{0,2},{3,5},{4,6},{7,9},{8,10},{11,13},{12,14},{15,17},{16,18},{19... | collective-permute-start | bytes 221192 | tf_op jit(solution)/shard_map/ppermute | solution.py:390
  17.8 1.3 %collective-permute-start.5 = (f32[72,256]{1,0:T(8,128)S(1)}, f32[72,256]{1,0:T(8,128)S(1)}, u32[]{:S(2)}, u32[]{:S(2)}) collective-permute-start(f32[72,256]{1,0:T(8,128)S(1)} %collective-permute-done.4.received), channel_id=1, source_target_pairs={{0,1},{1,0},{2,3},{3,2},{4,5},{5,4},{6,7},{7,6},{8,9},{9,8},{10,11... | collective-permute-start | bytes 221192 | tf_op jit(solution)/shard_map/ppermute | solution.py:388

commit v5 on v4

--- a/solution.py
+++ b/solution.py
@@ -69,15 +69,16 @@
     return jnp.where(side == 0, slab > 0, slab < lax.axis_size("slab") - 1)
 
 
-def across_pairs(slabs):
-    last = slabs - 1
-    up_out = lambda s: 0 if s == 0 else s % 2
-    up_in = lambda s: 1 if s == 0 else s % 2
-    down_out = lambda s: 1 if s == last else 1 - s % 2
-    down_in = lambda s: 0 if s == last else 1 - s % 2
+def across_pairs(slabs, second):
+    last, first_out = slabs - 1, 1 if second else 0
+    up_out = lambda s: first_out if s == 0 else s % 2
+    up_in = lambda s: 1 - first_out if s == 0 else s % 2
+    down_out = lambda s: 1 - first_out if s == last else 1 - s % 2
+    down_in = lambda s: first_out if s == last else 1 - s % 2
     pairs = [(s * 2 + up_out(s), (s + 1) * 2 + down_in(s + 1)) for s in range(last)]
     pairs += [((s + 1) * 2 + down_out(s + 1), s * 2 + up_in(s)) for s in range(last)]
-    return pairs + [(1, 0), (last * 2, last * 2 + 1)]
+    closing = [(1 - first_out, first_out), (last * 2 + first_out, last * 2 + 1 - first_out)]
+    return pairs + closing
 
 
 def plane_moments(plane, sizes, weights, cells, plane_shape):
@@ -124,7 +125,7 @@
 
 
 def load_kernel(*refs):
-    inputs, live, out, kept, active, sems = refs[:8], refs[8], refs[9], refs[10:18], *refs[18:]
+    inputs, live, out, kept, active, sems = refs[:9], refs[9], refs[10], refs[11:20], *refs[20:]
     copies = [pltpu.make_async_copy(src, dst, sems.at[i]) for i, (src, dst) in enumerate(zip(inputs, kept))]
     for copy in copies:
         copy.start()
@@ -187,15 +188,15 @@
 
 def late_kernel(state, packed, event_cell, event_count, inlet, out, late, *, parcel_rows):
     plane_shape = out.shape[1:]
-    events, width = event_cell.shape[1:]
-    spans, _ = sections(parcel_rows, events * width // LANES, plane_shape[0])
+    events = event_cell.shape[1:]
+    spans, _ = sections(parcel_rows, events[0] * events[1] // LANES, plane_shape[0])
     plane = receiving_side()
     for c in range(5):
         out[c] = state[c]
     out[5] = inlet[0].astype(F32)
     for k in range(SUBS):
         mine = plane_counts(plane, *own_events(event_cell, event_count, SUBS + k), plane_shape)
-        late[k] = mine + plane_counts(plane, *packed_events(packed, spans[3:5], SUBS + k, width), plane_shape)
+        late[k] = mine + plane_counts(plane, *packed_events(packed, spans[3:5], SUBS + k, events[1]), plane_shape)
 
 
 def moved(field):
@@ -215,7 +216,7 @@
     return field + inlet * (INLET - field)
 
 
-def second_kernel(beside, mine, other, late, given, out):
+def second_kernel(beside, mine, other, late, info, their_info, front, total, out, *, parts):
     lines = beside.shape[1]
     now, zeroth, first, second, grown = (jnp.where(ends(), other[c], mine[c]) for c in range(5))
     partner_field = jnp.where(ends(), mine[0], other[0])
@@ -223,41 +224,48 @@
     now = transport(now, beside[0], partner_field, inlet, receiving_side())
     for k in range(SUBS):
         now, first, second, grown = substep(now, zeroth, first, second, late[k], grown)
-    out[pl.ds(0, lines)] = now
-    out[pl.ds(lines, lines)] = grown
-    out[pl.ds(2 * lines, given.shape[0])] = given[...]
-
-
-def migrants_kernel(size, weight, cell, rows, count, keep, give, *, places):
-    side = sending_side()
+    front[0] = now
+    total[0] = grown
+    half = info.shape[0] // 2
+    rows = by_owner(info[pl.ds(half, half)], their_info[pl.ds(0, half)], parts)
+    for i, value in enumerate(plane_growth(grown, rows, parts)):
+        out[i : i + 1] = value
+    out[2 * parts :] = jnp.zeros((out.shape[0] - 2 * parts, out.shape[1]), F32)
+
+
+def migrants_kernel(size, weight, cell, rows, count, out, *, places):
+    side = receiving_side()
     table_rows = size.shape[0]
     slots = rows.shape[2]
-    table = []
+    table, nothing = [], jnp.zeros(size.shape, BF16)
     for values in (size[...], weight[...]):
-        rest = values
+        stack, rest = [], values
         for _ in range(3):
             part = rest.astype(BF16)
             rest = rest - part.astype(F32)
-            table.append(part)
+            stack.append(part)
+        table.append(jnp.concatenate(stack, axis=0))
     cells = cell[...]
-    table += [(cells // places).astype(F32).astype(BF16), (cells % places).astype(F32).astype(BF16)]
+    for values in (cells // places, cells % places):
+        table.append(jnp.concatenate([values.astype(F32).astype(BF16), nothing, nothing], axis=0))
     table = jnp.concatenate(table, axis=1)
     slot = lax.broadcasted_iota(jnp.int32, (1, slots), 1)
-    for out, j in ((keep, side), (give, 1 - side)):
+    half = out.shape[0] // 2
+    for block, j in ((0, side), (half, 1 - side)):
         row = jnp.where(j == 0, rows[0, 0:1, :], rows[0, 1:2, :])
         used = jnp.where(j == 0, count[0:1, 0:1], count[0:1, 1:2])
         valid = jnp.where(slot < used, 1.0, 0.0)
-        picked = lax.dot_general(table, hot(table_rows, row // LANES), TN, preferred_element_type=F32)
+        hot_row = jnp.concatenate([hot(table_rows, row // LANES)] * 3, axis=0)
+        picked = lax.dot_general(table, hot_row, TN, preferred_element_type=F32)
         hot_lane = hot(LANES, row % LANES).astype(F32)
-        found = [jnp.sum(picked[c * LANES : (c + 1) * LANES] * hot_lane, axis=0, keepdims=True) for c in range(8)]
-        sizes = (found[0] + found[1] + found[2]) * valid
-        weights = (found[3] + found[4] + found[5]) * valid
-        at = 0
-        for value in (sizes, weights, found[6], found[7], valid):
+        found = [jnp.sum(picked[c * LANES : (c + 1) * LANES] * hot_lane, axis=0, keepdims=True) for c in range(4)]
+        sizes, weights = found[0] * valid, found[1] * valid
+        at = block
+        for value in (sizes, weights, found[2], found[3], valid):
             for start in range(0, slots, places):
                 out[at : at + 1] = value[:, start : start + places]
                 at += 1
-        out[at:] = jnp.zeros((out.shape[0] - at, places), F32)
+        out[at : block + half] = jnp.zeros((block + half - at, places), F32)
 
 
 def grown_at(stacked, line, place):
@@ -268,39 +276,51 @@
     return jnp.sum(jnp.where(index == line, picked, 0.0), axis=0, keepdims=True)
 
 
-def both_planes(planes, partner, lines):
-    mine, other = planes[pl.ds(lines, lines)], partner[pl.ds(lines, lines)]
+def both_planes(mine, other):
     first = receiving_side() == 0
     low = jnp.where(first, mine, other)
     high = jnp.where(first, other, mine)
     return jnp.concatenate(pieces(jnp.concatenate([low, high], axis=0)), axis=0)
 
 
-def leaving_kernel(planes, partner, kept, out, *, lines, parts):
-    stacked = both_planes(planes, partner, lines)
-    here = pl.ds(0, lines)
-    out[here] = jnp.where(ends(), partner[here], planes[here])
-    grp = lax.axis_index("grp")
-    taken = partner[pl.ds(2 * lines, kept.shape[0])]
-    keeping = kept[...]
-    blocks = [jnp.where(grp == 0, one, other) for one, other in ((keeping, taken), (taken, keeping))]
-    pick = lambda c: [block[i : i + 1] for block in blocks for i in range(c * parts, (c + 1) * parts)]
-    sizes, weights, valid = pick(0), pick(1), pick(4)
-    line = jnp.concatenate(pick(2), axis=1).astype(jnp.int32)
-    place = jnp.concatenate(pick(3), axis=1).astype(jnp.int32)
-    grown = grown_at(stacked, line, place)
-    places = planes.shape[1]
+def by_owner(mine, partners, parts):
+    first = lax.axis_index("grp") == 0
+    blocks = [jnp.where(first, one, other) for one, other in ((mine, partners), (partners, mine))]
+    return lambda c: [block[i : i + 1] for block in blocks for i in range(c * parts, (c + 1) * parts)]
+
+
+def plane_growth(grown, rows, parts):
+    lines, places = grown.shape
+    stacked = jnp.concatenate(pieces(grown), axis=0)
+    line = jnp.concatenate(rows(2), axis=1).astype(jnp.int32) - receiving_side() * lines
+    found = grown_at(stacked, line, jnp.concatenate(rows(3), axis=1).astype(jnp.int32))
+    valid = rows(4)
+    return [found[:, i * places : (i + 1) * places] * valid[i] for i in range(2 * parts)]
+
+
+def own_kernel(total, info, their_info, out, *, parts):
+    half = info.shape[0] // 2
+    rows = by_owner(info[pl.ds(0, half)], their_info[pl.ds(half, half)], parts)
+    found = plane_growth(total[0], rows, parts)
+    sizes, weights = rows(0), rows(1)
+    for i in range(2 * parts):
+        at = (i // parts) * 2 * parts + i % parts
+        out[at : at + 1] = sizes[i] + found[i]
+        out[at + parts : at + parts + 1] = weights[i]
+
+
+def leaving_kernel(front, own, theirs, out, *, parts):
+    lines = front.shape[1]
+    out[pl.ds(0, lines)] = front[0]
     for j in range(2):
-        at = lines + 2 * parts * j
-        for p in range(parts):
-            i = j * parts + p
-            out[at + p : at + p + 1] = sizes[i] + grown[:, i * places : (i + 1) * places] * valid[i]
-            out[at + parts + p : at + parts + p + 1] = weights[i]
-
-
-def sizes_kernel(planes, partner, size, cell, active, out, *, lines):
-    places = planes.shape[1]
-    stacked = both_planes(planes, partner, lines)
+        at = 2 * parts * j
+        out[lines + at : lines + at + parts] = own[at : at + parts] + theirs[j * parts : (j + 1) * parts]
+        out[lines + at + parts : lines + at + 2 * parts] = own[at + parts : at + 2 * parts]
+
+
+def sizes_kernel(total, their_total, size, cell, active, out):
+    places = total.shape[2]
+    stacked = both_planes(total[0], their_total[0])
     cells = cell[...]
     line = cells // places
     place = cells % places
@@ -318,12 +338,10 @@
     out[...] = active[...] * (size[...] + grown)
 
 
-def rest_kernel(planes, partner, inlet, out):
-    lines = inlet.shape[1]
-    here = pl.ds(0, lines)
+def rest_kernel(front, their_front, inlet, out):
     other = receives_other()
-    field = jnp.where(other, partner[here], planes[here])
-    beyond = jnp.where(other, planes[here], partner[here])
+    field = jnp.where(other, their_front[0], front[0])
+    beyond = jnp.where(other, front[0], their_front[0])
     keep = 1.0 - inlet[0].astype(F32)
     field = field + DIFFUSE * (beyond + moved(field) - 6.0 * field)
     out[0] = keep * field + (1.0 - keep) * INLET
@@ -333,11 +351,11 @@
 def last_kernel(rest, received, relayed, field_out, arrivals_out, *, lines, parts):
     slab, grp = lax.axis_index("slab"), lax.axis_index("grp")
     here = pl.ds(0, lines)
-    field_out[0] = rest[0] + rest[1] * jnp.where(receives_other(), relayed[here], received[here])
+    field_out[0] = rest[0] + rest[1] * jnp.where(sends_other(), relayed[here], received[here])
     rows = 2 * parts
     pick = lambda block: jnp.where(grp == 0, block[lines : lines + rows], block[lines + rows : lines + 2 * rows])
     mine, theirs = pick(received), pick(relayed)
-    from_lower = receiving_side() == 0
+    from_lower = sending_side() == 0
     lower = jnp.where(slab > 0, jnp.where(from_lower, mine, theirs), 0.0)
     upper = jnp.where(slab < lax.axis_size("slab") - 1, jnp.where(from_lower, theirs, mine), 0.0)
     places = mine.shape[1]
@@ -386,21 +404,21 @@
     slots = migrant_rows.shape[2]
     parts = slots // places
     swap = lambda value: lax.ppermute(value, "grp", [(0, 1), (1, 0)])
-    pairs = across_pairs(lax.axis_size("slab"))
-    across = lambda value: lax.ppermute(value, ("slab", "grp"), pairs)
+    slabs = lax.axis_size("slab")
+    across = lambda value, second: lax.ppermute(value, ("slab", "grp"), across_pairs(slabs, second))
 
     hbm = lambda a: pltpu.with_memory_space_constraint(a, pltpu.HBM)
     like = lambda a: jax.ShapeDtypeStruct(a.shape, a.dtype)
     inputs = [a.reshape(-1, LANES) for a in (crystal_size, crystal_weight, crystal_cell)]
-    inputs += [nucleus_cell, nucleus_count, saturation, inlet_mask, migrant_rows]
+    inputs += [nucleus_cell, nucleus_count, saturation, inlet_mask, migrant_rows, migrant_count]
     parcel_rows, events = inputs[0].shape[0], nucleus_cell.shape[1:]
     _, packed_rows = sections(parcel_rows, events[0] * events[1] // LANES, lines)
-    packed, size, weight, cell, event_cell, event_count, field, inlet, rows, active = call(
+    packed, size, weight, cell, event_cell, event_count, field, inlet, rows, count, active = call(
         load_kernel,
         [shape(packed_rows, LANES)] + [like(a) for a in inputs] + [shape(*inputs[0].shape)],
         *[hbm(a) for a in inputs],
         live_count,
-        specs=[HBM] * 8 + [SMEM],
+        specs=[HBM] * 9 + [SMEM],
         scratch=[pltpu.SemaphoreType.DMA((len(inputs),))],
         name="load",
     )
@@ -413,34 +431,40 @@
         functools.partial(front_kernel, parcel_rows=parcel_rows, events=events),
         (shape(1, lines, places), shape(5, lines, places)), field, home, packed, name="front",
     )
-    beside = across(front)
+    beside = across(front, False)
     _, state = lax.optimization_barrier((front, state))
     mine, late = call(
         functools.partial(late_kernel, parcel_rows=parcel_rows), (shape(6, lines, places), shape(SUBS, lines, places)),
         state, packed, event_cell, event_count, inlet, cost=1 << 28, name="late",
     )
     other = swap(mine)
-    info = (shape(16, places), shape(16, places))
-    kept, given = call(
-        functools.partial(migrants_kernel, places=places), info, size, weight, cell, rows, migrant_count,
+    info = call(
+        functools.partial(migrants_kernel, places=places), shape(32, places), size, weight, cell, rows, count,
         cost=1 << 33, name="migrants",
     )
-    planes = call(
-        second_kernel, shape(2 * lines + 16, places), beside, mine, other, late, given, name="second"
-    )
-    partner = swap(planes)
+    their_info = swap(info)
+    front, total, given = call(
+        functools.partial(second_kernel, parts=parts),
+        (shape(1, lines, places), shape(1, lines, places), shape(8, places)),
+        beside, mine, other, late, info, their_info, name="second",
+    )
+    theirs = swap(given)
+    own = call(
+        functools.partial(own_kernel, parts=parts), shape(4 * parts, places), total, info, their_info,
+        cost=1 << 28, name="own",
+    )
     leaving = call(
-        functools.partial(leaving_kernel, lines=lines, parts=parts),
-        shape(lines + 4 * parts, places), planes, partner, kept, name="leaving",
-    )
-    received = across(leaving)
+        functools.partial(leaving_kernel, parts=parts), shape(lines + 4 * parts, places), front, own, theirs, name="leaving"
+    )
+    received = across(leaving, True)
+    _, later = lax.optimization_barrier((leaving, total))
+    their_total, their_front = swap(later), swap(front)
     size_out = call(
-        functools.partial(sizes_kernel, lines=lines), shape(*size.shape), planes, partner, size, cell, active,
-        cost=1 << 31, name="sizes",
+        sizes_kernel, shape(*size.shape), total, their_total, size, cell, active, cost=1 << 26, name="sizes",
     )
     received, size_out = lax.optimization_barrier((received, size_out))
     relayed = swap(received)
-    rest = call(rest_kernel, shape(2, lines, places), planes, partner, inlet, cost=1 << 28, name="rest")
+    rest = call(rest_kernel, shape(2, lines, places), front, their_front, inlet, cost=1 << 28, name="rest")
     field_out, arrivals = call(
         functools.partial(last_kernel, lines=lines, parts=parts),
         (shape(1, lines, places), shape(1, 2, 2, slots)), rest, received, relayed, name="last",

time: 20 us -> 19.7 us (0.985)
  starting transfers between devices: 5.02 us -> 6.15 us
  waiting for transfers between devices: 4.91 us -> 4.18 us
  local copies, waits for them, and re-layouts: 0.57 us -> 0 us
    ppermute x2, waiting for transfers between devices: 2.47 us -> 0.64 us  [local(): lax.ppermute(value, ('slab', 'grp'), across_pairs(slabs, second))]
    ppermute x4 -> x7, waiting for transfers between devices: 2.44 us -> 3.55 us  [local(): swap = lambda value: lax.ppermute(value, 'grp', [(0, 1), (1, 0)])]
    ppermute x4 -> x7, starting transfers between devices: 0.93 us -> 2.03 us  [local(): swap = lambda value: lax.ppermute(value, 'grp', [(0, 1), (1, 0)])]
    unnamed x2 -> x0, local copies, waits for them, and re-layouts: 0.57 us -> none
    pallas_call x10 -> x11, Pallas kernels: 7.86 us -> 7.74 us  [call(): pl.pallas_call(kernel, out_shape=out_shape, in_specs=specs or [VMEM] * le...]
  transfers between devices with their start and end apart: 6 -> 9, of which waited for: 4 -> 6; matrix products, arithmetic and copies ran while one was open for 0% -> 0% of each run, Pallas kernels for 22% -> 22%
where the time goes in v5:
time: 19.7 us; the launch traced here: 19.4 us
  Pallas kernels  7.74 us (39%)
  starting transfers between devices  6.15 us (31%)
  waiting for transfers between devices  4.18 us (21%)
  between operations  1.37 us (7%)
    pallas_call x11, Pallas kernels, call(): pl.pallas_call(kernel, out_shape=out_shape, in_specs=specs or [VMEM] * le...  7.74 us
    ppermute x2, starting transfers between devices, local(): lax.ppermute(value, ('slab', 'grp'), across_pairs(slabs, second))  4.12 us
    ppermute x7, waiting for transfers between devices, local(): swap = lambda value: lax.ppermute(value, 'grp', [(0, 1), (1, 0)])  3.55 us
    ppermute x7, starting transfers between devices, local(): swap = lambda value: lax.ppermute(value, 'grp', [(0, 1), (1, 0)])  2.03 us
    ppermute x2, waiting for transfers between devices, local(): lax.ppermute(value, ('slab', 'grp'), across_pairs(slabs, second))  0.64 us
  transfers between devices with their start and end apart: 9, of which 6 were waited for; matrix products, arithmetic and copies ran while one was open for 0% of the time, Pallas kernels for 22%

profile of v5, /device:TPU:9, one launch (start us, length us, event | category | flops | bytes accessed | tf_op | source)
XLA Modules:
  0.0 19.4 jit_solution(10147043241143982400)
XLA Ops:
  1.3 1.1 %load.1 = (f32[256,128]{1,0:T(8,128)S(1)}, f32[32,128]{1,0:T(8,128)S(1)}, f32[32,128]{1,0:T(8,128)S(1)}, s32[32,128]{1,0:T(8,128)S(1)}, s32[1,4,512]{2,1,0:T(4,1...) custom-call(f32[32,128]{1,0:T(8,128)} %bitcast.4, ...), custom_call_target="tpu_custom_call" | custom-call | tf_op jit(solution)/shard_map/load/pallas_call | solution.py:379
  2.4 0.7 %collective-permute-start = (f32[256,128]{1,0:T(8,128)S(1)}, f32[256,128]{1,0:T(8,128)S(1)}, u32[]{:S(2)}, u32[]{:S(2)}) collective-permute-start(f32[256,128]{1,0:T(8,128)S(1)} %get-tuple-element.33), channel_id=1, source_target_pairs={{0,1},{1,0},{2,3},{3,2},{4,5},{5,4},{6,7},{7,6},{8,9},{9,8},{10,11... | collective-permute-start | bytes 393224 | tf_op jit(solution)/shard_map/ppermute | solution.py:406
  3.1 1.1 %home.1 = f32[5,64,256]{2,1,0:T(8,128)S(1)} custom-call(f32[32,128]{1,0:T(8,128)S(1)} %get-tuple-element.28.size, f32[32,128]{1,0:T(8,128)S(1)} %get-tuple-element.29.weight, s32[32,128]{1,0:T(8,128)S(1)} %get-tuple-element.30.cell, s32[1,4,512]{2,1,0:T(4,128)S(1)} %get-tuple-element.31.event_cell, s32[1,4,512]{2,1,0:T(4,128)S(1)} %get-tuple-element.32.event_count), custom_call_target="tpu_custom_call" | custom-call | flops 1073741824 | tf_op jit(solution)/shard_map/home/pallas_call | solution.py:379
  4.2 0.0 collective-permute-done.packed
  4.3 1.3 %front.1 = (f32[1,64,256]{2,1,0:T(8,128)S(1)}, f32[5,64,256]{2,1,0:T(8,128)S(1)}) custom-call(f32[1,64,256]{2,1,0:T(8,128)S(1)} %get-tuple-element.27.field, f32[5,64,256]{2,1,0:T(8,128)S(1)} %home.1, f32[256,128]{1,0:T(8,128)S(1)} %collective-permute-done.packed), custom_call_target="tpu_custom_call" | custom-call | tf_op jit(solution)/shard_map/front/pallas_call | solution.py:379
  5.5 2.1 %collective-permute-start.1 = (f32[1,64,256]{2,1,0:T(8,128)S(1)}, f32[1,64,256]{2,1,0:T(8,128)S(1)}, u32[]{:S(2)}, u32[]{:S(2)}) collective-permute-start(f32[1,64,256]{2,1,0:T(8,128)S(1)} %get-tuple-element.34), channel_id=1, source_target_pairs={{0,2},{3,5},{4,6},{7,9},{8,10},{11,13},{12,14},{15,17},{16,18},{19... | collective-permute-start | bytes 196616 | tf_op jit(solution)/shard_map/ppermute | solution.py:408
  7.6 0.5 %late.1 = (f32[6,64,256]{2,1,0:T(8,128)S(1)}, f32[2,64,256]{2,1,0:T(8,128)S(1)}) custom-call(f32[5,64,256]{2,1,0:T(8,128)S(1)} %get-tuple-element.35.state, f32[256,128]{1,0:T(8,128)S(1)} %collective-permute-done.packed, s32[1,4,512]{2,1,0:T(4,128)S(1)} %get-tuple-element.31.event_cell, s32[1,4,512]{2,1,0:T(4,128)S(1)} %get-tuple-element.32.event_count, ...), custom_call_target="tpu_custom_call" | custom-call | flops 268435456 | tf_op jit(solution)/shard_map/late/pallas_call | solution.py:379
  8.1 0.1 collective-permute-start.2
  8.2 0.5 %migrants.1.info = f32[32,256]{1,0:T(8,128)S(1)} custom-call(f32[32,128]{1,0:T(8,128)S(1)} %get-tuple-element.28.size, f32[32,128]{1,0:T(8,128)S(1)} %get-tuple-element.29.weight, s32[32,128]{1,0:T(8,128)S(1)} %get-tuple-element.30.cell, s32[1,2,512]{2,1,0:T(2,128)S(1)} %get-tuple-element.39.rows, s32[1,2]{1,0:T(1,128)S(1)} %get-tuple-element.40.count), custom_call_target="tpu_custom_call" | custom-call | flops 8589934592 | tf_op jit(solution)/shard_map/migrants/pallas_call | solution.py:379
  8.7 0.6 %collective-permute-start.3 = (f32[32,256]{1,0:T(8,128)S(1)}, f32[32,256]{1,0:T(8,128)S(1)}, u32[]{:S(2)}, u32[]{:S(2)}) collective-permute-start(f32[32,256]{1,0:T(8,128)S(1)} %migrants.1.info), channel_id=1, source_target_pairs={{0,1},{1,0},{2,3},{3,2},{4,5},{5,4},{6,7},{7,6},{8,9},{9,8},{10,11... | collective-permute-start | bytes 98312 | tf_op jit(solution)/shard_map/ppermute | solution.py:406
  9.3 0.9 %collective-permute-done.3.their_info = f32[32,256]{1,0:T(8,128)S(1)} collective-permute-done((f32[32,256]{1,0:T(8,128)S(1)}, f32[32,256]{1,0:T(8,128)S(1)}, u32[]{:S(2)}, u32[]{:S(2)}) %collective-permute-start.3) | collective-permute-done | bytes 32800 | tf_op jit(solution)/shard_map/ppermute | solution.py:406
  10.1 0.5 %collective-permute-done.1.beside = f32[1,64,256]{2,1,0:T(8,128)S(1)} collective-permute-done((f32[1,64,256]{2,1,0:T(8,128)S(1)}, f32[1,64,256]{2,1,0:T(8,128)S(1)}, u32[]{:S(2)}, u32[]{:S(2)}) %collective-permute-start.1) | collective-permute-done | bytes 65568 | tf_op jit(solution)/shard_map/ppermute | solution.py:408
  10.6 0.0 collective-permute-done.2.other
  10.6 0.5 %second.1 = (f32[1,64,256]{2,1,0:T(8,128)S(1)}, f32[1,64,256]{2,1,0:T(8,128)S(1)}, f32[8,256]{1,0:T(8,128)S(1)}) custom-call(f32[1,64,256]{2,1,0:T(8,128)S(1)} %collective-permute-done.1.beside, f32[6,64,256]{2,1,0:T(8,128)S(1)} %get-tuple-element.37.mine, f32[6,64,256]{2,1,0:T(8,128)S(1)} %collective-permute-done.2.other, ...), custom_call_target="tpu_custom_call" | custom-call | tf_op jit(solution)/shard_map/second/pallas_call | solution.py:379
  11.1 0.1 collective-permute-start.5
  11.2 0.3 %own.1 = f32[8,256]{1,0:T(8,128)S(1)} custom-call(f32[1,64,256]{2,1,0:T(8,128)S(1)} %get-tuple-element.44.total, f32[32,256]{1,0:T(8,128)S(1)} %migrants.1.info, f32[32,256]{1,0:T(8,128)S(1)} %collective-permute-done.3.their_info), custom_call_target="tpu_custom_call" | custom-call | flops 268435456 | tf_op jit(solution)/shard_map/own/pallas_call | solution.py:379
  11.5 0.9 %collective-permute-done.5.theirs = f32[8,256]{1,0:T(8,128)S(1)} collective-permute-done((f32[8,256]{1,0:T(8,128)S(1)}, f32[8,256]{1,0:T(8,128)S(1)}, u32[]{:S(2)}, u32[]{:S(2)}) %collective-permute-start.5) | collective-permute-done | bytes 8224 | tf_op jit(solution)/shard_map/ppermute | solution.py:406
  12.4 2.0 %collective-permute-start.6 = (f32[72,256]{1,0:T(8,128)S(1)}, f32[72,256]{1,0:T(8,128)S(1)}, u32[]{:S(2)}, u32[]{:S(2)}) collective-permute-start(f32[72,256]{1,0:T(8,128)S(1)} %leaving.1), channel_id=1, source_target_pairs={{1,2},{3,5},{4,6},{7,9},{8,10},{11,13},{12,14},{15,17},{16,18},{19... | collective-permute-start | bytes 221192 | tf_op jit(solution)/shard_map/ppermute | solution.py:408
  14.4 0.0 collective-permute-start.7
  14.4 0.5 %collective-permute-start.4 = (f32[1,64,256]{2,1,0:T(8,128)S(1)}, f32[1,64,256]{2,1,0:T(8,128)S(1)}, u32[]{:S(2)}, u32[]{:S(2)}) collective-permute-start(f32[1,64,256]{2,1,0:T(8,128)S(1)} %get-tuple-element.41.front), channel_id=1, source_target_pairs={{0,1},{1,0},{2,3},{3,2},{4,5},{5,4},{6,7},{7,6},{8,9},{9,8},{10,11... | collective-permute-start | bytes 196616 | tf_op jit(solution)/shard_map/ppermute | solution.py:406
  14.9 0.7 %collective-permute-done.7.their_total = f32[1,64,256]{2,1,0:T(8,128)S(1)} collective-permute-done((f32[1,64,256]{2,1,0:T(8,128)S(1)}, f32[1,64,256]{2,1,0:T(8,128)S(1)}, u32[]{:S(2)}, u32[]{:S(2)}) %collective-permute-start.7) | collective-permute-done | bytes 65568 | tf_op jit(solution)/shard_map/ppermute | solution.py:406
  15.6 1.7 %sizes.1 = f32[32,128]{1,0:T(8,128)} custom-call(f32[1,64,256]{2,1,0:T(8,128)S(1)} %get-tuple-element.44.total, f32[1,64,256]{2,1,0:T(8,128)S(1)} %collective-permute-done.7.their_total, f32[32,128]{1,0:T(8,128)S(1)} %get-tuple-element.28.size, s32[32,128]{1,0:T(8,128)S(1)} %get-tuple-element.30.cell, f32[32,128]{1,0:T(8,128)S(1)} %get-tuple-element.45.active), custom_call_target="tpu_custom_call" | custom-call | flops 67108864 | tf_op jit(solution)/shard_map/sizes/pallas_call | solution.py:379
  17.3 0.2 collective-permute-done.6.received
  17.5 0.1 collective-permute-start.8
  17.6 0.0 collective-permute-done.4.their_front
  17.6 0.1 rest.1
  17.7 1.0 %collective-permute-done.8.relayed = f32[72,256]{1,0:T(8,128)S(1)} collective-permute-done((f32[72,256]{1,0:T(8,128)S(1)}, f32[72,256]{1,0:T(8,128)S(1)}, u32[]{:S(2)}, u32[]{:S(2)}) %collective-permute-start.8) | collective-permute-done | bytes 73760 | tf_op jit(solution)/shard_map/ppermute | solution.py:406
  18.8 0.7 %last.1 = (f32[1,64,256]{2,1,0:T(8,128)}, f32[1,2,2,512]{3,2,1,0:T(2,128)}) custom-call(f32[2,64,256]{2,1,0:T(8,128)S(1)} %rest.1, f32[72,256]{1,0:T(8,128)S(1)} %collective-permute-done.6.received, f32[72,256]{1,0:T(8,128)S(1)} %collective-permute-done.8.relayed), custom_call_target="tpu_custom_call" | custom-call | tf_op jit(solution)/shard_map/last/pallas_call | solution.py:379
  (1 shorter events, 0.0 us)
Async XLA Ops:
  2.4 1.9 %collective-permute-start = (f32[256,128]{1,0:T(8,128)S(1)}, f32[256,128]{1,0:T(8,128)S(1)}, u32[]{:S(2)}, u32[]{:S(2)}) collective-permute-start(f32[256,128]{1,0:T(8,128)S(1)} %get-tuple-element.33), channel_id=1, source_target_pairs={{0,1},{1,0},{2,3},{3,2},{4,5},{5,4},{6,7},{7,6},{8,9},{9,8},{10,11... | collective-permute-start | bytes 393224 | tf_op jit(solution)/shard_map/ppermute | solution.py:406
  5.5 5.1 %collective-permute-start.1 = (f32[1,64,256]{2,1,0:T(8,128)S(1)}, f32[1,64,256]{2,1,0:T(8,128)S(1)}, u32[]{:S(2)}, u32[]{:S(2)}) collective-permute-start(f32[1,64,256]{2,1,0:T(8,128)S(1)} %get-tuple-element.34), channel_id=1, source_target_pairs={{0,2},{3,5},{4,6},{7,9},{8,10},{11,13},{12,14},{15,17},{16,18},{19... | collective-permute-start | bytes 196616 | tf_op jit(solution)/shard_map/ppermute | solution.py:408
  8.1 2.5 %collective-permute-start.2 = (f32[6,64,256]{2,1,0:T(8,128)S(1)}, f32[6,64,256]{2,1,0:T(8,128)S(1)}, u32[]{:S(2)}, u32[]{:S(2)}) collective-permute-start(f32[6,64,256]{2,1,0:T(8,128)S(1)} %get-tuple-element.37.mine), channel_id=1, source_target_pairs={{0,1},{1,0},{2,3},{3,2},{4,5},{5,4},{6,7},{7,6},{8,9},{9,8},{10,11... | collective-permute-start | bytes 1179656 | tf_op jit(solution)/shard_map/ppermute | solution.py:406
  8.7 1.4 %collective-permute-start.3 = (f32[32,256]{1,0:T(8,128)S(1)}, f32[32,256]{1,0:T(8,128)S(1)}, u32[]{:S(2)}, u32[]{:S(2)}) collective-permute-start(f32[32,256]{1,0:T(8,128)S(1)} %migrants.1.info), channel_id=1, source_target_pairs={{0,1},{1,0},{2,3},{3,2},{4,5},{5,4},{6,7},{7,6},{8,9},{9,8},{10,11... | collective-permute-start | bytes 98312 | tf_op jit(solution)/shard_map/ppermute | solution.py:406
  11.1 1.2 %collective-permute-start.5 = (f32[8,256]{1,0:T(8,128)S(1)}, f32[8,256]{1,0:T(8,128)S(1)}, u32[]{:S(2)}, u32[]{:S(2)}) collective-permute-start(f32[8,256]{1,0:T(8,128)S(1)} %get-tuple-element.43), channel_id=1, source_target_pairs={{0,1},{1,0},{2,3},{3,2},{4,5},{5,4},{6,7},{7,6},{8,9},{9,8},{10,11... | collective-permute-start | bytes 24584 | tf_op jit(solution)/shard_map/ppermute | solution.py:406
  12.4 5.2 %collective-permute-start.6 = (f32[72,256]{1,0:T(8,128)S(1)}, f32[72,256]{1,0:T(8,128)S(1)}, u32[]{:S(2)}, u32[]{:S(2)}) collective-permute-start(f32[72,256]{1,0:T(8,128)S(1)} %leaving.1), channel_id=1, source_target_pairs={{1,2},{3,5},{4,6},{7,9},{8,10},{11,13},{12,14},{15,17},{16,18},{19... | collective-permute-start | bytes 221192 | tf_op jit(solution)/shard_map/ppermute | solution.py:408
  14.4 1.3 %collective-permute-start.7 = (f32[1,64,256]{2,1,0:T(8,128)S(1)}, f32[1,64,256]{2,1,0:T(8,128)S(1)}, u32[]{:S(2)}, u32[]{:S(2)}) collective-permute-start(f32[1,64,256]{2,1,0:T(8,128)S(1)} %get-tuple-element.44.total), channel_id=1, source_target_pairs={{0,1},{1,0},{2,3},{3,2},{4,5},{5,4},{6,7},{7,6},{8,9},{9,8},{10,11... | collective-permute-start | bytes 196616 | tf_op jit(solution)/shard_map/ppermute | solution.py:406
  14.4 3.2 %collective-permute-start.4 = (f32[1,64,256]{2,1,0:T(8,128)S(1)}, f32[1,64,256]{2,1,0:T(8,128)S(1)}, u32[]{:S(2)}, u32[]{:S(2)}) collective-permute-start(f32[1,64,256]{2,1,0:T(8,128)S(1)} %get-tuple-element.41.front), channel_id=1, source_target_pairs={{0,1},{1,0},{2,3},{3,2},{4,5},{5,4},{6,7},{7,6},{8,9},{9,8},{10,11... | collective-permute-start | bytes 196616 | tf_op jit(solution)/shard_map/ppermute | solution.py:406
  17.5 1.3 %collective-permute-start.8 = (f32[72,256]{1,0:T(8,128)S(1)}, f32[72,256]{1,0:T(8,128)S(1)}, u32[]{:S(2)}, u32[]{:S(2)}) collective-permute-start(f32[72,256]{1,0:T(8,128)S(1)} %collective-permute-done.6.received), channel_id=1, source_target_pairs={{0,1},{1,0},{2,3},{3,2},{4,5},{5,4},{6,7},{7,6},{8,9},{9,8},{10,11... | collective-permute-start | bytes 221192 | tf_op jit(solution)/shard_map/ppermute | solution.py:406

commit v6 on v5

--- a/solution.py
+++ b/solution.py
@@ -24,7 +24,7 @@
 
 
 def softplus(x):
-    return jnp.maximum(x, 0.0) + jnp.log1p(jnp.exp(-jnp.abs(x)))
+    return jnp.maximum(x, 0.0) + jnp.log(1.0 + jnp.exp(-jnp.abs(x)))
 
 
 def pieces(x):
@@ -111,6 +111,11 @@
     return event_cell[0, row, :], event_count[0, row, :].astype(F32)
 
 
+def own_counts(event_cell, event_count, out):
+    for k in range(SUBS):
+        out[k] = plane_counts(sending_side(), *own_events(event_cell, event_count, k), out.shape[1:])
+
+
 def sections(parcel_rows, event_rows, field_rows):
     sizes = [parcel_rows] * 3 + [event_rows] * 2 + [field_rows] * 2
     starts = [sum(sizes[:i]) for i in range(len(sizes) + 1)]
@@ -125,7 +130,7 @@
 
 
 def load_kernel(*refs):
-    inputs, live, out, kept, active, sems = refs[:9], refs[9], refs[10], refs[11:20], *refs[20:]
+    inputs, live, out, kept, active, counts, sems = refs[:9], refs[9], refs[10], refs[11:20], *refs[20:]
     copies = [pltpu.make_async_copy(src, dst, sems.at[i]) for i, (src, dst) in enumerate(zip(inputs, kept))]
     for copy in copies:
         copy.start()
@@ -148,14 +153,27 @@
     for j in range(2):
         out[spans[5 + j]] = field[0, :, pl.ds(j * LANES, LANES)]
 
-
-def home_kernel(size, weight, cell, event_cell, event_count, out):
-    plane_shape = out.shape[1:]
-    plane = sending_side()
-    for c, moment in enumerate(plane_moments(plane, size[...], weight[...], cell[...], plane_shape)):
-        out[c] = moment
-    for k in range(SUBS):
-        out[3 + k] = plane_counts(plane, *own_events(event_cell, event_count, k), plane_shape)
+    @pl.when(lax.axis_index("grp") == 1)
+    def _():
+        own_counts(event_cell, event_count, counts)
+
+
+def home_kernel(size, weight, cell, event_cell, event_count, counted, out, counts):
+    grp = lax.axis_index("grp")
+
+    def own_moments():
+        for c, moment in enumerate(plane_moments(sending_side(), size[...], weight[...], cell[...], out.shape[1:])):
+            out[c] = moment
+
+    @pl.when(grp == 0)
+    def _():
+        own_moments()
+        own_counts(event_cell, event_count, counts)
+
+    @pl.when(grp == 1)
+    def _():
+        own_moments()
+        counts[...] = counted[...]
 
 
 def substep(field, zeroth, first, second, counts, grown):
@@ -168,7 +186,7 @@
     return field, first, second, grown + growth
 
 
-def front_kernel(field, home, packed, out, state, *, parcel_rows, events):
+def front_kernel(field, home, home_counts, packed, out, state, *, parcel_rows, events):
     plane_shape = out.shape[1:]
     plane = sending_side()
     spans, _ = sections(parcel_rows, events[0] * events[1] // LANES, plane_shape[0])
@@ -179,24 +197,28 @@
     now = jnp.where(sends_other(), theirs, field[0])
     grown = jnp.zeros_like(now)
     for k in range(SUBS):
-        counts = home[3 + k] + plane_counts(plane, *packed_events(packed, spans[3:5], k, events[1]), plane_shape)
+        counts = home_counts[k] + plane_counts(plane, *packed_events(packed, spans[3:5], k, events[1]), plane_shape)
         now, first, second, grown = substep(now, zeroth, first, second, counts, grown)
     out[0] = now
     for c, value in enumerate((now, zeroth, first, second, grown)):
         state[c] = value
 
 
-def late_kernel(state, packed, event_cell, event_count, inlet, out, late, *, parcel_rows):
-    plane_shape = out.shape[1:]
-    events = event_cell.shape[1:]
-    spans, _ = sections(parcel_rows, events[0] * events[1] // LANES, plane_shape[0])
-    plane = receiving_side()
+def pack_kernel(state, inlet, out):
     for c in range(5):
         out[c] = state[c]
     out[5] = inlet[0].astype(F32)
+
+
+def late_kernel(packed, event_cell, event_count, late, *, parcel_rows):
+    plane_shape = late.shape[1:]
+    events, width = event_cell.shape[1:]
+    spans, _ = sections(parcel_rows, events * width // LANES, plane_shape[0])
     for k in range(SUBS):
-        mine = plane_counts(plane, *own_events(event_cell, event_count, SUBS + k), plane_shape)
-        late[k] = mine + plane_counts(plane, *packed_events(packed, spans[3:5], SUBS + k, events[1]), plane_shape)
+        mine = own_events(event_cell, event_count, SUBS + k)
+        theirs = packed_events(packed, spans[3:5], SUBS + k, width)
+        both = [jnp.concatenate(pair, axis=1) for pair in zip(mine, theirs)]
+        late[k] = plane_counts(receiving_side(), *both, plane_shape)
 
 
 def moved(field):
@@ -210,27 +232,39 @@
     return total
 
 
-def transport(field, beside, other, inlet, side):
-    around = jnp.where(has_beside(side), beside, 0.0) + other + moved(field)
-    field = field + DIFFUSE * (around - 6.0 * field)
-    return field + inlet * (INLET - field)
-
-
-def second_kernel(beside, mine, other, late, info, their_info, front, total, out, *, parts):
-    lines = beside.shape[1]
+def split_transport(field, other, inlet, side):
+    keep = 1.0 - inlet
+    field = field + DIFFUSE * (other + moved(field) - 6.0 * field)
+    return keep * field + inlet * INLET, jnp.where(has_beside(side), DIFFUSE * keep, 0.0)
+
+
+def ready_kernel(mine, other, info, their_info, out, hot_place, lists, *, parts):
     now, zeroth, first, second, grown = (jnp.where(ends(), other[c], mine[c]) for c in range(5))
     partner_field = jnp.where(ends(), mine[0], other[0])
     inlet = jnp.where(receives_other(), other[5], mine[5])
-    now = transport(now, beside[0], partner_field, inlet, receiving_side())
+    base, slope = split_transport(now, partner_field, inlet, receiving_side())
+    for c, value in enumerate((base, slope, zeroth, first, second, grown)):
+        out[c] = value
+    half = info.shape[0] // 2
+    rows = by_owner(info[pl.ds(half, half)], their_info[pl.ds(0, half)], parts)
+    lists[0:1] = jnp.concatenate(rows(2), axis=1) - (receiving_side() * base.shape[0]).astype(F32)
+    lists[1:2] = jnp.concatenate(rows(4), axis=1)
+    hot_place[...] = hot(base.shape[1], jnp.concatenate(rows(3), axis=1).astype(jnp.int32))
+
+
+def second_kernel(beside, ready, late, hot_place, lists, front, total, out, *, parts):
+    base, slope, zeroth, first, second, grown = (ready[c] for c in range(6))
+    now = base + slope * beside[0]
     for k in range(SUBS):
         now, first, second, grown = substep(now, zeroth, first, second, late[k], grown)
     front[0] = now
     total[0] = grown
-    half = info.shape[0] // 2
-    rows = by_owner(info[pl.ds(half, half)], their_info[pl.ds(0, half)], parts)
-    for i, value in enumerate(plane_growth(grown, rows, parts)):
-        out[i : i + 1] = value
-    out[2 * parts :] = jnp.zeros((out.shape[0] - 2 * parts, out.shape[1]), F32)
+    stacked = jnp.concatenate(pieces(grown), axis=0)
+    found = picked_growth(stacked, hot_place[...], lists[0:1].astype(jnp.int32)) * lists[1:2]
+    places = now.shape[1]
+    for i in range(2 * parts):
+        out[i : i + 1] = found[:, i * places : (i + 1) * places]
+    out[2 * parts :] = jnp.zeros((out.shape[0] - 2 * parts, places), F32)
 
 
 def migrants_kernel(size, weight, cell, rows, count, out, *, places):
@@ -268,12 +302,16 @@
         out[at : block + half] = jnp.zeros((block + half - at, places), F32)
 
 
-def grown_at(stacked, line, place):
+def picked_growth(stacked, hot_place, line):
     lines = stacked.shape[0] // 2
-    picked = lax.dot_general(stacked, hot(stacked.shape[1], place), NN, preferred_element_type=F32)
+    picked = lax.dot_general(stacked, hot_place, NN, preferred_element_type=F32)
     picked = picked[:lines] + picked[lines:]
     index = lax.broadcasted_iota(jnp.int32, picked.shape, 0)
     return jnp.sum(jnp.where(index == line, picked, 0.0), axis=0, keepdims=True)
+
+
+def grown_at(stacked, line, place):
+    return picked_growth(stacked, hot(stacked.shape[1], place), line)
 
 
 def both_planes(mine, other):
@@ -342,10 +380,7 @@
     other = receives_other()
     field = jnp.where(other, their_front[0], front[0])
     beyond = jnp.where(other, front[0], their_front[0])
-    keep = 1.0 - inlet[0].astype(F32)
-    field = field + DIFFUSE * (beyond + moved(field) - 6.0 * field)
-    out[0] = keep * field + (1.0 - keep) * INLET
-    out[1] = jnp.where(has_beside(lax.axis_index("grp")), DIFFUSE * keep, 0.0)
+    out[0], out[1] = split_transport(field, beyond, inlet[0].astype(F32), lax.axis_index("grp"))
 
 
 def last_kernel(rest, received, relayed, field_out, arrivals_out, *, lines, parts):
@@ -413,9 +448,11 @@
     inputs += [nucleus_cell, nucleus_count, saturation, inlet_mask, migrant_rows, migrant_count]
     parcel_rows, events = inputs[0].shape[0], nucleus_cell.shape[1:]
     _, packed_rows = sections(parcel_rows, events[0] * events[1] // LANES, lines)
-    packed, size, weight, cell, event_cell, event_count, field, inlet, rows, count, active = call(
+    packed, size, weight, cell, event_cell, event_count, field, inlet, rows, count, active, counted = call(
         load_kernel,
-        [shape(packed_rows, LANES)] + [like(a) for a in inputs] + [shape(*inputs[0].shape)],
+        [shape(packed_rows, LANES)]
+        + [like(a) for a in inputs]
+        + [shape(*inputs[0].shape), shape(SUBS, lines, places)],
         *[hbm(a) for a in inputs],
         live_count,
         specs=[HBM] * 9 + [SMEM],
@@ -423,30 +460,38 @@
         name="load",
     )
     packed = swap(packed)
-    home = call(
-        home_kernel, shape(3 + SUBS, lines, places), size, weight, cell, event_cell, event_count,
+    home, counts = call(
+        home_kernel, (shape(3, lines, places), shape(SUBS, lines, places)),
+        size, weight, cell, event_cell, event_count, counted,
         cost=1 << 30, name="home",
     )
     front, state = call(
         functools.partial(front_kernel, parcel_rows=parcel_rows, events=events),
-        (shape(1, lines, places), shape(5, lines, places)), field, home, packed, name="front",
+        (shape(1, lines, places), shape(5, lines, places)), field, home, counts, packed, name="front",
     )
     beside = across(front, False)
     _, state = lax.optimization_barrier((front, state))
-    mine, late = call(
-        functools.partial(late_kernel, parcel_rows=parcel_rows), (shape(6, lines, places), shape(SUBS, lines, places)),
-        state, packed, event_cell, event_count, inlet, cost=1 << 28, name="late",
-    )
+    mine = call(pack_kernel, shape(6, lines, places), state, inlet, cost=1 << 28, name="pack")
     other = swap(mine)
     info = call(
         functools.partial(migrants_kernel, places=places), shape(32, places), size, weight, cell, rows, count,
         cost=1 << 33, name="migrants",
     )
     their_info = swap(info)
+    late = call(
+        functools.partial(late_kernel, parcel_rows=parcel_rows), shape(SUBS, lines, places),
+        packed, event_cell, event_count, cost=1 << 28, name="late",
+    )
+    info, late = lax.optimization_barrier((info, late))
+    ready, hot_place, lists = call(
+        functools.partial(ready_kernel, parts=parts),
+        (shape(6, lines, places), jax.ShapeDtypeStruct((places, 2 * slots), BF16), shape(8, 2 * slots)),
+        mine, other, info, their_info, cost=1 << 26, name="ready",
+    )
     front, total, given = call(
         functools.partial(second_kernel, parts=parts),
         (shape(1, lines, places), shape(1, lines, places), shape(8, places)),
-        beside, mine, other, late, info, their_info, name="second",
+        beside, ready, late, hot_place, lists, name="second",
     )
     theirs = swap(given)
     own = call(

time: 19.7 us -> 19.4 us (0.985)
  starting transfers between devices: 6.15 us -> 5.79 us
  Pallas kernels: 7.74 us -> 8.1 us
  waiting for transfers between devices: 4.18 us -> 3.91 us
    ppermute x7, waiting for transfers between devices: 3.55 us -> 3.11 us  [local(): swap = lambda value: lax.ppermute(value, 'grp', [(0, 1), (1, 0)])]
    pallas_call x11 -> x13, Pallas kernels: 7.74 us -> 8.1 us  [call(): pl.pallas_call(kernel, out_shape=out_shape, in_specs=specs or [VMEM] * le...]
    ppermute x7, starting transfers between devices: 2.03 us -> 1.69 us  [local(): swap = lambda value: lax.ppermute(value, 'grp', [(0, 1), (1, 0)])]
  transfers between devices with their start and end apart: 9 -> 9, of which waited for: 6 -> 6; matrix products, arithmetic and copies ran while one was open for 0% -> 0% of each run, Pallas kernels for 22% -> 23%
where the time goes in v6:
time: 19.4 us; the launch traced here: 19.2 us
  Pallas kernels  8.1 us (42%)
  starting transfers between devices  5.79 us (30%)
  waiting for transfers between devices  3.91 us (20%)
  between operations  1.37 us (7%)
    pallas_call x13, Pallas kernels, call(): pl.pallas_call(kernel, out_shape=out_shape, in_specs=specs or [VMEM] * le...  8.1 us
    ppermute x2, starting transfers between devices, local(): lax.ppermute(value, ('slab', 'grp'), across_pairs(slabs, second))  4.1 us
    ppermute x7, waiting for transfers between devices, local(): swap = lambda value: lax.ppermute(value, 'grp', [(0, 1), (1, 0)])  3.11 us
    ppermute x7, starting transfers between devices, local(): swap = lambda value: lax.ppermute(value, 'grp', [(0, 1), (1, 0)])  1.69 us
    ppermute x2, waiting for transfers between devices, local(): lax.ppermute(value, ('slab', 'grp'), across_pairs(slabs, second))  0.79 us
  transfers between devices with their start and end apart: 9, of which 6 were waited for; matrix products, arithmetic and copies ran while one was open for 0% of the time, Pallas kernels for 23%

profile of v6, /device:TPU:9, one launch (start us, length us, event | category | flops | bytes accessed | tf_op | source)
XLA Modules:
  0.0 19.2 jit_solution(14498807650232624823)
XLA Ops:
  1.3 1.4 %load.1 = (f32[256,128]{1,0:T(8,128)S(1)}, f32[32,128]{1,0:T(8,128)S(1)}, f32[32,128]{1,0:T(8,128)S(1)}, s32[32,128]{1,0:T(8,128)S(1)}, s32[1,4,512]{2,1,0:T(4,1...) custom-call(f32[32,128]{1,0:T(8,128)} %bitcast.4, ...), custom_call_target="tpu_custom_call" | custom-call | tf_op jit(solution)/shard_map/load/pallas_call | solution.py:414
  2.7 0.4 %collective-permute-start = (f32[256,128]{1,0:T(8,128)S(1)}, f32[256,128]{1,0:T(8,128)S(1)}, u32[]{:S(2)}, u32[]{:S(2)}) collective-permute-start(f32[256,128]{1,0:T(8,128)S(1)} %get-tuple-element.42), channel_id=1, source_target_pairs={{0,1},{1,0},{2,3},{3,2},{4,5},{5,4},{6,7},{7,6},{8,9},{9,8},{10,11... | collective-permute-start | bytes 393224 | tf_op jit(solution)/shard_map/ppermute | solution.py:441
  3.1 1.0 %home.1 = (f32[3,64,256]{2,1,0:T(8,128)S(1)}, f32[2,64,256]{2,1,0:T(8,128)S(1)}) custom-call(f32[32,128]{1,0:T(8,128)S(1)} %get-tuple-element.34.size, f32[32,128]{1,0:T(8,128)S(1)} %get-tuple-element.35.weight, s32[32,128]{1,0:T(8,128)S(1)} %get-tuple-element.36.cell, s32[1,4,512]{2,1,0:T(4,128)S(1)} %get-tuple-element.37.event_cell, ...), custom_call_target="tpu_custom_call" | custom-call | flops 1073741824 | tf_op jit(solution)/shard_map/home/pallas_call | solution.py:414
  4.1 0.0 collective-permute-done.packed
  4.1 1.2 %front.1 = (f32[1,64,256]{2,1,0:T(8,128)S(1)}, f32[5,64,256]{2,1,0:T(8,128)S(1)}) custom-call(f32[1,64,256]{2,1,0:T(8,128)S(1)} %get-tuple-element.33.field, f32[3,64,256]{2,1,0:T(8,128)S(1)} %get-tuple-element.40.home, f32[2,64,256]{2,1,0:T(8,128)S(1)} %get-tuple-element.41.home_counts, f32[256,128]{1,0:T(8,128)S(1)} %collective-permute-done.packed), custom_call_target="tpu_custom_call" | custom-call | tf_op jit(solution)/shard_map/front/pallas_call | solution.py:414
  5.4 2.1 %collective-permute-start.1 = (f32[1,64,256]{2,1,0:T(8,128)S(1)}, f32[1,64,256]{2,1,0:T(8,128)S(1)}, u32[]{:S(2)}, u32[]{:S(2)}) collective-permute-start(f32[1,64,256]{2,1,0:T(8,128)S(1)} %get-tuple-element.43), channel_id=1, source_target_pairs={{0,2},{3,5},{4,6},{7,9},{8,10},{11,13},{12,14},{15,17},{16,18},{19... | collective-permute-start | bytes 196616 | tf_op jit(solution)/shard_map/ppermute | solution.py:443
  7.5 0.1 collective-permute-start.2
  7.6 0.5 %migrants.1.info = f32[32,256]{1,0:T(8,128)S(1)} custom-call(f32[32,128]{1,0:T(8,128)S(1)} %get-tuple-element.34.size, f32[32,128]{1,0:T(8,128)S(1)} %get-tuple-element.35.weight, s32[32,128]{1,0:T(8,128)S(1)} %get-tuple-element.36.cell, s32[1,2,512]{2,1,0:T(2,128)S(1)} %get-tuple-element.46.rows, s32[1,2]{1,0:T(1,128)S(1)} %get-tuple-element.47.count), custom_call_target="tpu_custom_call" | custom-call | flops 8589934592 | tf_op jit(solution)/shard_map/migrants/pallas_call | solution.py:414
  8.1 0.6 %collective-permute-start.3 = (f32[32,256]{1,0:T(8,128)S(1)}, f32[32,256]{1,0:T(8,128)S(1)}, u32[]{:S(2)}, u32[]{:S(2)}) collective-permute-start(f32[32,256]{1,0:T(8,128)S(1)} %migrants.1.info), channel_id=1, source_target_pairs={{0,1},{1,0},{2,3},{3,2},{4,5},{5,4},{6,7},{7,6},{8,9},{9,8},{10,11... | collective-permute-start | bytes 98312 | tf_op jit(solution)/shard_map/ppermute | solution.py:441
  8.7 0.5 %late.1 = f32[2,64,256]{2,1,0:T(8,128)S(1)} custom-call(f32[256,128]{1,0:T(8,128)S(1)} %collective-permute-done.packed, s32[1,4,512]{2,1,0:T(4,128)S(1)} %get-tuple-element.37.event_cell, s32[1,4,512]{2,1,0:T(4,128)S(1)} %get-tuple-element.38.event_count), custom_call_target="tpu_custom_call" | custom-call | flops 268435456 | tf_op jit(solution)/shard_map/late/pallas_call | solution.py:414
  9.1 0.4 %collective-permute-done.3.their_info = f32[32,256]{1,0:T(8,128)S(1)} collective-permute-done((f32[32,256]{1,0:T(8,128)S(1)}, f32[32,256]{1,0:T(8,128)S(1)}, u32[]{:S(2)}, u32[]{:S(2)}) %collective-permute-start.3) | collective-permute-done | bytes 32800 | tf_op jit(solution)/shard_map/ppermute | solution.py:441
  9.5 0.0 collective-permute-done.2.other
  9.5 0.3 %ready.1 = (f32[6,64,256]{2,1,0:T(8,128)S(1)}, bf16[256,1024]{1,0:T(8,128)(2,1)S(1)}, f32[8,1024]{1,0:T(8,128)S(1)}) custom-call(f32[6,64,256]{2,1,0:T(8,128)S(1)} %pack.1.mine, f32[6,64,256]{2,1,0:T(8,128)S(1)} %collective-permute-done.2.other, f32[32,256]{1,0:T(8,128)S(1)} %migrants.1.info, f32[32,256]{1,0:T(8,128)S(1)} %collective-permute-done.3.their_info), custom_call_target="tpu_custom_call" | custom-call | flops 67108864 | tf_op jit(solution)/shard_map/ready/pallas_call | solution.py:414
  9.9 0.6 %collective-permute-done.1.beside = f32[1,64,256]{2,1,0:T(8,128)S(1)} collective-permute-done((f32[1,64,256]{2,1,0:T(8,128)S(1)}, f32[1,64,256]{2,1,0:T(8,128)S(1)}, u32[]{:S(2)}, u32[]{:S(2)}) %collective-permute-start.1) | collective-permute-done | bytes 65568 | tf_op jit(solution)/shard_map/ppermute | solution.py:443
  10.5 0.4 %second.1 = (f32[1,64,256]{2,1,0:T(8,128)S(1)}, f32[1,64,256]{2,1,0:T(8,128)S(1)}, f32[8,256]{1,0:T(8,128)S(1)}) custom-call(f32[1,64,256]{2,1,0:T(8,128)S(1)} %collective-permute-done.1.beside, f32[6,64,256]{2,1,0:T(8,128)S(1)} %get-tuple-element.49.ready, f32[2,64,256]{2,1,0:T(8,128)S(1)} %late.1, bf16[256,1024]{1,0:T(8,128)(2,1)S(1)} %get-tuple-element.51.hot_place, ...), custom_call_target="tpu_custom_call" | custom-call | tf_op jit(solution)/shard_map/second/pallas_call | solution.py:414
  10.8 0.1 collective-permute-start.5
  11.0 0.3 %own.1 = f32[8,256]{1,0:T(8,128)S(1)} custom-call(f32[1,64,256]{2,1,0:T(8,128)S(1)} %get-tuple-element.56.total, f32[32,256]{1,0:T(8,128)S(1)} %migrants.1.info, f32[32,256]{1,0:T(8,128)S(1)} %collective-permute-done.3.their_info), custom_call_target="tpu_custom_call" | custom-call | flops 268435456 | tf_op jit(solution)/shard_map/own/pallas_call | solution.py:414
  11.2 0.8 %collective-permute-done.5.theirs = f32[8,256]{1,0:T(8,128)S(1)} collective-permute-done((f32[8,256]{1,0:T(8,128)S(1)}, f32[8,256]{1,0:T(8,128)S(1)}, u32[]{:S(2)}, u32[]{:S(2)}) %collective-permute-start.5) | collective-permute-done | bytes 8224 | tf_op jit(solution)/shard_map/ppermute | solution.py:441
  12.1 2.0 %collective-permute-start.6 = (f32[72,256]{1,0:T(8,128)S(1)}, f32[72,256]{1,0:T(8,128)S(1)}, u32[]{:S(2)}, u32[]{:S(2)}) collective-permute-start(f32[72,256]{1,0:T(8,128)S(1)} %leaving.1), channel_id=1, source_target_pairs={{1,2},{3,5},{4,6},{7,9},{8,10},{11,13},{12,14},{15,17},{16,18},{19... | collective-permute-start | bytes 221192 | tf_op jit(solution)/shard_map/ppermute | solution.py:443
  14.1 0.0 collective-permute-start.7
  14.1 0.5 %collective-permute-start.4 = (f32[1,64,256]{2,1,0:T(8,128)S(1)}, f32[1,64,256]{2,1,0:T(8,128)S(1)}, u32[]{:S(2)}, u32[]{:S(2)}) collective-permute-start(f32[1,64,256]{2,1,0:T(8,128)S(1)} %get-tuple-element.53.front), channel_id=1, source_target_pairs={{0,1},{1,0},{2,3},{3,2},{4,5},{5,4},{6,7},{7,6},{8,9},{9,8},{10,11... | collective-permute-start | bytes 196616 | tf_op jit(solution)/shard_map/ppermute | solution.py:441
  14.6 0.7 %collective-permute-done.7.their_total = f32[1,64,256]{2,1,0:T(8,128)S(1)} collective-permute-done((f32[1,64,256]{2,1,0:T(8,128)S(1)}, f32[1,64,256]{2,1,0:T(8,128)S(1)}, u32[]{:S(2)}, u32[]{:S(2)}) %collective-permute-start.7) | collective-permute-done | bytes 65568 | tf_op jit(solution)/shard_map/ppermute | solution.py:441
  15.3 1.7 %sizes.1 = f32[32,128]{1,0:T(8,128)} custom-call(f32[1,64,256]{2,1,0:T(8,128)S(1)} %get-tuple-element.56.total, f32[1,64,256]{2,1,0:T(8,128)S(1)} %collective-permute-done.7.their_total, f32[32,128]{1,0:T(8,128)S(1)} %get-tuple-element.34.size, s32[32,128]{1,0:T(8,128)S(1)} %get-tuple-element.36.cell, f32[32,128]{1,0:T(8,128)S(1)} %get-tuple-element.57.active), custom_call_target="tpu_custom_call" | custom-call | flops 67108864 | tf_op jit(solution)/shard_map/sizes/pallas_call | solution.py:414
  17.1 0.2 collective-permute-done.6.received
  17.2 0.0 collective-permute-start.8
  17.2 0.0 collective-permute-done.4.their_front
  17.2 0.1 rest.1
  17.4 1.1 %collective-permute-done.8.relayed = f32[72,256]{1,0:T(8,128)S(1)} collective-permute-done((f32[72,256]{1,0:T(8,128)S(1)}, f32[72,256]{1,0:T(8,128)S(1)}, u32[]{:S(2)}, u32[]{:S(2)}) %collective-permute-start.8) | collective-permute-done | bytes 73760 | tf_op jit(solution)/shard_map/ppermute | solution.py:441
  18.5 0.7 %last.1 = (f32[1,64,256]{2,1,0:T(8,128)}, f32[1,2,2,512]{3,2,1,0:T(2,128)}) custom-call(f32[2,64,256]{2,1,0:T(8,128)S(1)} %rest.1, f32[72,256]{1,0:T(8,128)S(1)} %collective-permute-done.6.received, f32[72,256]{1,0:T(8,128)S(1)} %collective-permute-done.8.relayed), custom_call_target="tpu_custom_call" | custom-call | tf_op jit(solution)/shard_map/last/pallas_call | solution.py:414
  (2 shorter events, 0.0 us)
Async XLA Ops:
  2.7 1.5 %collective-permute-start = (f32[256,128]{1,0:T(8,128)S(1)}, f32[256,128]{1,0:T(8,128)S(1)}, u32[]{:S(2)}, u32[]{:S(2)}) collective-permute-start(f32[256,128]{1,0:T(8,128)S(1)} %get-tuple-element.42), channel_id=1, source_target_pairs={{0,1},{1,0},{2,3},{3,2},{4,5},{5,4},{6,7},{7,6},{8,9},{9,8},{10,11... | collective-permute-start | bytes 393224 | tf_op jit(solution)/shard_map/ppermute | solution.py:441
  5.4 5.1 %collective-permute-start.1 = (f32[1,64,256]{2,1,0:T(8,128)S(1)}, f32[1,64,256]{2,1,0:T(8,128)S(1)}, u32[]{:S(2)}, u32[]{:S(2)}) collective-permute-start(f32[1,64,256]{2,1,0:T(8,128)S(1)} %get-tuple-element.43), channel_id=1, source_target_pairs={{0,2},{3,5},{4,6},{7,9},{8,10},{11,13},{12,14},{15,17},{16,18},{19... | collective-permute-start | bytes 196616 | tf_op jit(solution)/shard_map/ppermute | solution.py:443
  7.5 2.0 %collective-permute-start.2 = (f32[6,64,256]{2,1,0:T(8,128)S(1)}, f32[6,64,256]{2,1,0:T(8,128)S(1)}, u32[]{:S(2)}, u32[]{:S(2)}) collective-permute-start(f32[6,64,256]{2,1,0:T(8,128)S(1)} %pack.1.mine), channel_id=1, source_target_pairs={{0,1},{1,0},{2,3},{3,2},{4,5},{5,4},{6,7},{7,6},{8,9},{9,8},{10,11... | collective-permute-start | bytes 1179656 | tf_op jit(solution)/shard_map/ppermute | solution.py:441
  8.1 1.4 %collective-permute-start.3 = (f32[32,256]{1,0:T(8,128)S(1)}, f32[32,256]{1,0:T(8,128)S(1)}, u32[]{:S(2)}, u32[]{:S(2)}) collective-permute-start(f32[32,256]{1,0:T(8,128)S(1)} %migrants.1.info), channel_id=1, source_target_pairs={{0,1},{1,0},{2,3},{3,2},{4,5},{5,4},{6,7},{7,6},{8,9},{9,8},{10,11... | collective-permute-start | bytes 98312 | tf_op jit(solution)/shard_map/ppermute | solution.py:441
  10.8 1.2 %collective-permute-start.5 = (f32[8,256]{1,0:T(8,128)S(1)}, f32[8,256]{1,0:T(8,128)S(1)}, u32[]{:S(2)}, u32[]{:S(2)}) collective-permute-start(f32[8,256]{1,0:T(8,128)S(1)} %get-tuple-element.55), channel_id=1, source_target_pairs={{0,1},{1,0},{2,3},{3,2},{4,5},{5,4},{6,7},{7,6},{8,9},{9,8},{10,11... | collective-permute-start | bytes 24584 | tf_op jit(solution)/shard_map/ppermute | solution.py:441
  12.1 5.2 %collective-permute-start.6 = (f32[72,256]{1,0:T(8,128)S(1)}, f32[72,256]{1,0:T(8,128)S(1)}, u32[]{:S(2)}, u32[]{:S(2)}) collective-permute-start(f32[72,256]{1,0:T(8,128)S(1)} %leaving.1), channel_id=1, source_target_pairs={{1,2},{3,5},{4,6},{7,9},{8,10},{11,13},{12,14},{15,17},{16,18},{19... | collective-permute-start | bytes 221192 | tf_op jit(solution)/shard_map/ppermute | solution.py:443
  14.1 1.3 %collective-permute-start.7 = (f32[1,64,256]{2,1,0:T(8,128)S(1)}, f32[1,64,256]{2,1,0:T(8,128)S(1)}, u32[]{:S(2)}, u32[]{:S(2)}) collective-permute-start(f32[1,64,256]{2,1,0:T(8,128)S(1)} %get-tuple-element.56.total), channel_id=1, source_target_pairs={{0,1},{1,0},{2,3},{3,2},{4,5},{5,4},{6,7},{7,6},{8,9},{9,8},{10,11... | collective-permute-start | bytes 196616 | tf_op jit(solution)/shard_map/ppermute | solution.py:441
  14.1 3.2 %collective-permute-start.4 = (f32[1,64,256]{2,1,0:T(8,128)S(1)}, f32[1,64,256]{2,1,0:T(8,128)S(1)}, u32[]{:S(2)}, u32[]{:S(2)}) collective-permute-start(f32[1,64,256]{2,1,0:T(8,128)S(1)} %get-tuple-element.53.front), channel_id=1, source_target_pairs={{0,1},{1,0},{2,3},{3,2},{4,5},{5,4},{6,7},{7,6},{8,9},{9,8},{10,11... | collective-permute-start | bytes 196616 | tf_op jit(solution)/shard_map/ppermute | solution.py:441
  17.2 1.3 %collective-permute-start.8 = (f32[72,256]{1,0:T(8,128)S(1)}, f32[72,256]{1,0:T(8,128)S(1)}, u32[]{:S(2)}, u32[]{:S(2)}) collective-permute-start(f32[72,256]{1,0:T(8,128)S(1)} %collective-permute-done.6.received), channel_id=1, source_target_pairs={{0,1},{1,0},{2,3},{3,2},{4,5},{5,4},{6,7},{7,6},{8,9},{9,8},{10,11... | collective-permute-start | bytes 221192 | tf_op jit(solution)/shard_map/ppermute | solution.py:441

commit v7 on v6

--- a/solution.py
+++ b/solution.py
@@ -252,16 +252,19 @@
     hot_place[...] = hot(base.shape[1], jnp.concatenate(rows(3), axis=1).astype(jnp.int32))
 
 
-def second_kernel(beside, ready, late, hot_place, lists, front, total, out, *, parts):
+def second_substeps(beside, ready, late):
     base, slope, zeroth, first, second, grown = (ready[c] for c in range(6))
     now = base + slope * beside[0]
     for k in range(SUBS):
         now, first, second, grown = substep(now, zeroth, first, second, late[k], grown)
-    front[0] = now
-    total[0] = grown
+    return now, grown
+
+
+def second_kernel(beside, ready, late, hot_place, lists, out, *, parts):
+    _, grown = second_substeps(beside, ready, late)
     stacked = jnp.concatenate(pieces(grown), axis=0)
     found = picked_growth(stacked, hot_place[...], lists[0:1].astype(jnp.int32)) * lists[1:2]
-    places = now.shape[1]
+    places = grown.shape[1]
     for i in range(2 * parts):
         out[i : i + 1] = found[:, i * places : (i + 1) * places]
     out[2 * parts :] = jnp.zeros((out.shape[0] - 2 * parts, places), F32)
@@ -336,7 +339,8 @@
     return [found[:, i * places : (i + 1) * places] * valid[i] for i in range(2 * parts)]
 
 
-def own_kernel(total, info, their_info, out, *, parts):
+def own_kernel(beside, ready, late, info, their_info, out, front, total, *, parts):
+    front[0], total[0] = second_substeps(beside, ready, late)
     half = info.shape[0] // 2
     rows = by_owner(info[pl.ds(0, half)], their_info[pl.ds(half, half)], parts)
     found = plane_growth(total[0], rows, parts)
@@ -488,15 +492,15 @@
         (shape(6, lines, places), jax.ShapeDtypeStruct((places, 2 * slots), BF16), shape(8, 2 * slots)),
         mine, other, info, their_info, cost=1 << 26, name="ready",
     )
-    front, total, given = call(
-        functools.partial(second_kernel, parts=parts),
-        (shape(1, lines, places), shape(1, lines, places), shape(8, places)),
-        beside, ready, late, hot_place, lists, name="second",
+    given = call(
+        functools.partial(second_kernel, parts=parts), shape(8, places), beside, ready, late, hot_place, lists,
+        name="second",
     )
     theirs = swap(given)
-    own = call(
-        functools.partial(own_kernel, parts=parts), shape(4 * parts, places), total, info, their_info,
-        cost=1 << 28, name="own",
+    own, front, total = call(
+        functools.partial(own_kernel, parts=parts),
+        (shape(4 * parts, places), shape(1, lines, places), shape(1, lines, places)),
+        beside, ready, late, info, their_info, cost=1 << 28, name="own",
     )
     leaving = call(
         functools.partial(leaving_kernel, parts=parts), shape(lines + 4 * parts, places), front, own, theirs, name="leaving"

time: 19.4 us -> 19.4 us (level)
  transfers between devices with their start and end apart: 9 -> 9, of which waited for: 6 -> 6; matrix products, arithmetic and copies ran while one was open for 0% -> 0% of each run, Pallas kernels for 23% -> 24%
where the time goes in v7:
time: 19.4 us; the launch traced here: 19.1 us
  Pallas kernels  8.2 us (42%)
  starting transfers between devices  5.8 us (30%)
  waiting for transfers between devices  3.75 us (19%)
  between operations  1.37 us (7%)
    pallas_call x13, Pallas kernels, call(): pl.pallas_call(kernel, out_shape=out_shape, in_specs=specs or [VMEM] * le...  8.2 us
    ppermute x2, starting transfers between devices, local(): lax.ppermute(value, ('slab', 'grp'), across_pairs(slabs, second))  4.1 us
    ppermute x7, waiting for transfers between devices, local(): swap = lambda value: lax.ppermute(value, 'grp', [(0, 1), (1, 0)])  2.97 us
    ppermute x7, starting transfers between devices, local(): swap = lambda value: lax.ppermute(value, 'grp', [(0, 1), (1, 0)])  1.7 us
    ppermute x2, waiting for transfers between devices, local(): lax.ppermute(value, ('slab', 'grp'), across_pairs(slabs, second))  0.79 us
  transfers between devices with their start and end apart: 9, of which 6 were waited for; matrix products, arithmetic and copies ran while one was open for 0% of the time, Pallas kernels for 24%

profile of v7, /device:TPU:9, one launch (start us, length us, event | category | flops | bytes accessed | tf_op | source)
XLA Modules:
  0.0 19.1 jit_solution(12281929152439179246)
XLA Ops:
  1.3 1.4 %load.1 = (f32[256,128]{1,0:T(8,128)S(1)}, f32[32,128]{1,0:T(8,128)S(1)}, f32[32,128]{1,0:T(8,128)S(1)}, s32[32,128]{1,0:T(8,128)S(1)}, s32[1,4,512]{2,1,0:T(4,1...) custom-call(f32[32,128]{1,0:T(8,128)} %bitcast.4, ...), custom_call_target="tpu_custom_call" | custom-call | tf_op jit(solution)/shard_map/load/pallas_call | solution.py:418
  2.7 0.4 %collective-permute-start = (f32[256,128]{1,0:T(8,128)S(1)}, f32[256,128]{1,0:T(8,128)S(1)}, u32[]{:S(2)}, u32[]{:S(2)}) collective-permute-start(f32[256,128]{1,0:T(8,128)S(1)} %get-tuple-element.42), channel_id=1, source_target_pairs={{0,1},{1,0},{2,3},{3,2},{4,5},{5,4},{6,7},{7,6},{8,9},{9,8},{10,11... | collective-permute-start | bytes 393224 | tf_op jit(solution)/shard_map/ppermute | solution.py:445
  3.1 1.0 %home.1 = (f32[3,64,256]{2,1,0:T(8,128)S(1)}, f32[2,64,256]{2,1,0:T(8,128)S(1)}) custom-call(f32[32,128]{1,0:T(8,128)S(1)} %get-tuple-element.34.size, f32[32,128]{1,0:T(8,128)S(1)} %get-tuple-element.35.weight, s32[32,128]{1,0:T(8,128)S(1)} %get-tuple-element.36.cell, s32[1,4,512]{2,1,0:T(4,128)S(1)} %get-tuple-element.37.event_cell, ...), custom_call_target="tpu_custom_call" | custom-call | flops 1073741824 | tf_op jit(solution)/shard_map/home/pallas_call | solution.py:418
  4.1 0.0 collective-permute-done.packed
  4.1 1.2 %front.1 = (f32[1,64,256]{2,1,0:T(8,128)S(1)}, f32[5,64,256]{2,1,0:T(8,128)S(1)}) custom-call(f32[1,64,256]{2,1,0:T(8,128)S(1)} %get-tuple-element.33.field, f32[3,64,256]{2,1,0:T(8,128)S(1)} %get-tuple-element.40.home, f32[2,64,256]{2,1,0:T(8,128)S(1)} %get-tuple-element.41.home_counts, f32[256,128]{1,0:T(8,128)S(1)} %collective-permute-done.packed), custom_call_target="tpu_custom_call" | custom-call | tf_op jit(solution)/shard_map/front/pallas_call | solution.py:418
  5.4 2.1 %collective-permute-start.1 = (f32[1,64,256]{2,1,0:T(8,128)S(1)}, f32[1,64,256]{2,1,0:T(8,128)S(1)}, u32[]{:S(2)}, u32[]{:S(2)}) collective-permute-start(f32[1,64,256]{2,1,0:T(8,128)S(1)} %get-tuple-element.43), channel_id=1, source_target_pairs={{0,2},{3,5},{4,6},{7,9},{8,10},{11,13},{12,14},{15,17},{16,18},{19... | collective-permute-start | bytes 196616 | tf_op jit(solution)/shard_map/ppermute | solution.py:447
  7.5 0.1 collective-permute-start.2
  7.6 0.5 %migrants.1.info = f32[32,256]{1,0:T(8,128)S(1)} custom-call(f32[32,128]{1,0:T(8,128)S(1)} %get-tuple-element.34.size, f32[32,128]{1,0:T(8,128)S(1)} %get-tuple-element.35.weight, s32[32,128]{1,0:T(8,128)S(1)} %get-tuple-element.36.cell, s32[1,2,512]{2,1,0:T(2,128)S(1)} %get-tuple-element.46.rows, s32[1,2]{1,0:T(1,128)S(1)} %get-tuple-element.47.count), custom_call_target="tpu_custom_call" | custom-call | flops 8589934592 | tf_op jit(solution)/shard_map/migrants/pallas_call | solution.py:418
  8.1 0.6 %collective-permute-start.3 = (f32[32,256]{1,0:T(8,128)S(1)}, f32[32,256]{1,0:T(8,128)S(1)}, u32[]{:S(2)}, u32[]{:S(2)}) collective-permute-start(f32[32,256]{1,0:T(8,128)S(1)} %migrants.1.info), channel_id=1, source_target_pairs={{0,1},{1,0},{2,3},{3,2},{4,5},{5,4},{6,7},{7,6},{8,9},{9,8},{10,11... | collective-permute-start | bytes 98312 | tf_op jit(solution)/shard_map/ppermute | solution.py:445
  8.7 0.5 %late.1 = f32[2,64,256]{2,1,0:T(8,128)S(1)} custom-call(f32[256,128]{1,0:T(8,128)S(1)} %collective-permute-done.packed, s32[1,4,512]{2,1,0:T(4,128)S(1)} %get-tuple-element.37.event_cell, s32[1,4,512]{2,1,0:T(4,128)S(1)} %get-tuple-element.38.event_count), custom_call_target="tpu_custom_call" | custom-call | flops 268435456 | tf_op jit(solution)/shard_map/late/pallas_call | solution.py:418
  9.1 0.4 %collective-permute-done.3.their_info = f32[32,256]{1,0:T(8,128)S(1)} collective-permute-done((f32[32,256]{1,0:T(8,128)S(1)}, f32[32,256]{1,0:T(8,128)S(1)}, u32[]{:S(2)}, u32[]{:S(2)}) %collective-permute-start.3) | collective-permute-done | bytes 32800 | tf_op jit(solution)/shard_map/ppermute | solution.py:445
  9.5 0.0 collective-permute-done.2.other
  9.5 0.3 %ready.1 = (f32[6,64,256]{2,1,0:T(8,128)S(1)}, bf16[256,1024]{1,0:T(8,128)(2,1)S(1)}, f32[8,1024]{1,0:T(8,128)S(1)}) custom-call(f32[6,64,256]{2,1,0:T(8,128)S(1)} %pack.1.mine, f32[6,64,256]{2,1,0:T(8,128)S(1)} %collective-permute-done.2.other, f32[32,256]{1,0:T(8,128)S(1)} %migrants.1.info, f32[32,256]{1,0:T(8,128)S(1)} %collective-permute-done.3.their_info), custom_call_target="tpu_custom_call" | custom-call | flops 67108864 | tf_op jit(solution)/shard_map/ready/pallas_call | solution.py:418
  9.9 0.6 %collective-permute-done.1.beside = f32[1,64,256]{2,1,0:T(8,128)S(1)} collective-permute-done((f32[1,64,256]{2,1,0:T(8,128)S(1)}, f32[1,64,256]{2,1,0:T(8,128)S(1)}, u32[]{:S(2)}, u32[]{:S(2)}) %collective-permute-start.1) | collective-permute-done | bytes 65568 | tf_op jit(solution)/shard_map/ppermute | solution.py:447
  10.5 0.3 %second.1 = f32[8,256]{1,0:T(8,128)S(1)} custom-call(f32[1,64,256]{2,1,0:T(8,128)S(1)} %collective-permute-done.1.beside, f32[6,64,256]{2,1,0:T(8,128)S(1)} %get-tuple-element.49.ready, f32[2,64,256]{2,1,0:T(8,128)S(1)} %late.1, bf16[256,1024]{1,0:T(8,128)(2,1)S(1)} %get-tuple-element.53.hot_place, f32[8,1024]{1,0:T(8,128)S(1)} %get-tuple-element.54.lists), custom_call_target="tpu_custom_call" | custom-call | tf_op jit(solution)/shard_map/second/pallas_call | solution.py:418
  10.8 0.1 collective-permute-start.5
  10.9 0.4 %own.1 = (f32[8,256]{1,0:T(8,128)S(1)}, f32[1,64,256]{2,1,0:T(8,128)S(1)}, f32[1,64,256]{2,1,0:T(8,128)S(1)}) custom-call(f32[1,64,256]{2,1,0:T(8,128)S(1)} %collective-permute-done.1.beside, f32[6,64,256]{2,1,0:T(8,128)S(1)} %get-tuple-element.49.ready, f32[2,64,256]{2,1,0:T(8,128)S(1)} %late.1, f32[32,256]{1,0:T(8,128)S(1)} %migrants.1.info, ...), custom_call_target="tpu_custom_call" | custom-call | flops 268435456 | tf_op jit(solution)/shard_map/own/pallas_call | solution.py:418
  11.3 0.7 %collective-permute-done.5.theirs = f32[8,256]{1,0:T(8,128)S(1)} collective-permute-done((f32[8,256]{1,0:T(8,128)S(1)}, f32[8,256]{1,0:T(8,128)S(1)}, u32[]{:S(2)}, u32[]{:S(2)}) %collective-permute-start.5) | collective-permute-done | bytes 8224 | tf_op jit(solution)/shard_map/ppermute | solution.py:445
  12.0 2.0 %collective-permute-start.6 = (f32[72,256]{1,0:T(8,128)S(1)}, f32[72,256]{1,0:T(8,128)S(1)}, u32[]{:S(2)}, u32[]{:S(2)}) collective-permute-start(f32[72,256]{1,0:T(8,128)S(1)} %leaving.1), channel_id=1, source_target_pairs={{1,2},{3,5},{4,6},{7,9},{8,10},{11,13},{12,14},{15,17},{16,18},{19... | collective-permute-start | bytes 221192 | tf_op jit(solution)/shard_map/ppermute | solution.py:447
  14.0 0.0 collective-permute-start.7
  14.0 0.5 %collective-permute-start.4 = (f32[1,64,256]{2,1,0:T(8,128)S(1)}, f32[1,64,256]{2,1,0:T(8,128)S(1)}, u32[]{:S(2)}, u32[]{:S(2)}) collective-permute-start(f32[1,64,256]{2,1,0:T(8,128)S(1)} %get-tuple-element.51.front), channel_id=1, source_target_pairs={{0,1},{1,0},{2,3},{3,2},{4,5},{5,4},{6,7},{7,6},{8,9},{9,8},{10,11... | collective-permute-start | bytes 196616 | tf_op jit(solution)/shard_map/ppermute | solution.py:445
  14.5 0.7 %collective-permute-done.7.their_total = f32[1,64,256]{2,1,0:T(8,128)S(1)} collective-permute-done((f32[1,64,256]{2,1,0:T(8,128)S(1)}, f32[1,64,256]{2,1,0:T(8,128)S(1)}, u32[]{:S(2)}, u32[]{:S(2)}) %collective-permute-start.7) | collective-permute-done | bytes 65568 | tf_op jit(solution)/shard_map/ppermute | solution.py:445
  15.3 1.7 %sizes.1 = f32[32,128]{1,0:T(8,128)} custom-call(f32[1,64,256]{2,1,0:T(8,128)S(1)} %get-tuple-element.56.total, f32[1,64,256]{2,1,0:T(8,128)S(1)} %collective-permute-done.7.their_total, f32[32,128]{1,0:T(8,128)S(1)} %get-tuple-element.34.size, s32[32,128]{1,0:T(8,128)S(1)} %get-tuple-element.36.cell, f32[32,128]{1,0:T(8,128)S(1)} %get-tuple-element.57.active), custom_call_target="tpu_custom_call" | custom-call | flops 67108864 | tf_op jit(solution)/shard_map/sizes/pallas_call | solution.py:418
  17.0 0.2 collective-permute-done.6.received
  17.2 0.0 collective-permute-start.8
  17.2 0.0 collective-permute-done.4.their_front
  17.2 0.1 rest.1
  17.3 1.1 %collective-permute-done.8.relayed = f32[72,256]{1,0:T(8,128)S(1)} collective-permute-done((f32[72,256]{1,0:T(8,128)S(1)}, f32[72,256]{1,0:T(8,128)S(1)}, u32[]{:S(2)}, u32[]{:S(2)}) %collective-permute-start.8) | collective-permute-done | bytes 73760 | tf_op jit(solution)/shard_map/ppermute | solution.py:445
  18.5 0.7 %last.1 = (f32[1,64,256]{2,1,0:T(8,128)}, f32[1,2,2,512]{3,2,1,0:T(2,128)}) custom-call(f32[2,64,256]{2,1,0:T(8,128)S(1)} %rest.1, f32[72,256]{1,0:T(8,128)S(1)} %collective-permute-done.6.received, f32[72,256]{1,0:T(8,128)S(1)} %collective-permute-done.8.relayed), custom_call_target="tpu_custom_call" | custom-call | tf_op jit(solution)/shard_map/last/pallas_call | solution.py:418
  (2 shorter events, 0.0 us)
Async XLA Ops:
  2.7 1.5 %collective-permute-start = (f32[256,128]{1,0:T(8,128)S(1)}, f32[256,128]{1,0:T(8,128)S(1)}, u32[]{:S(2)}, u32[]{:S(2)}) collective-permute-start(f32[256,128]{1,0:T(8,128)S(1)} %get-tuple-element.42), channel_id=1, source_target_pairs={{0,1},{1,0},{2,3},{3,2},{4,5},{5,4},{6,7},{7,6},{8,9},{9,8},{10,11... | collective-permute-start | bytes 393224 | tf_op jit(solution)/shard_map/ppermute | solution.py:445
  5.4 5.1 %collective-permute-start.1 = (f32[1,64,256]{2,1,0:T(8,128)S(1)}, f32[1,64,256]{2,1,0:T(8,128)S(1)}, u32[]{:S(2)}, u32[]{:S(2)}) collective-permute-start(f32[1,64,256]{2,1,0:T(8,128)S(1)} %get-tuple-element.43), channel_id=1, source_target_pairs={{0,2},{3,5},{4,6},{7,9},{8,10},{11,13},{12,14},{15,17},{16,18},{19... | collective-permute-start | bytes 196616 | tf_op jit(solution)/shard_map/ppermute | solution.py:447
  7.5 2.0 %collective-permute-start.2 = (f32[6,64,256]{2,1,0:T(8,128)S(1)}, f32[6,64,256]{2,1,0:T(8,128)S(1)}, u32[]{:S(2)}, u32[]{:S(2)}) collective-permute-start(f32[6,64,256]{2,1,0:T(8,128)S(1)} %pack.1.mine), channel_id=1, source_target_pairs={{0,1},{1,0},{2,3},{3,2},{4,5},{5,4},{6,7},{7,6},{8,9},{9,8},{10,11... | collective-permute-start | bytes 1179656 | tf_op jit(solution)/shard_map/ppermute | solution.py:445
  8.1 1.4 %collective-permute-start.3 = (f32[32,256]{1,0:T(8,128)S(1)}, f32[32,256]{1,0:T(8,128)S(1)}, u32[]{:S(2)}, u32[]{:S(2)}) collective-permute-start(f32[32,256]{1,0:T(8,128)S(1)} %migrants.1.info), channel_id=1, source_target_pairs={{0,1},{1,0},{2,3},{3,2},{4,5},{5,4},{6,7},{7,6},{8,9},{9,8},{10,11... | collective-permute-start | bytes 98312 | tf_op jit(solution)/shard_map/ppermute | solution.py:445
  10.8 1.2 %collective-permute-start.5 = (f32[8,256]{1,0:T(8,128)S(1)}, f32[8,256]{1,0:T(8,128)S(1)}, u32[]{:S(2)}, u32[]{:S(2)}) collective-permute-start(f32[8,256]{1,0:T(8,128)S(1)} %second.1), channel_id=1, source_target_pairs={{0,1},{1,0},{2,3},{3,2},{4,5},{5,4},{6,7},{7,6},{8,9},{9,8},{10,11... | collective-permute-start | bytes 24584 | tf_op jit(solution)/shard_map/ppermute | solution.py:445
  12.0 5.2 %collective-permute-start.6 = (f32[72,256]{1,0:T(8,128)S(1)}, f32[72,256]{1,0:T(8,128)S(1)}, u32[]{:S(2)}, u32[]{:S(2)}) collective-permute-start(f32[72,256]{1,0:T(8,128)S(1)} %leaving.1), channel_id=1, source_target_pairs={{1,2},{3,5},{4,6},{7,9},{8,10},{11,13},{12,14},{15,17},{16,18},{19... | collective-permute-start | bytes 221192 | tf_op jit(solution)/shard_map/ppermute | solution.py:447
  14.0 1.3 %collective-permute-start.7 = (f32[1,64,256]{2,1,0:T(8,128)S(1)}, f32[1,64,256]{2,1,0:T(8,128)S(1)}, u32[]{:S(2)}, u32[]{:S(2)}) collective-permute-start(f32[1,64,256]{2,1,0:T(8,128)S(1)} %get-tuple-element.56.total), channel_id=1, source_target_pairs={{0,1},{1,0},{2,3},{3,2},{4,5},{5,4},{6,7},{7,6},{8,9},{9,8},{10,11... | collective-permute-start | bytes 196616 | tf_op jit(solution)/shard_map/ppermute | solution.py:445
  14.0 3.2 %collective-permute-start.4 = (f32[1,64,256]{2,1,0:T(8,128)S(1)}, f32[1,64,256]{2,1,0:T(8,128)S(1)}, u32[]{:S(2)}, u32[]{:S(2)}) collective-permute-start(f32[1,64,256]{2,1,0:T(8,128)S(1)} %get-tuple-element.51.front), channel_id=1, source_target_pairs={{0,1},{1,0},{2,3},{3,2},{4,5},{5,4},{6,7},{7,6},{8,9},{9,8},{10,11... | collective-permute-start | bytes 196616 | tf_op jit(solution)/shard_map/ppermute | solution.py:445
  17.2 1.3 %collective-permute-start.8 = (f32[72,256]{1,0:T(8,128)S(1)}, f32[72,256]{1,0:T(8,128)S(1)}, u32[]{:S(2)}, u32[]{:S(2)}) collective-permute-start(f32[72,256]{1,0:T(8,128)S(1)} %collective-permute-done.6.received), channel_id=1, source_target_pairs={{0,1},{1,0},{2,3},{3,2},{4,5},{5,4},{6,7},{7,6},{8,9},{9,8},{10,11... | collective-permute-start | bytes 221192 | tf_op jit(solution)/shard_map/ppermute | solution.py:445

commit v8 on v7

--- a/solution.py
+++ b/solution.py
@@ -130,7 +130,7 @@
 
 
 def load_kernel(*refs):
-    inputs, live, out, kept, active, counts, sems = refs[:9], refs[9], refs[10], refs[11:20], *refs[20:]
+    inputs, live, out, kept, active, counts, sems = refs[:6], refs[6], refs[7], refs[8:14], *refs[14:]
     copies = [pltpu.make_async_copy(src, dst, sems.at[i]) for i, (src, dst) in enumerate(zip(inputs, kept))]
     for copy in copies:
         copy.start()
@@ -158,7 +158,11 @@
         own_counts(event_cell, event_count, counts)
 
 
-def home_kernel(size, weight, cell, event_cell, event_count, counted, out, counts):
+def home_kernel(size, weight, cell, event_cell, event_count, counted, inlet, rows, count, out, counts, *rest):
+    kept, sems = rest[:3], rest[3]
+    copies = [pltpu.make_async_copy(src, dst, sems.at[i]) for i, (src, dst) in enumerate(zip((inlet, rows, count), kept))]
+    for copy in copies:
+        copy.start()
     grp = lax.axis_index("grp")
 
     def own_moments():
@@ -174,6 +178,9 @@
     def _():
         own_moments()
         counts[...] = counted[...]
+
+    for copy in copies:
+        copy.wait()
 
 
 def substep(field, zeroth, first, second, counts, grown):
@@ -449,24 +456,26 @@
     hbm = lambda a: pltpu.with_memory_space_constraint(a, pltpu.HBM)
     like = lambda a: jax.ShapeDtypeStruct(a.shape, a.dtype)
     inputs = [a.reshape(-1, LANES) for a in (crystal_size, crystal_weight, crystal_cell)]
-    inputs += [nucleus_cell, nucleus_count, saturation, inlet_mask, migrant_rows, migrant_count]
+    inputs += [nucleus_cell, nucleus_count, saturation]
+    others = [inlet_mask, migrant_rows, migrant_count]
     parcel_rows, events = inputs[0].shape[0], nucleus_cell.shape[1:]
     _, packed_rows = sections(parcel_rows, events[0] * events[1] // LANES, lines)
-    packed, size, weight, cell, event_cell, event_count, field, inlet, rows, count, active, counted = call(
+    packed, size, weight, cell, event_cell, event_count, field, active, counted = call(
         load_kernel,
         [shape(packed_rows, LANES)]
         + [like(a) for a in inputs]
         + [shape(*inputs[0].shape), shape(SUBS, lines, places)],
         *[hbm(a) for a in inputs],
         live_count,
-        specs=[HBM] * 9 + [SMEM],
+        specs=[HBM] * 6 + [SMEM],
         scratch=[pltpu.SemaphoreType.DMA((len(inputs),))],
         name="load",
     )
     packed = swap(packed)
-    home, counts = call(
-        home_kernel, (shape(3, lines, places), shape(SUBS, lines, places)),
-        size, weight, cell, event_cell, event_count, counted,
+    home, counts, inlet, rows, count = call(
+        home_kernel, [shape(3, lines, places), shape(SUBS, lines, places)] + [like(a) for a in others],
+        size, weight, cell, event_cell, event_count, counted, *[hbm(a) for a in others],
+        specs=[VMEM] * 6 + [HBM] * 3, scratch=[pltpu.SemaphoreType.DMA((3,))],
         cost=1 << 30, name="home",
     )
     front, state = call(

time: 19.4 us -> 19.3 us (level)
  no operation moved by 1% of the time
where the time goes in v8:
time: 19.3 us; the launch traced here: 19.1 us
  Pallas kernels  8.16 us (42%)
  starting transfers between devices  5.74 us (30%)
  waiting for transfers between devices  3.82 us (20%)
  between operations  1.37 us (7%)
    pallas_call x13, Pallas kernels, call(): pl.pallas_call(kernel, out_shape=out_shape, in_specs=specs or [VMEM] * le...  8.16 us
    ppermute x2, starting transfers between devices, local(): lax.ppermute(value, ('slab', 'grp'), across_pairs(slabs, second))  4.09 us
    ppermute x7, waiting for transfers between devices, local(): swap = lambda value: lax.ppermute(value, 'grp', [(0, 1), (1, 0)])  3.02 us
    ppermute x7, starting transfers between devices, local(): swap = lambda value: lax.ppermute(value, 'grp', [(0, 1), (1, 0)])  1.65 us
    ppermute x2, waiting for transfers between devices, local(): lax.ppermute(value, ('slab', 'grp'), across_pairs(slabs, second))  0.8 us
  transfers between devices with their start and end apart: 9, of which 6 were waited for; matrix products, arithmetic and copies ran while one was open for 0% of the time, Pallas kernels for 24%

profile of v8, /device:TPU:9, one launch (start us, length us, event | category | flops | bytes accessed | tf_op | source)
XLA Modules:
  0.0 19.1 jit_solution(16865375857963080960)
XLA Ops:
  1.3 1.3 %load.1 = (f32[256,128]{1,0:T(8,128)S(1)}, f32[32,128]{1,0:T(8,128)S(1)}, f32[32,128]{1,0:T(8,128)S(1)}, s32[32,128]{1,0:T(8,128)S(1)}, s32[1,4,512]{2,1,0:T(4,1...) custom-call(f32[32,128]{1,0:T(8,128)} %bitcast.4, ...), custom_call_target="tpu_custom_call" | custom-call | tf_op jit(solution)/shard_map/load/pallas_call | solution.py:425
  2.6 0.4 %collective-permute-start = (f32[256,128]{1,0:T(8,128)S(1)}, f32[256,128]{1,0:T(8,128)S(1)}, u32[]{:S(2)}, u32[]{:S(2)}) collective-permute-start(f32[256,128]{1,0:T(8,128)S(1)} %get-tuple-element.42), channel_id=1, source_target_pairs={{0,1},{1,0},{2,3},{3,2},{4,5},{5,4},{6,7},{7,6},{8,9},{9,8},{10,11... | collective-permute-start | bytes 393224 | tf_op jit(solution)/shard_map/ppermute | solution.py:452
  3.0 1.1 %home.1 = (f32[3,64,256]{2,1,0:T(8,128)S(1)}, f32[2,64,256]{2,1,0:T(8,128)S(1)}, s32[1,64,256]{2,1,0:T(8,128)S(1)}, s32[1,2,512]{2,1,0:T(2,128)S(1)}, s32[1,2]{1,0:T(1,128)S(1)}) custom-call(f32[32,128]{1,0:T(8,128)S(1)} %get-tuple-element.34.size, f32[32,128]{1,0:T(8,128)S(1)} %get-tuple-element.35.weight, s32[32,128]{1,0:T(8,128)S(1)} %get-tuple-element.36.cell, ...), custom_call_target="tpu_custom_call" | custom-call | flops 1073741824 | tf_op jit(solution)/shard_map/home/pallas_call | solution.py:425
  4.1 0.0 collective-permute-done.packed
  4.1 1.2 %front.1 = (f32[1,64,256]{2,1,0:T(8,128)S(1)}, f32[5,64,256]{2,1,0:T(8,128)S(1)}) custom-call(f32[1,64,256]{2,1,0:T(8,128)S(1)} %get-tuple-element.33.field, f32[3,64,256]{2,1,0:T(8,128)S(1)} %get-tuple-element.40.home, f32[2,64,256]{2,1,0:T(8,128)S(1)} %get-tuple-element.41.home_counts, f32[256,128]{1,0:T(8,128)S(1)} %collective-permute-done.packed), custom_call_target="tpu_custom_call" | custom-call | tf_op jit(solution)/shard_map/front/pallas_call | solution.py:425
  5.4 2.1 %collective-permute-start.1 = (f32[1,64,256]{2,1,0:T(8,128)S(1)}, f32[1,64,256]{2,1,0:T(8,128)S(1)}, u32[]{:S(2)}, u32[]{:S(2)}) collective-permute-start(f32[1,64,256]{2,1,0:T(8,128)S(1)} %get-tuple-element.43), channel_id=1, source_target_pairs={{0,2},{3,5},{4,6},{7,9},{8,10},{11,13},{12,14},{15,17},{16,18},{19... | collective-permute-start | bytes 196616 | tf_op jit(solution)/shard_map/ppermute | solution.py:454
  7.5 0.1 collective-permute-start.2
  7.6 0.5 %migrants.1.info = f32[32,256]{1,0:T(8,128)S(1)} custom-call(f32[32,128]{1,0:T(8,128)S(1)} %get-tuple-element.34.size, f32[32,128]{1,0:T(8,128)S(1)} %get-tuple-element.35.weight, s32[32,128]{1,0:T(8,128)S(1)} %get-tuple-element.36.cell, s32[1,2,512]{2,1,0:T(2,128)S(1)} %get-tuple-element.46.rows, s32[1,2]{1,0:T(1,128)S(1)} %get-tuple-element.47.count), custom_call_target="tpu_custom_call" | custom-call | flops 8589934592 | tf_op jit(solution)/shard_map/migrants/pallas_call | solution.py:425
  8.1 0.6 %collective-permute-start.3 = (f32[32,256]{1,0:T(8,128)S(1)}, f32[32,256]{1,0:T(8,128)S(1)}, u32[]{:S(2)}, u32[]{:S(2)}) collective-permute-start(f32[32,256]{1,0:T(8,128)S(1)} %migrants.1.info), channel_id=1, source_target_pairs={{0,1},{1,0},{2,3},{3,2},{4,5},{5,4},{6,7},{7,6},{8,9},{9,8},{10,11... | collective-permute-start | bytes 98312 | tf_op jit(solution)/shard_map/ppermute | solution.py:452
  8.6 0.5 %late.1 = f32[2,64,256]{2,1,0:T(8,128)S(1)} custom-call(f32[256,128]{1,0:T(8,128)S(1)} %collective-permute-done.packed, s32[1,4,512]{2,1,0:T(4,128)S(1)} %get-tuple-element.37.event_cell, s32[1,4,512]{2,1,0:T(4,128)S(1)} %get-tuple-element.38.event_count), custom_call_target="tpu_custom_call" | custom-call | flops 268435456 | tf_op jit(solution)/shard_map/late/pallas_call | solution.py:425
  9.1 0.4 %collective-permute-done.3.their_info = f32[32,256]{1,0:T(8,128)S(1)} collective-permute-done((f32[32,256]{1,0:T(8,128)S(1)}, f32[32,256]{1,0:T(8,128)S(1)}, u32[]{:S(2)}, u32[]{:S(2)}) %collective-permute-start.3) | collective-permute-done | bytes 32800 | tf_op jit(solution)/shard_map/ppermute | solution.py:452
  9.5 0.0 collective-permute-done.2.other
  9.5 0.3 %ready.1 = (f32[6,64,256]{2,1,0:T(8,128)S(1)}, bf16[256,1024]{1,0:T(8,128)(2,1)S(1)}, f32[8,1024]{1,0:T(8,128)S(1)}) custom-call(f32[6,64,256]{2,1,0:T(8,128)S(1)} %pack.1.mine, f32[6,64,256]{2,1,0:T(8,128)S(1)} %collective-permute-done.2.other, f32[32,256]{1,0:T(8,128)S(1)} %migrants.1.info, f32[32,256]{1,0:T(8,128)S(1)} %collective-permute-done.3.their_info), custom_call_target="tpu_custom_call" | custom-call | flops 67108864 | tf_op jit(solution)/shard_map/ready/pallas_call | solution.py:425
  9.8 0.6 %collective-permute-done.1.beside = f32[1,64,256]{2,1,0:T(8,128)S(1)} collective-permute-done((f32[1,64,256]{2,1,0:T(8,128)S(1)}, f32[1,64,256]{2,1,0:T(8,128)S(1)}, u32[]{:S(2)}, u32[]{:S(2)}) %collective-permute-start.1) | collective-permute-done | bytes 65568 | tf_op jit(solution)/shard_map/ppermute | solution.py:454
  10.4 0.3 %second.1 = f32[8,256]{1,0:T(8,128)S(1)} custom-call(f32[1,64,256]{2,1,0:T(8,128)S(1)} %collective-permute-done.1.beside, f32[6,64,256]{2,1,0:T(8,128)S(1)} %get-tuple-element.49.ready, f32[2,64,256]{2,1,0:T(8,128)S(1)} %late.1, bf16[256,1024]{1,0:T(8,128)(2,1)S(1)} %get-tuple-element.53.hot_place, f32[8,1024]{1,0:T(8,128)S(1)} %get-tuple-element.54.lists), custom_call_target="tpu_custom_call" | custom-call | tf_op jit(solution)/shard_map/second/pallas_call | solution.py:425
  10.8 0.1 collective-permute-start.5
  10.8 0.4 %own.1 = (f32[8,256]{1,0:T(8,128)S(1)}, f32[1,64,256]{2,1,0:T(8,128)S(1)}, f32[1,64,256]{2,1,0:T(8,128)S(1)}) custom-call(f32[1,64,256]{2,1,0:T(8,128)S(1)} %collective-permute-done.1.beside, f32[6,64,256]{2,1,0:T(8,128)S(1)} %get-tuple-element.49.ready, f32[2,64,256]{2,1,0:T(8,128)S(1)} %late.1, f32[32,256]{1,0:T(8,128)S(1)} %migrants.1.info, ...), custom_call_target="tpu_custom_call" | custom-call | flops 268435456 | tf_op jit(solution)/shard_map/own/pallas_call | solution.py:425
  11.2 0.8 %collective-permute-done.5.theirs = f32[8,256]{1,0:T(8,128)S(1)} collective-permute-done((f32[8,256]{1,0:T(8,128)S(1)}, f32[8,256]{1,0:T(8,128)S(1)}, u32[]{:S(2)}, u32[]{:S(2)}) %collective-permute-start.5) | collective-permute-done | bytes 8224 | tf_op jit(solution)/shard_map/ppermute | solution.py:452
  12.0 2.0 %collective-permute-start.6 = (f32[72,256]{1,0:T(8,128)S(1)}, f32[72,256]{1,0:T(8,128)S(1)}, u32[]{:S(2)}, u32[]{:S(2)}) collective-permute-start(f32[72,256]{1,0:T(8,128)S(1)} %leaving.1), channel_id=1, source_target_pairs={{1,2},{3,5},{4,6},{7,9},{8,10},{11,13},{12,14},{15,17},{16,18},{19... | collective-permute-start | bytes 221192 | tf_op jit(solution)/shard_map/ppermute | solution.py:454
  14.0 0.0 collective-permute-start.7
  14.0 0.5 %collective-permute-start.4 = (f32[1,64,256]{2,1,0:T(8,128)S(1)}, f32[1,64,256]{2,1,0:T(8,128)S(1)}, u32[]{:S(2)}, u32[]{:S(2)}) collective-permute-start(f32[1,64,256]{2,1,0:T(8,128)S(1)} %get-tuple-element.51.front), channel_id=1, source_target_pairs={{0,1},{1,0},{2,3},{3,2},{4,5},{5,4},{6,7},{7,6},{8,9},{9,8},{10,11... | collective-permute-start | bytes 196616 | tf_op jit(solution)/shard_map/ppermute | solution.py:452
  14.5 0.7 %collective-permute-done.7.their_total = f32[1,64,256]{2,1,0:T(8,128)S(1)} collective-permute-done((f32[1,64,256]{2,1,0:T(8,128)S(1)}, f32[1,64,256]{2,1,0:T(8,128)S(1)}, u32[]{:S(2)}, u32[]{:S(2)}) %collective-permute-start.7) | collective-permute-done | bytes 65568 | tf_op jit(solution)/shard_map/ppermute | solution.py:452
  15.3 1.7 %sizes.1 = f32[32,128]{1,0:T(8,128)} custom-call(f32[1,64,256]{2,1,0:T(8,128)S(1)} %get-tuple-element.56.total, f32[1,64,256]{2,1,0:T(8,128)S(1)} %collective-permute-done.7.their_total, f32[32,128]{1,0:T(8,128)S(1)} %get-tuple-element.34.size, s32[32,128]{1,0:T(8,128)S(1)} %get-tuple-element.36.cell, f32[32,128]{1,0:T(8,128)S(1)} %get-tuple-element.57.active), custom_call_target="tpu_custom_call" | custom-call | flops 67108864 | tf_op jit(solution)/shard_map/sizes/pallas_call | solution.py:425
  17.0 0.2 collective-permute-done.6.received
  17.2 0.0 collective-permute-start.8
  17.2 0.0 collective-permute-done.4.their_front
  17.2 0.1 rest.1
  17.3 1.1 %collective-permute-done.8.relayed = f32[72,256]{1,0:T(8,128)S(1)} collective-permute-done((f32[72,256]{1,0:T(8,128)S(1)}, f32[72,256]{1,0:T(8,128)S(1)}, u32[]{:S(2)}, u32[]{:S(2)}) %collective-permute-start.8) | collective-permute-done | bytes 73760 | tf_op jit(solution)/shard_map/ppermute | solution.py:452
  18.4 0.7 %last.1 = (f32[1,64,256]{2,1,0:T(8,128)}, f32[1,2,2,512]{3,2,1,0:T(2,128)}) custom-call(f32[2,64,256]{2,1,0:T(8,128)S(1)} %rest.1, f32[72,256]{1,0:T(8,128)S(1)} %collective-permute-done.6.received, f32[72,256]{1,0:T(8,128)S(1)} %collective-permute-done.8.relayed), custom_call_target="tpu_custom_call" | custom-call | tf_op jit(solution)/shard_map/last/pallas_call | solution.py:425
  (2 shorter events, 0.0 us)
Async XLA Ops:
  2.6 1.5 %collective-permute-start = (f32[256,128]{1,0:T(8,128)S(1)}, f32[256,128]{1,0:T(8,128)S(1)}, u32[]{:S(2)}, u32[]{:S(2)}) collective-permute-start(f32[256,128]{1,0:T(8,128)S(1)} %get-tuple-element.42), channel_id=1, source_target_pairs={{0,1},{1,0},{2,3},{3,2},{4,5},{5,4},{6,7},{7,6},{8,9},{9,8},{10,11... | collective-permute-start | bytes 393224 | tf_op jit(solution)/shard_map/ppermute | solution.py:452
  5.4 5.1 %collective-permute-start.1 = (f32[1,64,256]{2,1,0:T(8,128)S(1)}, f32[1,64,256]{2,1,0:T(8,128)S(1)}, u32[]{:S(2)}, u32[]{:S(2)}) collective-permute-start(f32[1,64,256]{2,1,0:T(8,128)S(1)} %get-tuple-element.43), channel_id=1, source_target_pairs={{0,2},{3,5},{4,6},{7,9},{8,10},{11,13},{12,14},{15,17},{16,18},{19... | collective-permute-start | bytes 196616 | tf_op jit(solution)/shard_map/ppermute | solution.py:454
  7.5 2.0 %collective-permute-start.2 = (f32[6,64,256]{2,1,0:T(8,128)S(1)}, f32[6,64,256]{2,1,0:T(8,128)S(1)}, u32[]{:S(2)}, u32[]{:S(2)}) collective-permute-start(f32[6,64,256]{2,1,0:T(8,128)S(1)} %pack.1.mine), channel_id=1, source_target_pairs={{0,1},{1,0},{2,3},{3,2},{4,5},{5,4},{6,7},{7,6},{8,9},{9,8},{10,11... | collective-permute-start | bytes 1179656 | tf_op jit(solution)/shard_map/ppermute | solution.py:452
  8.1 1.4 %collective-permute-start.3 = (f32[32,256]{1,0:T(8,128)S(1)}, f32[32,256]{1,0:T(8,128)S(1)}, u32[]{:S(2)}, u32[]{:S(2)}) collective-permute-start(f32[32,256]{1,0:T(8,128)S(1)} %migrants.1.info), channel_id=1, source_target_pairs={{0,1},{1,0},{2,3},{3,2},{4,5},{5,4},{6,7},{7,6},{8,9},{9,8},{10,11... | collective-permute-start | bytes 98312 | tf_op jit(solution)/shard_map/ppermute | solution.py:452
  10.8 1.2 %collective-permute-start.5 = (f32[8,256]{1,0:T(8,128)S(1)}, f32[8,256]{1,0:T(8,128)S(1)}, u32[]{:S(2)}, u32[]{:S(2)}) collective-permute-start(f32[8,256]{1,0:T(8,128)S(1)} %second.1), channel_id=1, source_target_pairs={{0,1},{1,0},{2,3},{3,2},{4,5},{5,4},{6,7},{7,6},{8,9},{9,8},{10,11... | collective-permute-start | bytes 24584 | tf_op jit(solution)/shard_map/ppermute | solution.py:452
  12.0 5.2 %collective-permute-start.6 = (f32[72,256]{1,0:T(8,128)S(1)}, f32[72,256]{1,0:T(8,128)S(1)}, u32[]{:S(2)}, u32[]{:S(2)}) collective-permute-start(f32[72,256]{1,0:T(8,128)S(1)} %leaving.1), channel_id=1, source_target_pairs={{1,2},{3,5},{4,6},{7,9},{8,10},{11,13},{12,14},{15,17},{16,18},{19... | collective-permute-start | bytes 221192 | tf_op jit(solution)/shard_map/ppermute | solution.py:454
  14.0 1.3 %collective-permute-start.7 = (f32[1,64,256]{2,1,0:T(8,128)S(1)}, f32[1,64,256]{2,1,0:T(8,128)S(1)}, u32[]{:S(2)}, u32[]{:S(2)}) collective-permute-start(f32[1,64,256]{2,1,0:T(8,128)S(1)} %get-tuple-element.56.total), channel_id=1, source_target_pairs={{0,1},{1,0},{2,3},{3,2},{4,5},{5,4},{6,7},{7,6},{8,9},{9,8},{10,11... | collective-permute-start | bytes 196616 | tf_op jit(solution)/shard_map/ppermute | solution.py:452
  14.0 3.2 %collective-permute-start.4 = (f32[1,64,256]{2,1,0:T(8,128)S(1)}, f32[1,64,256]{2,1,0:T(8,128)S(1)}, u32[]{:S(2)}, u32[]{:S(2)}) collective-permute-start(f32[1,64,256]{2,1,0:T(8,128)S(1)} %get-tuple-element.51.front), channel_id=1, source_target_pairs={{0,1},{1,0},{2,3},{3,2},{4,5},{5,4},{6,7},{7,6},{8,9},{9,8},{10,11... | collective-permute-start | bytes 196616 | tf_op jit(solution)/shard_map/ppermute | solution.py:452
  17.2 1.3 %collective-permute-start.8 = (f32[72,256]{1,0:T(8,128)S(1)}, f32[72,256]{1,0:T(8,128)S(1)}, u32[]{:S(2)}, u32[]{:S(2)}) collective-permute-start(f32[72,256]{1,0:T(8,128)S(1)} %collective-permute-done.6.received), channel_id=1, source_target_pairs={{0,1},{1,0},{2,3},{3,2},{4,5},{5,4},{6,7},{7,6},{8,9},{9,8},{10,11... | collective-permute-start | bytes 221192 | tf_op jit(solution)/shard_map/ppermute | solution.py:452

commit v9 on v8

--- a/solution.py
+++ b/solution.py
@@ -129,16 +129,18 @@
     return cells.astype(jnp.int32), counts
 
 
+def zeros_kernel(out):
+    out[...] = jnp.zeros(out.shape, jnp.int32)
+
+
+def live_kernel(live, zeros, out):
+    out[...] = zeros[...] + live[0]
+
+
 def load_kernel(*refs):
-    inputs, live, out, kept, active, counts, sems = refs[:6], refs[6], refs[7], refs[8:14], *refs[14:]
-    copies = [pltpu.make_async_copy(src, dst, sems.at[i]) for i, (src, dst) in enumerate(zip(inputs, kept))]
-    for copy in copies:
-        copy.start()
-    for copy in copies:
-        copy.wait()
-    size, weight, cell, event_cell, event_count, field = kept[:6]
-    active[...] = jnp.where(row_numbers(size.shape) < live[0], 1.0, 0.0)
-    weight[...] = weight[...] * active[...]
+    size, all_weight, cell, event_cell, event_count, field, live, out, weight, active, counts = refs
+    active[...] = jnp.where(row_numbers(size.shape) < live[0:1, 0:1], 1.0, 0.0)
+    weight[...] = all_weight[...] * active[...]
     events, width = event_cell.shape[1:]
     per = width // LANES
     spans, _ = sections(size.shape[0], events * per, field.shape[1])
@@ -460,16 +462,14 @@
     others = [inlet_mask, migrant_rows, migrant_count]
     parcel_rows, events = inputs[0].shape[0], nucleus_cell.shape[1:]
     _, packed_rows = sections(parcel_rows, events[0] * events[1] // LANES, lines)
-    packed, size, weight, cell, event_cell, event_count, field, active, counted = call(
+    tile = jax.ShapeDtypeStruct((8, LANES), jnp.int32)
+    zeros = call(zeros_kernel, tile, cost=1 << 30, name="zeros")
+    live = call(live_kernel, tile, live_count, zeros, specs=[SMEM, VMEM], name="live")
+    size, _, cell, event_cell, event_count, field = inputs
+    packed, weight, active, counted = call(
         load_kernel,
-        [shape(packed_rows, LANES)]
-        + [like(a) for a in inputs]
-        + [shape(*inputs[0].shape), shape(SUBS, lines, places)],
-        *[hbm(a) for a in inputs],
-        live_count,
-        specs=[HBM] * 6 + [SMEM],
-        scratch=[pltpu.SemaphoreType.DMA((len(inputs),))],
-        name="load",
+        [shape(packed_rows, LANES), shape(*size.shape), shape(*size.shape), shape(SUBS, lines, places)],
+        *inputs, live, name="load",
     )
     packed = swap(packed)
     home, counts, inlet, rows, count = call(

time: 19.3 us -> 18.5 us (0.959)
  Pallas kernels: 8.16 us -> 7.21 us
    pallas_call x13 -> x15, Pallas kernels: 8.16 us -> 7.21 us  [call(): pl.pallas_call(kernel, out_shape=out_shape, in_specs=specs or [VMEM] * le...]
  transfers between devices with their start and end apart: 9 -> 9, of which waited for: 6 -> 6; matrix products, arithmetic and copies ran while one was open for 0% -> 0% of each run, Pallas kernels for 24% -> 25%
where the time goes in v9:
time: 18.5 us; the launch traced here: 18.3 us
  Pallas kernels  7.21 us (39%)
  starting transfers between devices  5.74 us (31%)
  waiting for transfers between devices  3.81 us (21%)
  between operations  1.49 us (8%)
    pallas_call x15, Pallas kernels, call(): pl.pallas_call(kernel, out_shape=out_shape, in_specs=specs or [VMEM] * le...  7.21 us
    ppermute x2, starting transfers between devices, local(): lax.ppermute(value, ('slab', 'grp'), across_pairs(slabs, second))  4.09 us
    ppermute x7, waiting for transfers between devices, local(): swap = lambda value: lax.ppermute(value, 'grp', [(0, 1), (1, 0)])  3.02 us
    ppermute x7, starting transfers between devices, local(): swap = lambda value: lax.ppermute(value, 'grp', [(0, 1), (1, 0)])  1.65 us
    ppermute x2, waiting for transfers between devices, local(): lax.ppermute(value, ('slab', 'grp'), across_pairs(slabs, second))  0.79 us
  transfers between devices with their start and end apart: 9, of which 6 were waited for; matrix products, arithmetic and copies ran while one was open for 0% of the time, Pallas kernels for 25%

profile of v9, /device:TPU:9, one launch (start us, length us, event | category | flops | bytes accessed | tf_op | source)
XLA Modules:
  0.0 18.3 jit_solution(2567793985394522302)
XLA Ops:
  0.6 0.0 copy-start
  0.6 0.0 copy-start.2
  0.7 0.0 copy-start.3
  0.7 0.0 copy-start.4
  0.7 0.0 copy-start.5
  0.7 0.0 copy-start.1
  1.4 0.1 copy-done
  1.5 0.0 copy-done.2
  1.5 0.0 copy-done.3
  1.5 0.0 copy-done.4
  1.5 0.0 copy-done.5
  1.5 0.0 copy-done.1
  1.5 0.4 %load.1 = (f32[256,128]{1,0:T(8,128)S(1)}, f32[32,128]{1,0:T(8,128)S(1)}, f32[32,128]{1,0:T(8,128)S(1)}, f32[2,64,256]{2,1,0:T(8,128)S(1)}) custom-call(f32[32,128]{1,0:T(8,128)S(1)} %bitcast.5, f32[32,128]{1,0:T(8,128)S(1)} %bitcast.4, s32[32,128]{1,0:T(8,128)S(1)} %bitcast.9, s32[1,4,512]{2,1,0:T(4,128)S(1)} %copy-done.4, s32[1,4,512]{2,1,0:T(4,128)S(1)} %copy-done.5, ...), custom_call_target="tpu_custom_call" | custom-call | tf_op jit(solution)/shard_map/load/pallas_call | solution.py:427
  1.9 0.4 %collective-permute-start = (f32[256,128]{1,0:T(8,128)S(1)}, f32[256,128]{1,0:T(8,128)S(1)}, u32[]{:S(2)}, u32[]{:S(2)}) collective-permute-start(f32[256,128]{1,0:T(8,128)S(1)} %get-tuple-element.32), channel_id=1, source_target_pairs={{0,1},{1,0},{2,3},{3,2},{4,5},{5,4},{6,7},{7,6},{8,9},{9,8},{10,11... | collective-permute-start | bytes 393224 | tf_op jit(solution)/shard_map/ppermute | solution.py:454
  2.3 1.1 %home.1 = (f32[3,64,256]{2,1,0:T(8,128)S(1)}, f32[2,64,256]{2,1,0:T(8,128)S(1)}, s32[1,64,256]{2,1,0:T(8,128)S(1)}, s32[1,2,512]{2,1,0:T(2,128)S(1)}, s32[1,2]{1,0:T(1,128)S(1)}) custom-call(f32[32,128]{1,0:T(8,128)S(1)} %bitcast.6, f32[32,128]{1,0:T(8,128)S(1)} %get-tuple-element.28.weight, s32[32,128]{1,0:T(8,128)S(1)} %bitcast.10, ...), custom_call_target="tpu_custom_call" | custom-call | flops 1073741824 | tf_op jit(solution)/shard_map/home/pallas_call | solution.py:427
  3.4 0.0 collective-permute-done.packed
  3.4 1.2 %front.1 = (f32[1,64,256]{2,1,0:T(8,128)S(1)}, f32[5,64,256]{2,1,0:T(8,128)S(1)}) custom-call(f32[1,64,256]{2,1,0:T(8,128)S(1)} %copy-done, f32[3,64,256]{2,1,0:T(8,128)S(1)} %get-tuple-element.30.home, f32[2,64,256]{2,1,0:T(8,128)S(1)} %get-tuple-element.31.home_counts, f32[256,128]{1,0:T(8,128)S(1)} %collective-permute-done.packed), custom_call_target="tpu_custom_call" | custom-call | tf_op jit(solution)/shard_map/front/pallas_call | solution.py:427
  4.6 2.1 %collective-permute-start.1 = (f32[1,64,256]{2,1,0:T(8,128)S(1)}, f32[1,64,256]{2,1,0:T(8,128)S(1)}, u32[]{:S(2)}, u32[]{:S(2)}) collective-permute-start(f32[1,64,256]{2,1,0:T(8,128)S(1)} %get-tuple-element.33), channel_id=1, source_target_pairs={{0,2},{3,5},{4,6},{7,9},{8,10},{11,13},{12,14},{15,17},{16,18},{19... | collective-permute-start | bytes 196616 | tf_op jit(solution)/shard_map/ppermute | solution.py:456
  6.7 0.1 collective-permute-start.2
  6.8 0.5 %migrants.1.info = f32[32,256]{1,0:T(8,128)S(1)} custom-call(f32[32,128]{1,0:T(8,128)S(1)} %bitcast.7, f32[32,128]{1,0:T(8,128)S(1)} %get-tuple-element.28.weight, s32[32,128]{1,0:T(8,128)S(1)} %bitcast.11, s32[1,2,512]{2,1,0:T(2,128)S(1)} %get-tuple-element.36.rows, s32[1,2]{1,0:T(1,128)S(1)} %get-tuple-element.37.count), custom_call_target="tpu_custom_call" | custom-call | flops 8589934592 | tf_op jit(solution)/shard_map/migrants/pallas_call | solution.py:427
  7.3 0.6 %collective-permute-start.3 = (f32[32,256]{1,0:T(8,128)S(1)}, f32[32,256]{1,0:T(8,128)S(1)}, u32[]{:S(2)}, u32[]{:S(2)}) collective-permute-start(f32[32,256]{1,0:T(8,128)S(1)} %migrants.1.info), channel_id=1, source_target_pairs={{0,1},{1,0},{2,3},{3,2},{4,5},{5,4},{6,7},{7,6},{8,9},{9,8},{10,11... | collective-permute-start | bytes 98312 | tf_op jit(solution)/shard_map/ppermute | solution.py:454
  7.9 0.5 %late.1 = f32[2,64,256]{2,1,0:T(8,128)S(1)} custom-call(f32[256,128]{1,0:T(8,128)S(1)} %collective-permute-done.packed, s32[1,4,512]{2,1,0:T(4,128)S(1)} %copy-done.4, s32[1,4,512]{2,1,0:T(4,128)S(1)} %copy-done.5), custom_call_target="tpu_custom_call" | custom-call | flops 268435456 | tf_op jit(solution)/shard_map/late/pallas_call | solution.py:427
  8.4 0.4 %collective-permute-done.3.their_info = f32[32,256]{1,0:T(8,128)S(1)} collective-permute-done((f32[32,256]{1,0:T(8,128)S(1)}, f32[32,256]{1,0:T(8,128)S(1)}, u32[]{:S(2)}, u32[]{:S(2)}) %collective-permute-start.3) | collective-permute-done | bytes 32800 | tf_op jit(solution)/shard_map/ppermute | solution.py:454
  8.7 0.0 collective-permute-done.2.other
  8.7 0.3 %ready.1 = (f32[6,64,256]{2,1,0:T(8,128)S(1)}, bf16[256,1024]{1,0:T(8,128)(2,1)S(1)}, f32[8,1024]{1,0:T(8,128)S(1)}) custom-call(f32[6,64,256]{2,1,0:T(8,128)S(1)} %pack.1.mine, f32[6,64,256]{2,1,0:T(8,128)S(1)} %collective-permute-done.2.other, f32[32,256]{1,0:T(8,128)S(1)} %migrants.1.info, f32[32,256]{1,0:T(8,128)S(1)} %collective-permute-done.3.their_info), custom_call_target="tpu_custom_call" | custom-call | flops 67108864 | tf_op jit(solution)/shard_map/ready/pallas_call | solution.py:427
  9.1 0.6 %collective-permute-done.1.beside = f32[1,64,256]{2,1,0:T(8,128)S(1)} collective-permute-done((f32[1,64,256]{2,1,0:T(8,128)S(1)}, f32[1,64,256]{2,1,0:T(8,128)S(1)}, u32[]{:S(2)}, u32[]{:S(2)}) %collective-permute-start.1) | collective-permute-done | bytes 65568 | tf_op jit(solution)/shard_map/ppermute | solution.py:456
  9.7 0.3 %second.1 = f32[8,256]{1,0:T(8,128)S(1)} custom-call(f32[1,64,256]{2,1,0:T(8,128)S(1)} %collective-permute-done.1.beside, f32[6,64,256]{2,1,0:T(8,128)S(1)} %get-tuple-element.39.ready, f32[2,64,256]{2,1,0:T(8,128)S(1)} %late.1, bf16[256,1024]{1,0:T(8,128)(2,1)S(1)} %get-tuple-element.43.hot_place, f32[8,1024]{1,0:T(8,128)S(1)} %get-tuple-element.44.lists), custom_call_target="tpu_custom_call" | custom-call | tf_op jit(solution)/shard_map/second/pallas_call | solution.py:427
  10.0 0.1 collective-permute-start.5
  10.1 0.4 %own.1 = (f32[8,256]{1,0:T(8,128)S(1)}, f32[1,64,256]{2,1,0:T(8,128)S(1)}, f32[1,64,256]{2,1,0:T(8,128)S(1)}) custom-call(f32[1,64,256]{2,1,0:T(8,128)S(1)} %collective-permute-done.1.beside, f32[6,64,256]{2,1,0:T(8,128)S(1)} %get-tuple-element.39.ready, f32[2,64,256]{2,1,0:T(8,128)S(1)} %late.1, f32[32,256]{1,0:T(8,128)S(1)} %migrants.1.info, ...), custom_call_target="tpu_custom_call" | custom-call | flops 268435456 | tf_op jit(solution)/shard_map/own/pallas_call | solution.py:427
  10.5 0.8 %collective-permute-done.5.theirs = f32[8,256]{1,0:T(8,128)S(1)} collective-permute-done((f32[8,256]{1,0:T(8,128)S(1)}, f32[8,256]{1,0:T(8,128)S(1)}, u32[]{:S(2)}, u32[]{:S(2)}) %collective-permute-start.5) | collective-permute-done | bytes 8224 | tf_op jit(solution)/shard_map/ppermute | solution.py:454
  11.3 2.0 %collective-permute-start.6 = (f32[72,256]{1,0:T(8,128)S(1)}, f32[72,256]{1,0:T(8,128)S(1)}, u32[]{:S(2)}, u32[]{:S(2)}) collective-permute-start(f32[72,256]{1,0:T(8,128)S(1)} %leaving.1), channel_id=1, source_target_pairs={{1,2},{3,5},{4,6},{7,9},{8,10},{11,13},{12,14},{15,17},{16,18},{19... | collective-permute-start | bytes 221192 | tf_op jit(solution)/shard_map/ppermute | solution.py:456
  13.3 0.0 collective-permute-start.7
  13.3 0.5 %collective-permute-start.4 = (f32[1,64,256]{2,1,0:T(8,128)S(1)}, f32[1,64,256]{2,1,0:T(8,128)S(1)}, u32[]{:S(2)}, u32[]{:S(2)}) collective-permute-start(f32[1,64,256]{2,1,0:T(8,128)S(1)} %get-tuple-element.41.front), channel_id=1, source_target_pairs={{0,1},{1,0},{2,3},{3,2},{4,5},{5,4},{6,7},{7,6},{8,9},{9,8},{10,11... | collective-permute-start | bytes 196616 | tf_op jit(solution)/shard_map/ppermute | solution.py:454
  13.8 0.7 %collective-permute-done.7.their_total = f32[1,64,256]{2,1,0:T(8,128)S(1)} collective-permute-done((f32[1,64,256]{2,1,0:T(8,128)S(1)}, f32[1,64,256]{2,1,0:T(8,128)S(1)}, u32[]{:S(2)}, u32[]{:S(2)}) %collective-permute-start.7) | collective-permute-done | bytes 65568 | tf_op jit(solution)/shard_map/ppermute | solution.py:454
  14.5 1.7 %sizes.1 = f32[32,128]{1,0:T(8,128)} custom-call(f32[1,64,256]{2,1,0:T(8,128)S(1)} %get-tuple-element.46.total, f32[1,64,256]{2,1,0:T(8,128)S(1)} %collective-permute-done.7.their_total, f32[32,128]{1,0:T(8,128)S(1)} %bitcast.8, s32[32,128]{1,0:T(8,128)S(1)} %bitcast.12, f32[32,128]{1,0:T(8,128)S(1)} %get-tuple-element.47.active), custom_call_target="tpu_custom_call" | custom-call | flops 67108864 | tf_op jit(solution)/shard_map/sizes/pallas_call | solution.py:427
  16.2 0.2 %collective-permute-done.6.received = f32[72,256]{1,0:T(8,128)S(1)} collective-permute-done((f32[72,256]{1,0:T(8,128)S(1)}, f32[72,256]{1,0:T(8,128)S(1)}, u32[]{:S(2)}, u32[]{:S(2)}) %collective-permute-start.6) | collective-permute-done | bytes 73760 | tf_op jit(solution)/shard_map/ppermute | solution.py:456
  16.4 0.0 collective-permute-start.8
  16.4 0.0 collective-permute-done.4.their_front
  16.4 0.1 rest.1
  16.6 1.1 %collective-permute-done.8.relayed = f32[72,256]{1,0:T(8,128)S(1)} collective-permute-done((f32[72,256]{1,0:T(8,128)S(1)}, f32[72,256]{1,0:T(8,128)S(1)}, u32[]{:S(2)}, u32[]{:S(2)}) %collective-permute-start.8) | collective-permute-done | bytes 73760 | tf_op jit(solution)/shard_map/ppermute | solution.py:454
  17.7 0.7 %last.1 = (f32[1,64,256]{2,1,0:T(8,128)}, f32[1,2,2,512]{3,2,1,0:T(2,128)}) custom-call(f32[2,64,256]{2,1,0:T(8,128)S(1)} %rest.1, f32[72,256]{1,0:T(8,128)S(1)} %collective-permute-done.6.received, f32[72,256]{1,0:T(8,128)S(1)} %collective-permute-done.8.relayed), custom_call_target="tpu_custom_call" | custom-call | tf_op jit(solution)/shard_map/last/pallas_call | solution.py:427
  (4 shorter events, 0.0 us)
Async XLA Ops:
  0.6 0.8 %copy-start = (f32[1,64,256]{2,1,0:T(8,128)S(1)}, f32[1,64,256]{2,1,0:T(8,128)}, u32[]{:S(2)}) copy-start(f32[1,64,256]{2,1,0:T(8,128)} %field.1) | copy-start | bytes 196612
  0.6 0.8 %copy-start.2 = (f32[4096]{0:T(1024)S(1)}, f32[4096]{0:T(1024)}, u32[]{:S(2)}) copy-start(f32[4096]{0:T(1024)} %param.12) | copy-start | bytes 49156
  0.7 0.8 %copy-start.3 = (s32[4096]{0:T(1024)S(1)}, s32[4096]{0:T(1024)}, u32[]{:S(2)}) copy-start(s32[4096]{0:T(1024)} %param.14) | copy-start | bytes 49156
  0.7 0.8 %copy-start.4 = (s32[1,4,512]{2,1,0:T(4,128)S(1)}, s32[1,4,512]{2,1,0:T(4,128)}, u32[]{:S(2)}) copy-start(s32[1,4,512]{2,1,0:T(4,128)} %event_cell.3) | copy-start | bytes 24580
  0.7 0.8 %copy-start.5 = (s32[1,4,512]{2,1,0:T(4,128)S(1)}, s32[1,4,512]{2,1,0:T(4,128)}, u32[]{:S(2)}) copy-start(s32[1,4,512]{2,1,0:T(4,128)} %event_count.3) | copy-start | bytes 24580
  0.7 0.8 %copy-start.1 = (f32[4096]{0:T(1024)S(1)}, f32[4096]{0:T(1024)}, u32[]{:S(2)}) copy-start(f32[4096]{0:T(1024)} %param.13) | copy-start | bytes 49156
  1.9 1.5 %collective-permute-start = (f32[256,128]{1,0:T(8,128)S(1)}, f32[256,128]{1,0:T(8,128)S(1)}, u32[]{:S(2)}, u32[]{:S(2)}) collective-permute-start(f32[256,128]{1,0:T(8,128)S(1)} %get-tuple-element.32), channel_id=1, source_target_pairs={{0,1},{1,0},{2,3},{3,2},{4,5},{5,4},{6,7},{7,6},{8,9},{9,8},{10,11... | collective-permute-start | bytes 393224 | tf_op jit(solution)/shard_map/ppermute | solution.py:454
  4.6 5.1 %collective-permute-start.1 = (f32[1,64,256]{2,1,0:T(8,128)S(1)}, f32[1,64,256]{2,1,0:T(8,128)S(1)}, u32[]{:S(2)}, u32[]{:S(2)}) collective-permute-start(f32[1,64,256]{2,1,0:T(8,128)S(1)} %get-tuple-element.33), channel_id=1, source_target_pairs={{0,2},{3,5},{4,6},{7,9},{8,10},{11,13},{12,14},{15,17},{16,18},{19... | collective-permute-start | bytes 196616 | tf_op jit(solution)/shard_map/ppermute | solution.py:456
  6.7 2.0 %collective-permute-start.2 = (f32[6,64,256]{2,1,0:T(8,128)S(1)}, f32[6,64,256]{2,1,0:T(8,128)S(1)}, u32[]{:S(2)}, u32[]{:S(2)}) collective-permute-start(f32[6,64,256]{2,1,0:T(8,128)S(1)} %pack.1.mine), channel_id=1, source_target_pairs={{0,1},{1,0},{2,3},{3,2},{4,5},{5,4},{6,7},{7,6},{8,9},{9,8},{10,11... | collective-permute-start | bytes 1179656 | tf_op jit(solution)/shard_map/ppermute | solution.py:454
  7.3 1.4 %collective-permute-start.3 = (f32[32,256]{1,0:T(8,128)S(1)}, f32[32,256]{1,0:T(8,128)S(1)}, u32[]{:S(2)}, u32[]{:S(2)}) collective-permute-start(f32[32,256]{1,0:T(8,128)S(1)} %migrants.1.info), channel_id=1, source_target_pairs={{0,1},{1,0},{2,3},{3,2},{4,5},{5,4},{6,7},{7,6},{8,9},{9,8},{10,11... | collective-permute-start | bytes 98312 | tf_op jit(solution)/shard_map/ppermute | solution.py:454
  10.0 1.2 %collective-permute-start.5 = (f32[8,256]{1,0:T(8,128)S(1)}, f32[8,256]{1,0:T(8,128)S(1)}, u32[]{:S(2)}, u32[]{:S(2)}) collective-permute-start(f32[8,256]{1,0:T(8,128)S(1)} %second.1), channel_id=1, source_target_pairs={{0,1},{1,0},{2,3},{3,2},{4,5},{5,4},{6,7},{7,6},{8,9},{9,8},{10,11... | collective-permute-start | bytes 24584 | tf_op jit(solution)/shard_map/ppermute | solution.py:454
  11.3 5.2 %collective-permute-start.6 = (f32[72,256]{1,0:T(8,128)S(1)}, f32[72,256]{1,0:T(8,128)S(1)}, u32[]{:S(2)}, u32[]{:S(2)}) collective-permute-start(f32[72,256]{1,0:T(8,128)S(1)} %leaving.1), channel_id=1, source_target_pairs={{1,2},{3,5},{4,6},{7,9},{8,10},{11,13},{12,14},{15,17},{16,18},{19... | collective-permute-start | bytes 221192 | tf_op jit(solution)/shard_map/ppermute | solution.py:456
  13.3 1.3 %collective-permute-start.7 = (f32[1,64,256]{2,1,0:T(8,128)S(1)}, f32[1,64,256]{2,1,0:T(8,128)S(1)}, u32[]{:S(2)}, u32[]{:S(2)}) collective-permute-start(f32[1,64,256]{2,1,0:T(8,128)S(1)} %get-tuple-element.46.total), channel_id=1, source_target_pairs={{0,1},{1,0},{2,3},{3,2},{4,5},{5,4},{6,7},{7,6},{8,9},{9,8},{10,11... | collective-permute-start | bytes 196616 | tf_op jit(solution)/shard_map/ppermute | solution.py:454
  13.3 3.2 %collective-permute-start.4 = (f32[1,64,256]{2,1,0:T(8,128)S(1)}, f32[1,64,256]{2,1,0:T(8,128)S(1)}, u32[]{:S(2)}, u32[]{:S(2)}) collective-permute-start(f32[1,64,256]{2,1,0:T(8,128)S(1)} %get-tuple-element.41.front), channel_id=1, source_target_pairs={{0,1},{1,0},{2,3},{3,2},{4,5},{5,4},{6,7},{7,6},{8,9},{9,8},{10,11... | collective-permute-start | bytes 196616 | tf_op jit(solution)/shard_map/ppermute | solution.py:454
  16.4 1.3 %collective-permute-start.8 = (f32[72,256]{1,0:T(8,128)S(1)}, f32[72,256]{1,0:T(8,128)S(1)}, u32[]{:S(2)}, u32[]{:S(2)}) collective-permute-start(f32[72,256]{1,0:T(8,128)S(1)} %collective-permute-done.6.received), channel_id=1, source_target_pairs={{0,1},{1,0},{2,3},{3,2},{4,5},{5,4},{6,7},{7,6},{8,9},{9,8},{10,11... | collective-permute-start | bytes 221192 | tf_op jit(solution)/shard_map/ppermute | solution.py:454

commit v10 on v9

--- a/solution.py
+++ b/solution.py
@@ -124,7 +124,8 @@
 
 def packed_events(packed, spans, k, width):
     per = width // LANES
-    rows = [packed[pl.ds(span.start + k * per + j, 1)] for span in spans for j in range(per)]
+    events = spans[0].size // per
+    rows = [packed[pl.ds(span.start + j * events + k, 1)] for span in spans for j in range(per)]
     cells, counts = jnp.concatenate(rows[:per], axis=1), jnp.concatenate(rows[per:], axis=1)
     return cells.astype(jnp.int32), counts
 
@@ -149,9 +150,8 @@
     out[spans[2]] = cell[...].astype(F32)
     for span, array in ((spans[3], event_cell), (spans[4], event_count)):
         values = array[0].astype(F32)
-        for k in range(events):
-            for j in range(per):
-                out[pl.ds(span.start + k * per + j, 1)] = values[k : k + 1, j * LANES : (j + 1) * LANES]
+        for j in range(per):
+            out[pl.ds(span.start + j * events, events)] = values[:, j * LANES : (j + 1) * LANES]
     for j in range(2):
         out[spans[5 + j]] = field[0, :, pl.ds(j * LANES, LANES)]
 
@@ -188,11 +188,11 @@
 def substep(field, zeroth, first, second, counts, grown):
     rate = softplus(field - 1.0)
     growth = GROWTH * rate
-    taken = growth * (3.0 * second + growth * (3.0 * first + growth * zeroth))
-    field = field - (taken + counts * (NUCLEATE * rate))
-    second = second + growth * (2.0 * first + growth * zeroth)
-    first = first + growth * zeroth
-    return field, first, second, grown + growth
+    linear = growth * zeroth
+    inner = first + linear
+    field = field - (growth * (second + growth * inner) + counts * (NUCLEATE * rate))
+    second = second + growth * (inner + inner + linear)
+    return field, first + 3.0 * linear, second, grown + growth
 
 
 def front_kernel(field, home, home_counts, packed, out, state, *, parcel_rows, events):
@@ -201,7 +201,7 @@
     spans, _ = sections(parcel_rows, events[0] * events[1] // LANES, plane_shape[0])
     cells = packed[spans[2]].astype(jnp.int32)
     zeroth, first, second = plane_moments(plane, packed[spans[0]], packed[spans[1]], cells, plane_shape)
-    zeroth, first, second = zeroth + home[0], first + home[1], second + home[2]
+    zeroth, first, second = zeroth + home[0], 3.0 * (first + home[1]), 3.0 * (second + home[2])
     theirs = jnp.concatenate([packed[spans[5]], packed[spans[6]]], axis=1)
     now = jnp.where(sends_other(), theirs, field[0])
     grown = jnp.zeros_like(now)

time: 18.5 us -> 18.5 us (level)
  no operation moved by 1% of the time
where the time goes in v10:
time: 18.5 us; the launch traced here: 18.3 us
  Pallas kernels  7.2 us (39%)
  starting transfers between devices  5.74 us (31%)
  waiting for transfers between devices  3.81 us (21%)
  between operations  1.49 us (8%)
    pallas_call x15, Pallas kernels, call(): pl.pallas_call(kernel, out_shape=out_shape, in_specs=specs or [VMEM] * le...  7.2 us
    ppermute x2, starting transfers between devices, local(): lax.ppermute(value, ('slab', 'grp'), across_pairs(slabs, second))  4.09 us
    ppermute x7, waiting for transfers between devices, local(): swap = lambda value: lax.ppermute(value, 'grp', [(0, 1), (1, 0)])  3.02 us
    ppermute x7, starting transfers between devices, local(): swap = lambda value: lax.ppermute(value, 'grp', [(0, 1), (1, 0)])  1.65 us
    ppermute x2, waiting for transfers between devices, local(): lax.ppermute(value, ('slab', 'grp'), across_pairs(slabs, second))  0.79 us
  transfers between devices with their start and end apart: 9, of which 6 were waited for; matrix products, arithmetic and copies ran while one was open for 0% of the time, Pallas kernels for 25%

profile of v10, /device:TPU:9, one launch (start us, length us, event | category | flops | bytes accessed | tf_op | source)
XLA Modules:
  0.0 18.3 jit_solution(2074069778474732876)
XLA Ops:
  0.6 0.0 copy-start
  0.6 0.0 copy-start.2
  0.7 0.0 copy-start.3
  0.7 0.0 copy-start.4
  0.7 0.0 copy-start.5
  0.7 0.0 copy-start.1
  1.4 0.1 copy-done
  1.5 0.0 copy-done.2
  1.5 0.0 copy-done.3
  1.5 0.0 copy-done.4
  1.5 0.0 copy-done.5
  1.5 0.0 copy-done.1
  1.5 0.3 %load.1 = (f32[256,128]{1,0:T(8,128)S(1)}, f32[32,128]{1,0:T(8,128)S(1)}, f32[32,128]{1,0:T(8,128)S(1)}, f32[2,64,256]{2,1,0:T(8,128)S(1)}) custom-call(f32[32,128]{1,0:T(8,128)S(1)} %bitcast.5, f32[32,128]{1,0:T(8,128)S(1)} %bitcast.4, s32[32,128]{1,0:T(8,128)S(1)} %bitcast.9, s32[1,4,512]{2,1,0:T(4,128)S(1)} %copy-done.4, s32[1,4,512]{2,1,0:T(4,128)S(1)} %copy-done.5, ...), custom_call_target="tpu_custom_call" | custom-call | tf_op jit(solution)/shard_map/load/pallas_call | solution.py:427
  1.9 0.4 %collective-permute-start = (f32[256,128]{1,0:T(8,128)S(1)}, f32[256,128]{1,0:T(8,128)S(1)}, u32[]{:S(2)}, u32[]{:S(2)}) collective-permute-start(f32[256,128]{1,0:T(8,128)S(1)} %get-tuple-element.32), channel_id=1, source_target_pairs={{0,1},{1,0},{2,3},{3,2},{4,5},{5,4},{6,7},{7,6},{8,9},{9,8},{10,11... | collective-permute-start | bytes 393224 | tf_op jit(solution)/shard_map/ppermute | solution.py:454
  2.3 1.1 %home.1 = (f32[3,64,256]{2,1,0:T(8,128)S(1)}, f32[2,64,256]{2,1,0:T(8,128)S(1)}, s32[1,64,256]{2,1,0:T(8,128)S(1)}, s32[1,2,512]{2,1,0:T(2,128)S(1)}, s32[1,2]{1,0:T(1,128)S(1)}) custom-call(f32[32,128]{1,0:T(8,128)S(1)} %bitcast.6, f32[32,128]{1,0:T(8,128)S(1)} %get-tuple-element.28.weight, s32[32,128]{1,0:T(8,128)S(1)} %bitcast.10, ...), custom_call_target="tpu_custom_call" | custom-call | flops 1073741824 | tf_op jit(solution)/shard_map/home/pallas_call | solution.py:427
  3.4 0.0 collective-permute-done.packed
  3.4 1.2 %front.1 = (f32[1,64,256]{2,1,0:T(8,128)S(1)}, f32[5,64,256]{2,1,0:T(8,128)S(1)}) custom-call(f32[1,64,256]{2,1,0:T(8,128)S(1)} %copy-done, f32[3,64,256]{2,1,0:T(8,128)S(1)} %get-tuple-element.30.home, f32[2,64,256]{2,1,0:T(8,128)S(1)} %get-tuple-element.31.home_counts, f32[256,128]{1,0:T(8,128)S(1)} %collective-permute-done.packed), custom_call_target="tpu_custom_call" | custom-call | tf_op jit(solution)/shard_map/front/pallas_call | solution.py:427
  4.6 2.1 %collective-permute-start.1 = (f32[1,64,256]{2,1,0:T(8,128)S(1)}, f32[1,64,256]{2,1,0:T(8,128)S(1)}, u32[]{:S(2)}, u32[]{:S(2)}) collective-permute-start(f32[1,64,256]{2,1,0:T(8,128)S(1)} %get-tuple-element.33), channel_id=1, source_target_pairs={{0,2},{3,5},{4,6},{7,9},{8,10},{11,13},{12,14},{15,17},{16,18},{19... | collective-permute-start | bytes 196616 | tf_op jit(solution)/shard_map/ppermute | solution.py:456
  6.7 0.1 collective-permute-start.2
  6.8 0.5 %migrants.1.info = f32[32,256]{1,0:T(8,128)S(1)} custom-call(f32[32,128]{1,0:T(8,128)S(1)} %bitcast.7, f32[32,128]{1,0:T(8,128)S(1)} %get-tuple-element.28.weight, s32[32,128]{1,0:T(8,128)S(1)} %bitcast.11, s32[1,2,512]{2,1,0:T(2,128)S(1)} %get-tuple-element.36.rows, s32[1,2]{1,0:T(1,128)S(1)} %get-tuple-element.37.count), custom_call_target="tpu_custom_call" | custom-call | flops 8589934592 | tf_op jit(solution)/shard_map/migrants/pallas_call | solution.py:427
  7.3 0.6 %collective-permute-start.3 = (f32[32,256]{1,0:T(8,128)S(1)}, f32[32,256]{1,0:T(8,128)S(1)}, u32[]{:S(2)}, u32[]{:S(2)}) collective-permute-start(f32[32,256]{1,0:T(8,128)S(1)} %migrants.1.info), channel_id=1, source_target_pairs={{0,1},{1,0},{2,3},{3,2},{4,5},{5,4},{6,7},{7,6},{8,9},{9,8},{10,11... | collective-permute-start | bytes 98312 | tf_op jit(solution)/shard_map/ppermute | solution.py:454
  7.9 0.5 %late.1 = f32[2,64,256]{2,1,0:T(8,128)S(1)} custom-call(f32[256,128]{1,0:T(8,128)S(1)} %collective-permute-done.packed, s32[1,4,512]{2,1,0:T(4,128)S(1)} %copy-done.4, s32[1,4,512]{2,1,0:T(4,128)S(1)} %copy-done.5), custom_call_target="tpu_custom_call" | custom-call | flops 268435456 | tf_op jit(solution)/shard_map/late/pallas_call | solution.py:427
  8.4 0.4 %collective-permute-done.3.their_info = f32[32,256]{1,0:T(8,128)S(1)} collective-permute-done((f32[32,256]{1,0:T(8,128)S(1)}, f32[32,256]{1,0:T(8,128)S(1)}, u32[]{:S(2)}, u32[]{:S(2)}) %collective-permute-start.3) | collective-permute-done | bytes 32800 | tf_op jit(solution)/shard_map/ppermute | solution.py:454
  8.7 0.0 collective-permute-done.2.other
  8.7 0.3 %ready.1 = (f32[6,64,256]{2,1,0:T(8,128)S(1)}, bf16[256,1024]{1,0:T(8,128)(2,1)S(1)}, f32[8,1024]{1,0:T(8,128)S(1)}) custom-call(f32[6,64,256]{2,1,0:T(8,128)S(1)} %pack.1.mine, f32[6,64,256]{2,1,0:T(8,128)S(1)} %collective-permute-done.2.other, f32[32,256]{1,0:T(8,128)S(1)} %migrants.1.info, f32[32,256]{1,0:T(8,128)S(1)} %collective-permute-done.3.their_info), custom_call_target="tpu_custom_call" | custom-call | flops 67108864 | tf_op jit(solution)/shard_map/ready/pallas_call | solution.py:427
  9.1 0.6 %collective-permute-done.1.beside = f32[1,64,256]{2,1,0:T(8,128)S(1)} collective-permute-done((f32[1,64,256]{2,1,0:T(8,128)S(1)}, f32[1,64,256]{2,1,0:T(8,128)S(1)}, u32[]{:S(2)}, u32[]{:S(2)}) %collective-permute-start.1) | collective-permute-done | bytes 65568 | tf_op jit(solution)/shard_map/ppermute | solution.py:456
  9.7 0.3 %second.1 = f32[8,256]{1,0:T(8,128)S(1)} custom-call(f32[1,64,256]{2,1,0:T(8,128)S(1)} %collective-permute-done.1.beside, f32[6,64,256]{2,1,0:T(8,128)S(1)} %get-tuple-element.39.ready, f32[2,64,256]{2,1,0:T(8,128)S(1)} %late.1, bf16[256,1024]{1,0:T(8,128)(2,1)S(1)} %get-tuple-element.43.hot_place, f32[8,1024]{1,0:T(8,128)S(1)} %get-tuple-element.44.lists), custom_call_target="tpu_custom_call" | custom-call | tf_op jit(solution)/shard_map/second/pallas_call | solution.py:427
  10.0 0.1 collective-permute-start.5
  10.1 0.4 %own.1 = (f32[8,256]{1,0:T(8,128)S(1)}, f32[1,64,256]{2,1,0:T(8,128)S(1)}, f32[1,64,256]{2,1,0:T(8,128)S(1)}) custom-call(f32[1,64,256]{2,1,0:T(8,128)S(1)} %collective-permute-done.1.beside, f32[6,64,256]{2,1,0:T(8,128)S(1)} %get-tuple-element.39.ready, f32[2,64,256]{2,1,0:T(8,128)S(1)} %late.1, f32[32,256]{1,0:T(8,128)S(1)} %migrants.1.info, ...), custom_call_target="tpu_custom_call" | custom-call | flops 268435456 | tf_op jit(solution)/shard_map/own/pallas_call | solution.py:427
  10.5 0.8 %collective-permute-done.5.theirs = f32[8,256]{1,0:T(8,128)S(1)} collective-permute-done((f32[8,256]{1,0:T(8,128)S(1)}, f32[8,256]{1,0:T(8,128)S(1)}, u32[]{:S(2)}, u32[]{:S(2)}) %collective-permute-start.5) | collective-permute-done | bytes 8224 | tf_op jit(solution)/shard_map/ppermute | solution.py:454
  11.3 2.0 %collective-permute-start.6 = (f32[72,256]{1,0:T(8,128)S(1)}, f32[72,256]{1,0:T(8,128)S(1)}, u32[]{:S(2)}, u32[]{:S(2)}) collective-permute-start(f32[72,256]{1,0:T(8,128)S(1)} %leaving.1), channel_id=1, source_target_pairs={{1,2},{3,5},{4,6},{7,9},{8,10},{11,13},{12,14},{15,17},{16,18},{19... | collective-permute-start | bytes 221192 | tf_op jit(solution)/shard_map/ppermute | solution.py:456
  13.3 0.0 collective-permute-start.7
  13.3 0.5 %collective-permute-start.4 = (f32[1,64,256]{2,1,0:T(8,128)S(1)}, f32[1,64,256]{2,1,0:T(8,128)S(1)}, u32[]{:S(2)}, u32[]{:S(2)}) collective-permute-start(f32[1,64,256]{2,1,0:T(8,128)S(1)} %get-tuple-element.41.front), channel_id=1, source_target_pairs={{0,1},{1,0},{2,3},{3,2},{4,5},{5,4},{6,7},{7,6},{8,9},{9,8},{10,11... | collective-permute-start | bytes 196616 | tf_op jit(solution)/shard_map/ppermute | solution.py:454
  13.8 0.7 %collective-permute-done.7.their_total = f32[1,64,256]{2,1,0:T(8,128)S(1)} collective-permute-done((f32[1,64,256]{2,1,0:T(8,128)S(1)}, f32[1,64,256]{2,1,0:T(8,128)S(1)}, u32[]{:S(2)}, u32[]{:S(2)}) %collective-permute-start.7) | collective-permute-done | bytes 65568 | tf_op jit(solution)/shard_map/ppermute | solution.py:454
  14.5 1.7 %sizes.1 = f32[32,128]{1,0:T(8,128)} custom-call(f32[1,64,256]{2,1,0:T(8,128)S(1)} %get-tuple-element.46.total, f32[1,64,256]{2,1,0:T(8,128)S(1)} %collective-permute-done.7.their_total, f32[32,128]{1,0:T(8,128)S(1)} %bitcast.8, s32[32,128]{1,0:T(8,128)S(1)} %bitcast.12, f32[32,128]{1,0:T(8,128)S(1)} %get-tuple-element.47.active), custom_call_target="tpu_custom_call" | custom-call | flops 67108864 | tf_op jit(solution)/shard_map/sizes/pallas_call | solution.py:427
  16.2 0.2 collective-permute-done.6.received
  16.4 0.0 collective-permute-start.8
  16.4 0.0 collective-permute-done.4.their_front
  16.4 0.1 rest.1
  16.6 1.1 %collective-permute-done.8.relayed = f32[72,256]{1,0:T(8,128)S(1)} collective-permute-done((f32[72,256]{1,0:T(8,128)S(1)}, f32[72,256]{1,0:T(8,128)S(1)}, u32[]{:S(2)}, u32[]{:S(2)}) %collective-permute-start.8) | collective-permute-done | bytes 73760 | tf_op jit(solution)/shard_map/ppermute | solution.py:454
  17.7 0.7 %last.1 = (f32[1,64,256]{2,1,0:T(8,128)}, f32[1,2,2,512]{3,2,1,0:T(2,128)}) custom-call(f32[2,64,256]{2,1,0:T(8,128)S(1)} %rest.1, f32[72,256]{1,0:T(8,128)S(1)} %collective-permute-done.6.received, f32[72,256]{1,0:T(8,128)S(1)} %collective-permute-done.8.relayed), custom_call_target="tpu_custom_call" | custom-call | tf_op jit(solution)/shard_map/last/pallas_call | solution.py:427
  (4 shorter events, 0.0 us)
Async XLA Ops:
  0.6 0.8 %copy-start = (f32[1,64,256]{2,1,0:T(8,128)S(1)}, f32[1,64,256]{2,1,0:T(8,128)}, u32[]{:S(2)}) copy-start(f32[1,64,256]{2,1,0:T(8,128)} %field.1) | copy-start | bytes 196612
  0.6 0.8 %copy-start.2 = (f32[4096]{0:T(1024)S(1)}, f32[4096]{0:T(1024)}, u32[]{:S(2)}) copy-start(f32[4096]{0:T(1024)} %param.12) | copy-start | bytes 49156
  0.7 0.8 %copy-start.3 = (s32[4096]{0:T(1024)S(1)}, s32[4096]{0:T(1024)}, u32[]{:S(2)}) copy-start(s32[4096]{0:T(1024)} %param.14) | copy-start | bytes 49156
  0.7 0.8 %copy-start.4 = (s32[1,4,512]{2,1,0:T(4,128)S(1)}, s32[1,4,512]{2,1,0:T(4,128)}, u32[]{:S(2)}) copy-start(s32[1,4,512]{2,1,0:T(4,128)} %event_cell.3) | copy-start | bytes 24580
  0.7 0.8 %copy-start.5 = (s32[1,4,512]{2,1,0:T(4,128)S(1)}, s32[1,4,512]{2,1,0:T(4,128)}, u32[]{:S(2)}) copy-start(s32[1,4,512]{2,1,0:T(4,128)} %event_count.3) | copy-start | bytes 24580
  0.7 0.8 %copy-start.1 = (f32[4096]{0:T(1024)S(1)}, f32[4096]{0:T(1024)}, u32[]{:S(2)}) copy-start(f32[4096]{0:T(1024)} %param.13) | copy-start | bytes 49156
  1.9 1.5 %collective-permute-start = (f32[256,128]{1,0:T(8,128)S(1)}, f32[256,128]{1,0:T(8,128)S(1)}, u32[]{:S(2)}, u32[]{:S(2)}) collective-permute-start(f32[256,128]{1,0:T(8,128)S(1)} %get-tuple-element.32), channel_id=1, source_target_pairs={{0,1},{1,0},{2,3},{3,2},{4,5},{5,4},{6,7},{7,6},{8,9},{9,8},{10,11... | collective-permute-start | bytes 393224 | tf_op jit(solution)/shard_map/ppermute | solution.py:454
  4.6 5.1 %collective-permute-start.1 = (f32[1,64,256]{2,1,0:T(8,128)S(1)}, f32[1,64,256]{2,1,0:T(8,128)S(1)}, u32[]{:S(2)}, u32[]{:S(2)}) collective-permute-start(f32[1,64,256]{2,1,0:T(8,128)S(1)} %get-tuple-element.33), channel_id=1, source_target_pairs={{0,2},{3,5},{4,6},{7,9},{8,10},{11,13},{12,14},{15,17},{16,18},{19... | collective-permute-start | bytes 196616 | tf_op jit(solution)/shard_map/ppermute | solution.py:456
  6.7 2.0 %collective-permute-start.2 = (f32[6,64,256]{2,1,0:T(8,128)S(1)}, f32[6,64,256]{2,1,0:T(8,128)S(1)}, u32[]{:S(2)}, u32[]{:S(2)}) collective-permute-start(f32[6,64,256]{2,1,0:T(8,128)S(1)} %pack.1.mine), channel_id=1, source_target_pairs={{0,1},{1,0},{2,3},{3,2},{4,5},{5,4},{6,7},{7,6},{8,9},{9,8},{10,11... | collective-permute-start | bytes 1179656 | tf_op jit(solution)/shard_map/ppermute | solution.py:454
  7.3 1.4 %collective-permute-start.3 = (f32[32,256]{1,0:T(8,128)S(1)}, f32[32,256]{1,0:T(8,128)S(1)}, u32[]{:S(2)}, u32[]{:S(2)}) collective-permute-start(f32[32,256]{1,0:T(8,128)S(1)} %migrants.1.info), channel_id=1, source_target_pairs={{0,1},{1,0},{2,3},{3,2},{4,5},{5,4},{6,7},{7,6},{8,9},{9,8},{10,11... | collective-permute-start | bytes 98312 | tf_op jit(solution)/shard_map/ppermute | solution.py:454
  10.0 1.2 %collective-permute-start.5 = (f32[8,256]{1,0:T(8,128)S(1)}, f32[8,256]{1,0:T(8,128)S(1)}, u32[]{:S(2)}, u32[]{:S(2)}) collective-permute-start(f32[8,256]{1,0:T(8,128)S(1)} %second.1), channel_id=1, source_target_pairs={{0,1},{1,0},{2,3},{3,2},{4,5},{5,4},{6,7},{7,6},{8,9},{9,8},{10,11... | collective-permute-start | bytes 24584 | tf_op jit(solution)/shard_map/ppermute | solution.py:454
  11.3 5.2 %collective-permute-start.6 = (f32[72,256]{1,0:T(8,128)S(1)}, f32[72,256]{1,0:T(8,128)S(1)}, u32[]{:S(2)}, u32[]{:S(2)}) collective-permute-start(f32[72,256]{1,0:T(8,128)S(1)} %leaving.1), channel_id=1, source_target_pairs={{1,2},{3,5},{4,6},{7,9},{8,10},{11,13},{12,14},{15,17},{16,18},{19... | collective-permute-start | bytes 221192 | tf_op jit(solution)/shard_map/ppermute | solution.py:456
  13.3 1.3 %collective-permute-start.7 = (f32[1,64,256]{2,1,0:T(8,128)S(1)}, f32[1,64,256]{2,1,0:T(8,128)S(1)}, u32[]{:S(2)}, u32[]{:S(2)}) collective-permute-start(f32[1,64,256]{2,1,0:T(8,128)S(1)} %get-tuple-element.46.total), channel_id=1, source_target_pairs={{0,1},{1,0},{2,3},{3,2},{4,5},{5,4},{6,7},{7,6},{8,9},{9,8},{10,11... | collective-permute-start | bytes 196616 | tf_op jit(solution)/shard_map/ppermute | solution.py:454
  13.3 3.2 %collective-permute-start.4 = (f32[1,64,256]{2,1,0:T(8,128)S(1)}, f32[1,64,256]{2,1,0:T(8,128)S(1)}, u32[]{:S(2)}, u32[]{:S(2)}) collective-permute-start(f32[1,64,256]{2,1,0:T(8,128)S(1)} %get-tuple-element.41.front), channel_id=1, source_target_pairs={{0,1},{1,0},{2,3},{3,2},{4,5},{5,4},{6,7},{7,6},{8,9},{9,8},{10,11... | collective-permute-start | bytes 196616 | tf_op jit(solution)/shard_map/ppermute | solution.py:454
  16.4 1.3 %collective-permute-start.8 = (f32[72,256]{1,0:T(8,128)S(1)}, f32[72,256]{1,0:T(8,128)S(1)}, u32[]{:S(2)}, u32[]{:S(2)}) collective-permute-start(f32[72,256]{1,0:T(8,128)S(1)} %collective-permute-done.6.received), channel_id=1, source_target_pairs={{0,1},{1,0},{2,3},{3,2},{4,5},{5,4},{6,7},{7,6},{8,9},{9,8},{10,11... | collective-permute-start | bytes 221192 | tf_op jit(solution)/shard_map/ppermute | solution.py:454
